TPU v7x, 512 devices: a whole 4x8x8 slice. The times are simulated.
512 devices in a mesh: ops: 32 (over z, x), sec: 16 (over y, core).
Axes of the slice: x: 4, y: 8, z: 8, core: 2. Of those that a mesh axis runs over, the one named last changes fastest.
Arguments:
- psi: bfloat16 [64, 256, 256], P('sec'), may hold values from -6 to 6
- left_ops: bfloat16 [512, 256, 256], P('ops'), may hold values from -0.375 to 0.375
- right_ops: bfloat16 [512, 256, 256], P('ops'), may hold values from -0.375 to 0.375
- coef: float32 [512], P('ops'), may hold values from -1.25 to 1.25
- source: int32 [512, 64], P('ops', 'sec'), may hold values from 0 to 63
- active: int32 [512, 64], P('ops', 'sec'), may hold values from 0 to 1, as said below
- left_block: bfloat16 [64, 256, 256], P('sec'), may hold values from -0.375 to 0.375
- right_block: bfloat16 [64, 256, 256], P('sec'), may hold values from -0.375 to 0.375
Outputs:
- sigma: float32 [64, 256, 256], P('sec', 'ops')
Inputs may be any that keep to these rules, and one draw needn't show every extreme that they name: active[k, t] is 0 or 1; each target sector t has its own rate, the same for all terms, between 1/32 and 1/2, so most pairs are inactive and sectors differ.
All inputs are finite; a program needn't handle non-finite values.
Results may differ from a plain program's by a relative error of at most 0.0023.
Values may be sent and summed in bfloat16 or wider, within the bound.
No kernel may reach another device: no remote copies, remote signals or barrier semaphores. Data moves between devices by JAX's collectives and lax.ppermute only.
A program may use at most 64 MiB of HBM per device.

v0:
```python
import math

import jax
import jax.numpy as jnp
from jax import lax
from jax.sharding import PartitionSpec as P


def per_device(psi, left_ops, right_ops, coef, source, active, left_block, right_block):
    sec_dev = psi.shape[0]
    tile = psi.shape[1]
    term_dev = left_ops.shape[0]
    n_ops = lax.axis_size("ops")
    band = tile // n_ops
    band_start = lax.axis_index("ops") * band
    gathered = lax.all_gather(psi, "sec", axis=0, tiled=True)
    pairs = term_dev * sec_dev
    group = math.gcd(16, pairs)
    term_index = jnp.repeat(jnp.arange(term_dev, dtype=jnp.int32), sec_dev)
    target_index = jnp.tile(jnp.arange(sec_dev, dtype=jnp.int32), term_dev)
    source_flat = source.reshape(pairs)
    weight_flat = (coef[:, None] * active.astype(jnp.float32)).reshape(pairs)
    targets_all = jnp.arange(sec_dev, dtype=jnp.int32)

    def add_group(step, total, order):
        chosen = lax.dynamic_slice_in_dim(order, step * group, group, 0)
        terms_here = jnp.take(term_index, chosen)
        targets_here = jnp.take(target_index, chosen)
        sources_here = jnp.take(source_flat, chosen)
        weights_here = jnp.take(weight_flat, chosen)
        left_here = jnp.take(left_ops, terms_here, axis=0)
        right_here = jnp.take(right_ops, terms_here, axis=0)
        tiles_here = jnp.take(gathered, sources_here, axis=0)
        mixed = jnp.einsum(
            "pij,pjl->pil", left_here, tiles_here, preferred_element_type=jnp.float32
        ).astype(jnp.bfloat16)
        image = jnp.einsum("pil,plm->pim", mixed, right_here, preferred_element_type=jnp.float32)
        placing = (targets_here[:, None] == targets_all[None, :]).astype(
            jnp.float32
        ) * weights_here[:, None]
        return total + jnp.einsum("pt,pim->tim", placing, image, precision=lax.Precision.HIGHEST)

    start = jnp.zeros((sec_dev, tile, tile), jnp.float32)
    order = jnp.arange(pairs, dtype=jnp.int32)
    partial_sum = lax.fori_loop(
        0, pairs // group, lambda step, total: add_group(step, total, order), start
    )
    local_rows = lax.dynamic_slice_in_dim(psi, band_start, band, 1)
    block_rows = lax.dynamic_slice_in_dim(left_block, band_start, band, 1)
    local_part = jnp.einsum("tij,tjl->til", block_rows, psi, preferred_element_type=jnp.float32)
    local_part = local_part + jnp.einsum(
        "tij,tjl->til", local_rows, right_block, preferred_element_type=jnp.float32
    )
    summed = lax.psum_scatter(partial_sum, "ops", scatter_dimension=1, tiled=True)
    return local_part + summed


def solution(mesh):
    in_specs = (
        P("sec", None, None),
        P("ops", None, None),
        P("ops", None, None),
        P("ops"),
        P("ops", "sec"),
        P("ops", "sec"),
        P("sec", None, None),
        P("sec", None, None),
    )
    out_specs = P("sec", "ops", None)
    return jax.shard_map(
        per_device, mesh=mesh, in_specs=in_specs, out_specs=out_specs, check_vma=False
    )
```

profile of v0, /device:TPU:24, one launch (start us, length us, event | category | flops | bytes accessed | tf_op | source)
XLA Modules:
  0.0 415.3 jit_solution(7118794142501735898)
XLA Ops:
  6.5 0.7 all-gather.2.cloned.1.call-update
  7.3 0.7 convert_multiply_fusion
  8.2 0.8 copy.17
  9.0 62.9 %all-gather.2.cloned.1.call-done = bf16[64,256,256]{2,1,0:T(8,128)(2,1)} async-done(((bf16[4,256,256]{2,1,0:T(8,128)(2,1)}), bf16[64,256,256]{2,1,0:T(8,128)(2,1)}) %all-gather.2.cloned.1.call-update) | async-done | bytes 8388624 | tf_op jit(solution)/shard_map/all_gather | solution.py:16
  71.9 111.6 %while.14 = (s32[]{:T(128)}, f32[4,256,256]{2,0,1:T(4,128)}, s32[64]{0:T(128)S(1)}, f32[64]{0:T(128)S(1)}, bf16[16,256,256]{2,1,0:T(8,128)(2,1)}, /*index=5*/s32...) while((s32[]{:T(128)}, f32[4,256,256]{2,0,1:T(4,128)}, ...), condition=%wide.region_1.4_spmd.clone, body=%wide.region_0.3_spmd.clone.sunk | while | flops 1128795904 | bytes 46153592 | solution.py:45
  72.0 0.7 gather_fusion
  72.8 0.7 gather_fusion.1
  73.5 3.8 gather_fusion.2
  77.3 2.0 gather_fusion.3
  79.3 5.5 %gather_fusion.4 = bf16[16,256,256]{2,1,0:T(8,128)(2,1)} fusion(bf16[64,256,256]{2,1,0:T(8,128)(2,1)} %get-tuple-element.340, s32[1024]{0:T(1024)S(1)} %get-tuple-element.307), kind=kCustom, calls=%fused_computation.6.clone.clone.1 | custom fusion | bytes 4194368 | tf_op jit(solution)/shard_map/while/body/eval_jaxpr/jit(_take)/gather | solution.py:33
  84.8 5.6 %fusion.61 = f32[16,256,256]{2,1,0:T(8,128)} fusion(bf16[16,256,256]{2,1,0:T(8,128)(2,1)S(1)} %copy-done.2, bf16[16,256,256]{2,1,0:T(8,128)(2,1)} %gather_fusion.3, bf16[16,256,256]{2,1,0:T(8,128)(2,1)} %gather_fusion.4, pred[16]{0:T(512)(128)(4,1)S(1)} %get-tuple-element.308, pred[16]{0:T(512)(128)(4,1)S(1)} %get-tuple-element.309), kind=kOutput, calls=%fused_computation.12.clone.1 | convolution fusion | flops 1077936128 | bytes 10485792 | tf_op jit(solution)/shard_map/while/body/eval_jaxpr/pil,plm->pim/dot_general | solution.py:37
  90.5 0.7 gather_fusion.5
  91.2 0.1 tile.22
  91.3 0.7 gather_fusion.6
  92.0 7.5 %fusion.62 = f32[4,256,256]{2,0,1:T(4,128)} fusion(f32[16,256,256]{2,1,0:T(8,128)} %fusion.61, f32[4,256,256]{2,0,1:T(4,128)} %get-tuple-element.323, pred[]{:T(512)S(6)} %compare.3, f32[16]{0:T(128)S(1)} %broadcast_select_fusion.4, s32[16]{0:T(128)S(1)} %broadcast_select_fusion.5), kind=kOutput, calls=%fused_computation.20.clone.1 | convolution fusion | flops 50856064 | bytes 6291585 | tf_op jit(solution)/shard_map/while/body/eval_jaxpr/pt,pim->tim/dot_general | solution.py:41
  99.7 0.7 gather_fusion
  100.4 0.7 gather_fusion.1
  101.2 3.8 gather_fusion.2
  105.0 2.0 gather_fusion.3
  107.0 5.5 %gather_fusion.4 = bf16[16,256,256]{2,1,0:T(8,128)(2,1)} fusion(bf16[64,256,256]{2,1,0:T(8,128)(2,1)} %get-tuple-element.340, s32[1024]{0:T(1024)S(1)} %get-tuple-element.307), kind=kCustom, calls=%fused_computation.6.clone.clone.1 | custom fusion | bytes 4194368 | tf_op jit(solution)/shard_map/while/body/eval_jaxpr/jit(_take)/gather | solution.py:33
  112.5 5.6 %fusion.61 = f32[16,256,256]{2,1,0:T(8,128)} fusion(bf16[16,256,256]{2,1,0:T(8,128)(2,1)S(1)} %copy-done.2, bf16[16,256,256]{2,1,0:T(8,128)(2,1)} %gather_fusion.3, bf16[16,256,256]{2,1,0:T(8,128)(2,1)} %gather_fusion.4, pred[16]{0:T(512)(128)(4,1)S(1)} %get-tuple-element.308, pred[16]{0:T(512)(128)(4,1)S(1)} %get-tuple-element.309), kind=kOutput, calls=%fused_computation.12.clone.1 | convolution fusion | flops 1077936128 | bytes 10485792 | tf_op jit(solution)/shard_map/while/body/eval_jaxpr/pil,plm->pim/dot_general | solution.py:37
  118.1 0.7 gather_fusion.5
  118.9 0.1 tile.22
  119.0 0.7 gather_fusion.6
  119.7 7.8 %fusion.62 = f32[4,256,256]{2,0,1:T(4,128)} fusion(f32[16,256,256]{2,1,0:T(8,128)} %fusion.61, f32[4,256,256]{2,0,1:T(4,128)} %get-tuple-element.323, pred[]{:T(512)S(6)} %compare.3, f32[16]{0:T(128)S(1)} %broadcast_select_fusion.4, s32[16]{0:T(128)S(1)} %broadcast_select_fusion.5), kind=kOutput, calls=%fused_computation.20.clone.1 | convolution fusion | flops 50856064 | bytes 6291585 | tf_op jit(solution)/shard_map/while/body/eval_jaxpr/pt,pim->tim/dot_general | solution.py:41
  127.6 0.7 gather_fusion
  128.4 0.7 gather_fusion.1
  129.2 3.8 gather_fusion.2
  133.0 2.0 gather_fusion.3
  135.0 5.5 %gather_fusion.4 = bf16[16,256,256]{2,1,0:T(8,128)(2,1)} fusion(bf16[64,256,256]{2,1,0:T(8,128)(2,1)} %get-tuple-element.340, s32[1024]{0:T(1024)S(1)} %get-tuple-element.307), kind=kCustom, calls=%fused_computation.6.clone.clone.1 | custom fusion | bytes 4194368 | tf_op jit(solution)/shard_map/while/body/eval_jaxpr/jit(_take)/gather | solution.py:33
  140.5 5.6 %fusion.61 = f32[16,256,256]{2,1,0:T(8,128)} fusion(bf16[16,256,256]{2,1,0:T(8,128)(2,1)S(1)} %copy-done.2, bf16[16,256,256]{2,1,0:T(8,128)(2,1)} %gather_fusion.3, bf16[16,256,256]{2,1,0:T(8,128)(2,1)} %gather_fusion.4, pred[16]{0:T(512)(128)(4,1)S(1)} %get-tuple-element.308, pred[16]{0:T(512)(128)(4,1)S(1)} %get-tuple-element.309), kind=kOutput, calls=%fused_computation.12.clone.1 | convolution fusion | flops 1077936128 | bytes 10485792 | tf_op jit(solution)/shard_map/while/body/eval_jaxpr/pil,plm->pim/dot_general | solution.py:37
  146.1 0.7 gather_fusion.5
  146.9 0.7 gather_fusion.6
  147.7 7.8 %fusion.62 = f32[4,256,256]{2,0,1:T(4,128)} fusion(f32[16,256,256]{2,1,0:T(8,128)} %fusion.61, f32[4,256,256]{2,0,1:T(4,128)} %get-tuple-element.323, pred[]{:T(512)S(6)} %compare.3, f32[16]{0:T(128)S(1)} %broadcast_select_fusion.4, s32[16]{0:T(128)S(1)} %broadcast_select_fusion.5), kind=kOutput, calls=%fused_computation.20.clone.1 | convolution fusion | flops 50856064 | bytes 6291585 | tf_op jit(solution)/shard_map/while/body/eval_jaxpr/pt,pim->tim/dot_general | solution.py:41
  155.6 0.7 gather_fusion
  156.4 0.7 gather_fusion.1
  157.1 3.8 gather_fusion.2
  160.9 2.0 gather_fusion.3
  162.9 5.5 %gather_fusion.4 = bf16[16,256,256]{2,1,0:T(8,128)(2,1)} fusion(bf16[64,256,256]{2,1,0:T(8,128)(2,1)} %get-tuple-element.340, s32[1024]{0:T(1024)S(1)} %get-tuple-element.307), kind=kCustom, calls=%fused_computation.6.clone.clone.1 | custom fusion | bytes 4194368 | tf_op jit(solution)/shard_map/while/body/eval_jaxpr/jit(_take)/gather | solution.py:33
  168.4 5.6 %fusion.61 = f32[16,256,256]{2,1,0:T(8,128)} fusion(bf16[16,256,256]{2,1,0:T(8,128)(2,1)S(1)} %copy-done.2, bf16[16,256,256]{2,1,0:T(8,128)(2,1)} %gather_fusion.3, bf16[16,256,256]{2,1,0:T(8,128)(2,1)} %gather_fusion.4, pred[16]{0:T(512)(128)(4,1)S(1)} %get-tuple-element.308, pred[16]{0:T(512)(128)(4,1)S(1)} %get-tuple-element.309), kind=kOutput, calls=%fused_computation.12.clone.1 | convolution fusion | flops 1077936128 | bytes 10485792 | tf_op jit(solution)/shard_map/while/body/eval_jaxpr/pil,plm->pim/dot_general | solution.py:37
  174.1 0.7 gather_fusion.5
  174.8 0.1 tile.22
  174.9 0.7 gather_fusion.6
  175.6 7.8 %fusion.62 = f32[4,256,256]{2,0,1:T(4,128)} fusion(f32[16,256,256]{2,1,0:T(8,128)} %fusion.61, f32[4,256,256]{2,0,1:T(4,128)} %get-tuple-element.323, pred[]{:T(512)S(6)} %compare.3, f32[16]{0:T(128)S(1)} %broadcast_select_fusion.4, s32[16]{0:T(128)S(1)} %broadcast_select_fusion.5), kind=kOutput, calls=%fused_computation.20.clone.1 | convolution fusion | flops 50856064 | bytes 6291585 | tf_op jit(solution)/shard_map/while/body/eval_jaxpr/pt,pim->tim/dot_general | solution.py:41
  183.5 2.5 copy.18
  186.0 0.2 fusion.41
  186.2 220.7 %reduce-scatter.2.cloned.1.call-done = f32[4,8,256]{2,1,0:T(8,128)} async-done(((f32[4,256,256]{2,1,0:T(8,128)}), f32[4,8,256]{2,1,0:T(8,128)}) %reduce-scatter.2.cloned.1.call-update) | async-done | bytes 32784 | tf_op jit(solution)/shard_map/reduce_scatter | solution.py:54
  406.9 1.6 fusion.39
  (67 shorter events, 2.2 us)
Async XLA Ops:
  6.5 179.5 %copy-start = (bf16[4,256,256]{2,1,0:T(8,128)(2,1)S(1)}, bf16[4,256,256]{2,1,0:T(8,128)(2,1)}, u32[]{:S(2)}) copy-start(bf16[4,256,256]{2,1,0:T(8,128)(2,1)} %param.20) | copy-start | bytes 1572868
  6.5 65.4 %all-gather.2.cloned.1.call-start = ((), (), s32[]{:S(2)}) async-start(), calls=%async_computation.1 | async-start | bytes 8912896 | tf_op jit(solution)/shard_map/all_gather | solution.py:16
  7.3 399.6 %reduce-scatter.2.cloned.1.call-start = ((), (), s32[]{:S(2)}) async-start(), calls=%async_computation.2 | async-start | bytes 1081344 | tf_op jit(solution)/shard_map/reduce_scatter | solution.py:54
  73.5 3.8 copy-start.1
  79.3 5.5 %copy-start.2 = (bf16[16,256,256]{2,1,0:T(8,128)(2,1)S(1)}, bf16[16,256,256]{2,1,0:T(8,128)(2,1)}, u32[]{:S(2)}) copy-start(bf16[16,256,256]{2,1,0:T(8,128)(2,1)} %gather_fusion.2) | copy-start | bytes 6291460 | tf_op jit(solution)/shard_map/while
  101.2 3.8 copy-start.1
  107.0 5.5 %copy-start.2 = (bf16[16,256,256]{2,1,0:T(8,128)(2,1)S(1)}, bf16[16,256,256]{2,1,0:T(8,128)(2,1)}, u32[]{:S(2)}) copy-start(bf16[16,256,256]{2,1,0:T(8,128)(2,1)} %gather_fusion.2) | copy-start | bytes 6291460 | tf_op jit(solution)/shard_map/while
  129.2 3.8 copy-start.1
  135.0 5.5 %copy-start.2 = (bf16[16,256,256]{2,1,0:T(8,128)(2,1)S(1)}, bf16[16,256,256]{2,1,0:T(8,128)(2,1)}, u32[]{:S(2)}) copy-start(bf16[16,256,256]{2,1,0:T(8,128)(2,1)} %gather_fusion.2) | copy-start | bytes 6291460 | tf_op jit(solution)/shard_map/while
  157.1 3.8 copy-start.1
  162.9 5.5 %copy-start.2 = (bf16[16,256,256]{2,1,0:T(8,128)(2,1)S(1)}, bf16[16,256,256]{2,1,0:T(8,128)(2,1)}, u32[]{:S(2)}) copy-start(bf16[16,256,256]{2,1,0:T(8,128)(2,1)} %gather_fusion.2) | copy-start | bytes 6291460 | tf_op jit(solution)/shard_map/while
  183.5 2.5 copy-start.3
  183.5 223.4 %copy-start.4 = (bf16[4,256,256]{2,1,0:T(8,128)(2,1)S(1)}, bf16[4,256,256]{2,1,0:T(8,128)(2,1)}, u32[]{:S(2)}) copy-start(bf16[4,256,256]{2,1,0:T(8,128)(2,1)} %param.21) | copy-start | bytes 1572868
Sparse Core Ops, SparseCore 0:
  9.5 62.3 all-gather.1
  186.1 220.7 reduce-scatter.1
where the time goes:
time: 416 us; the launch traced here: 415 us
  waiting for transfers between devices  284 us (68%)
  local copies, waits for them, and re-layouts  60.1 us (14%)
  matrix products  55.2 us (13%)
  between operations  13.4 us (3%)
    reduce_scatter x1, waiting for transfers between devices, per_device(): lax.psum_scatter(partial_sum, 'ops', scatter_dimension=1, tiled=True)  221 us
    all_gather x1, waiting for transfers between devices, per_device(): gathered = lax.all_gather(psi, 'sec', axis=0, tiled=True)  62.9 us
    dot_general x4, matrix products, add_group(): jnp.einsum('pt,pim->tim', placing, image, precision=lax.Precision.HIGHEST)  31 us
    dot_general x4, matrix products, add_group(): jnp.einsum('pil,plm->pim', mixed, right_here, preferred_element_type=jnp....  22.5 us
    gather x4, local copies, waits for them, and re-layouts, add_group(): tiles_here = jnp.take(gathered, sources_here, axis=0)  22 us
    gather x4, local copies, waits for them, and re-layouts, add_group(): right_here = jnp.take(right_ops, terms_here, axis=0)  15.2 us
  transfers between devices with their start and end apart: 2, of which 2 were waited for; matrix products, arithmetic and copies ran while one was open for 0% of the time, Pallas kernels for 0%

commit v1 on v0

v1 whole, which is shorter than its diff:
```python
import functools

import jax
import jax.numpy as jnp
from jax import lax
from jax.experimental import pallas as pl
from jax.experimental.pallas import tpu as pltpu
from jax.sharding import Mesh, PartitionSpec as P

AXES = (8, 4, 8, 2)
NAMES = ("z", "x", "y", "core")
GROUP = 4

PLACES = ((0, 1, 0), (1, 4, 2), (-1, 5, 3), (2, 7, 6))


def places_of(codes, sec_dev, core, ring):
    source_core = (codes // sec_dev) % 2
    away = (codes // (2 * sec_dev) - ring) * jnp.where(source_core == 0, 1, -1)
    block = jnp.full_like(codes, -1)
    for far, other, own in PLACES:
        here = (away - far) % AXES[2] == 0
        block = jnp.where(here, jnp.where(source_core == core, own, other), block)
    held = jnp.logical_and(codes >= 0, block >= 0)
    return jnp.where(held, block * sec_dev + codes % sec_dev, 2 * len(PLACES) * sec_dev)


def plan_kernel(
    place_ref, coef_ref, left_hbm, right_hbm,
    list_ref, weight_ref, count_ref, left_ref, right_ref, start_ref, sems,
):
    copies = [
        pltpu.make_async_copy(left_hbm, left_ref, sems.at[0]),
        pltpu.make_async_copy(right_hbm, right_ref, sems.at[1]),
    ]
    for copy in copies:
        copy.start()
    pairs = place_ref.shape[0]
    sources = start_ref.shape[0] - 1
    targets = pairs // coef_ref.shape[0]

    def clear_start(s, carry):
        start_ref[s] = 0
        return carry

    def count(i, carry):
        place = place_ref[i]
        start_ref[place] = start_ref[place] + 1
        return carry

    def start_of(s, total):
        held = start_ref[s]
        start_ref[s] = total
        return total + held

    def put(i, carry):
        place = place_ref[i]
        at = start_ref[place]
        start_ref[place] = at + 1
        list_ref[at] = i + pairs * place
        weight_ref[at] = coef_ref[lax.div(i, targets)]
        return carry

    def clear(i, carry):
        list_ref[i] = 0
        weight_ref[i] = 0.0
        return carry

    lax.fori_loop(0, sources + 1, clear_start, 0)
    lax.fori_loop(0, pairs, count, 0)
    total = lax.fori_loop(0, sources, start_of, 0)
    start_ref[sources] = total
    lax.fori_loop(0, pairs, put, 0)
    lax.fori_loop(total, pairs + GROUP, clear, 0)
    count_ref[0] = total
    for copy in copies:
        copy.wait()


def add_kernel(parts_ref, out_ref):
    total = parts_ref[0].astype(jnp.float32)
    for i in range(1, parts_ref.shape[0]):
        total += parts_ref[i].astype(jnp.float32)
    out_ref[...] = total.astype(out_ref.dtype)


def terms_kernel(list_ref, weight_ref, count_ref, left_ref, right_ref, *refs):
    blocks, (out_ref, tiles, sums, sems) = refs[:-4], refs[-4:]
    n_x, n_z = out_ref.shape[:2]
    targets, tile, _ = sums.shape
    sec_dev = blocks[0].shape[0]
    pairs = left_ref.shape[0] * targets
    band = tile // (n_x * n_z)

    def fetch(b):
        return pltpu.make_async_copy(
            blocks[b], tiles.at[pl.ds(b * sec_dev, sec_dev)], sems.at[b]
        )

    for b in range(len(blocks)):
        fetch(b).start()
    sums[...] = jnp.zeros_like(sums)

    def step(g, ready):
        codes = [list_ref[g * GROUP + j] for j in range(GROUP)]
        origins = [lax.div(code, pairs) for code in codes]
        needed = lax.div(functools.reduce(jnp.maximum, origins), sec_dev) + 1
        for b in range(len(blocks)):
            pl.when(jnp.logical_and(ready <= b, b < needed))(fetch(b).wait)
        images = []
        for j in range(GROUP):
            pair = lax.rem(codes[j], pairs)
            term = lax.div(pair, targets)
            mixed = jnp.dot(
                left_ref[term], tiles[origins[j]], preferred_element_type=jnp.float32
            ).astype(jnp.bfloat16)
            image = jnp.dot(mixed, right_ref[term], preferred_element_type=jnp.float32)
            images.append((lax.rem(pair, targets), image * weight_ref[g * GROUP + j]))
        for target, image in images:
            sums[target] += image
        return jnp.maximum(ready, needed)

    ready = lax.fori_loop(0, lax.div(count_ref[0] + GROUP - 1, GROUP), step, 0)
    for b in range(len(blocks)):
        pl.when(ready <= b)(fetch(b).wait)
    for t in range(0, targets, 2):
        two = [sums[t + i].reshape(n_z, n_x, band, tile) for i in range(2)]
        rows = jnp.concatenate(two, axis=2).astype(out_ref.dtype)
        for x in range(n_x):
            out_ref[x, :, pl.ds(t * band, 2 * band), :] = rows[:, x]


def per_device(psi, left_ops, right_ops, coef, source, active, left_block, right_block):
    sec_dev, tile, _ = psi.shape
    term_dev = left_ops.shape[0]
    n_z, n_x, n_y, cores = (lax.axis_size(name) for name in NAMES)
    n_ops = n_z * n_x
    targets = 2 * sec_dev
    pairs = term_dev * targets
    band = tile // n_ops
    sources = len(PLACES) * 2 * sec_dev
    ops_index = lax.axis_index("z") * n_x + lax.axis_index("x")
    core = lax.axis_index("core").astype(jnp.int32)
    ring = lax.axis_index("y").astype(jnp.int32)
    smem = pl.BlockSpec(memory_space=pltpu.SMEM)
    vmem = pl.BlockSpec(memory_space=pltpu.VMEM)
    anywhere = pl.BlockSpec(memory_space=pl.ANY)

    def from_y(value, away):
        pairs = [(((y + a) % n_y) * 2 + c, y * 2 + c) for y in range(n_y) for c, a in ((0, away), (1, -away))]
        return lax.ppermute(value, ("y", "core"), pairs)

    def from_core(value):
        return lax.ppermute(value, "core", [(0, 1), (1, 0)])

    code = jnp.where(active != 0, source, -1)
    code, psi_out = lax.optimization_barrier((code, psi))
    codes = jnp.concatenate([code, from_y(code, n_y // 2)], axis=1)
    near = [from_y(psi_out, 1), from_y(psi_out, -1)]
    their_psi = from_core(psi_out)
    pair_list, weights, count, left_near, right_near = pl.pallas_call(
        plan_kernel,
        out_shape=(
            jax.ShapeDtypeStruct((pairs + GROUP,), jnp.int32),
            jax.ShapeDtypeStruct((pairs + GROUP,), jnp.float32),
            jax.ShapeDtypeStruct((1,), jnp.int32),
            jax.ShapeDtypeStruct(left_ops.shape, left_ops.dtype),
            jax.ShapeDtypeStruct(right_ops.shape, right_ops.dtype),
        ),
        in_specs=[smem] * 2 + [anywhere] * 2,
        out_specs=(smem,) * 3 + (vmem,) * 2,
        scratch_shapes=[
            pltpu.SMEM((sources + 1,), jnp.int32),
            pltpu.SemaphoreType.DMA((2,)),
        ],
        compiler_params=pltpu.CompilerParams(vmem_limit_bytes=56 * 2**20),
        name="plan",
    )(places_of(codes, sec_dev, core, ring).reshape(pairs), coef, left_ops, right_ops)

    count, near = lax.optimization_barrier((count, near))
    mine = [psi, *near, from_y(near[0], 1)]
    theirs = [their_psi] + [from_core(block) for block in mine[1:]]
    blocks = [None] * (2 * len(PLACES))
    for (_, other, own), my_block, their_block in zip(PLACES, mine, theirs):
        blocks[own], blocks[other] = my_block, their_block

    partial_sum = pl.pallas_call(
        terms_kernel,
        out_shape=jax.ShapeDtypeStruct((n_x, n_z, targets * band, tile), jnp.bfloat16),
        in_specs=[smem] * 3 + [vmem] * 2 + [anywhere] * len(blocks),
        out_specs=vmem,
        scratch_shapes=[
            pltpu.VMEM((sources, tile, tile), psi.dtype),
            pltpu.VMEM((targets, tile, tile), jnp.float32),
            pltpu.SemaphoreType.DMA((len(blocks),)),
        ],
        compiler_params=pltpu.CompilerParams(vmem_limit_bytes=24 * 2**20),
        cost_estimate=pl.CostEstimate(
            flops=pairs * tile**3, bytes_accessed=10 * 2**20, transcendentals=0
        ),
        name="terms",
    )(pair_list, weights, count, left_near, right_near, *blocks)

    local_rows = lax.dynamic_slice_in_dim(psi, ops_index * band, band, 1)
    block_rows = lax.dynamic_slice_in_dim(left_block, ops_index * band, band, 1)
    local_part = jnp.einsum("tij,tjl->til", block_rows, psi, preferred_element_type=jnp.float32)
    local_part = local_part + jnp.einsum(
        "tij,tjl->til", local_rows, right_block, preferred_element_type=jnp.float32
    )

    bands = lax.all_to_all(partial_sum, "x", 0, 0, tiled=True)
    bands = pl.pallas_call(
        add_kernel,
        out_shape=jax.ShapeDtypeStruct(bands.shape[1:], bands.dtype),
        in_specs=[vmem],
        out_specs=vmem,
        name="add",
    )(bands)
    bands = lax.all_to_all(bands, "z", 0, 0, tiled=True)
    summed = jnp.sum(bands.astype(jnp.float32), axis=0).reshape(2, sec_dev, band, tile)
    return local_part + summed[0] + from_y(summed[1], n_y // 2)


def solution(mesh):
    full = Mesh(mesh.devices.reshape(AXES), NAMES)
    ops, sec = ("z", "x"), ("y", "core")
    in_specs = (
        P(sec, None, None),
        P(ops, None, None),
        P(ops, None, None),
        P(ops),
        P(ops, sec),
        P(ops, sec),
        P(sec, None, None),
        P(sec, None, None),
    )
    return jax.shard_map(
        per_device, mesh=full, in_specs=in_specs, out_specs=P(sec, ops, None), check_vma=False
    )
```

time: 416 us -> 107 us (0.26)
  the two profiles are of different devices: /device:TPU:24 before, /device:TPU:8 now
where the time goes in v1:
time: 107 us; the launch traced here: 106 us
  starting transfers between devices  38.4 us (36%)
  waiting for transfers between devices  27.5 us (26%)
  blocking collectives  18.7 us (17%)
  Pallas kernels  14.5 us (14%)
  local copies, waits for them, and re-layouts  4.72 us (4%)
  other arithmetic  1.39 us (1%)
    ppermute x5, starting transfers between devices, from_y(): return lax.ppermute(value, ('y', 'core'), pairs)  19.3 us
    all_to_all x1, blocking collectives, per_device(): bands = lax.all_to_all(partial_sum, 'x', 0, 0, tiled=True)  18.7 us
    ppermute x5, waiting for transfers between devices, from_y(): return lax.ppermute(value, ('y', 'core'), pairs)  15 us
    all_to_all x1, starting transfers between devices, per_device(): bands = lax.all_to_all(bands, 'z', 0, 0, tiled=True)  10.8 us
    all_to_all x1, waiting for transfers between devices, per_device(): bands = lax.all_to_all(bands, 'z', 0, 0, tiled=True)  10.7 us
    ppermute x4, starting transfers between devices, from_core(): return lax.ppermute(value, 'core', [(0, 1), (1, 0)])  8.26 us
    pallas_call x1, Pallas kernels, per_device(): pl.pallas_call(terms_kernel, out_shape=jax.ShapeDtypeStruct((n_x, n_z, ta...  6.36 us
    pallas_call x1, Pallas kernels, per_device(): pl.pallas_call(plan_kernel, out_shape=(jax.ShapeDtypeStruct((pairs + GROU...  6.08 us
  transfers between devices with their start and end apart: 10, of which 5 were waited for; matrix products, arithmetic and copies ran while one was open for 1% of the time, Pallas kernels for 6%

profile of v1, /device:TPU:8, one launch (start us, length us, event | category | flops | bytes accessed | tf_op | source)
XLA Modules:
  0.0 106.3 jit_solution(1701389872822033765)
XLA Ops:
  0.0 0.0 copy-start
  0.0 0.8 compare_select_fusion.15
  0.8 7.7 %collective-permute-start.1 = (bf16[4,256,256]{2,1,0:T(8,128)(2,1)}, bf16[4,256,256]{2,1,0:T(8,128)(2,1)S(1)}, u32[]{:S(2)}, u32[]{:S(2)}) collective-permute-start(bf16[4,256,256]{2,1,0:T(8,128)(2,1)} %refs_0_.1), channel_id=1, source_target_pairs={{2,0},{15,1},{4,2},{1,3},{6,4},{3,5},{8,6},{5,7},{10,8},{7,9},{12,... | collective-permute-start | bytes 1572872 | tf_op jit(solution)/shard_map/ppermute | solution.py:151
  8.5 1.9 %collective-permute-start.2 = (bf16[4,256,256]{2,1,0:T(8,128)(2,1)}, bf16[4,256,256]{2,1,0:T(8,128)(2,1)S(1)}, u32[]{:S(2)}, u32[]{:S(2)}) collective-permute-start(bf16[4,256,256]{2,1,0:T(8,128)(2,1)} %refs_0_.1), channel_id=1, source_target_pairs={{14,0},{3,1},{0,2},{5,3},{2,4},{7,5},{4,6},{9,7},{6,8},{11,9},{8,1... | collective-permute-start | bytes 1572872 | tf_op jit(solution)/shard_map/ppermute | solution.py:151
  10.4 3.0 %collective-permute-start = (s32[16,4]{0,1:T(4,128)S(1)}, s32[16,4]{0,1:T(4,128)S(1)}, u32[]{:S(2)}, u32[]{:S(2)}) collective-permute-start(s32[16,4]{0,1:T(4,128)S(1)} %compare_select_fusion.15), channel_id=1, source_target_pairs={{8,0},{9,1},{10,2},{11,3},{12,4},{13,5},{14,6},{15,7},{0,8},{1,9},... | collective-permute-start | bytes 776 | tf_op jit(solution)/shard_map/ppermute | solution.py:151
  13.5 7.3 %collective-permute-done = s32[16,4]{0,1:T(4,128)S(1)} collective-permute-done((s32[16,4]{0,1:T(4,128)S(1)}, s32[16,4]{0,1:T(4,128)S(1)}, u32[]{:S(2)}, u32[]{:S(2)}) %collective-permute-start) | collective-permute-done | bytes 288 | tf_op jit(solution)/shard_map/ppermute | solution.py:151
  20.8 0.1 copy.10
  20.8 0.1 concatenate.6
  20.9 0.6 and_select_fusion.1.place_ref
  21.5 0.0 copy-start.1
  21.5 6.1 %plan.1 = (s32[132]{0:T(256)}, f32[132]{0:T(256)}, s32[1]{0:T(128)}, bf16[16,256,256]{2,1,0:T(8,128)(2,1)}, bf16[16,256,256]{2,1,0:T(8,128)(2,1)}) custom-call(s32[128]{0:T(128)} %and_select_fusion.1.place_ref, f32[16]{0:T(128)} %coef_ref.1, bf16[16,256,256]{2,1,0:T(8,128)(2,1)} %left_hbm.1, bf16[16,256,256]{2,1,0:T(8,128)(2,1)} %right_hbm.1), custom_call_target="tpu_custom_call" | custom-call | tf_op jit(solution)/shard_map/plan/pallas_call | solution.py:161
  27.6 0.0 collective-permute-done.1.refs_2_
  27.6 0.0 collective-permute-done.2.refs_3_
  27.6 3.1 %collective-permute-start.6 = (bf16[4,256,256]{2,1,0:T(8,128)(2,1)S(1)}, bf16[4,256,256]{2,1,0:T(8,128)(2,1)S(1)}, u32[]{:S(2)}, u32[]{:S(2)}) collective-permute-start(bf16[4,256,256]{2,1,0:T(8,128)(2,1)S(1)} %collective-permute-done.1.refs_2_), channel_id=1, source_target_pairs={{2,0},{15,1},{4,2},{1,3},{6,4},{3,5},{8,6},{5,7},{10,8},{7,9},{12,... | collective-permute-start | bytes 1572872 | tf_op jit(solution)/shard_map/ppermute | solution.py:151
  30.7 0.0 copy-done.1
  30.7 1.9 %collective-permute-start.3 = (bf16[4,256,256]{2,1,0:T(8,128)(2,1)S(1)}, bf16[4,256,256]{2,1,0:T(8,128)(2,1)S(1)}, u32[]{:S(2)}, u32[]{:S(2)}) collective-permute-start(bf16[4,256,256]{2,1,0:T(8,128)(2,1)S(1)} %copy-done.1), channel_id=1, source_target_pairs={{0,1},{1,0},{2,3},{3,2},{4,5},{5,4},{6,7},{7,6},{8,9},{9,8},{10,11... | collective-permute-start | bytes 1572872 | tf_op jit(solution)/shard_map/ppermute | solution.py:154
  32.7 2.4 %collective-permute-start.4 = (bf16[4,256,256]{2,1,0:T(8,128)(2,1)S(1)}, bf16[4,256,256]{2,1,0:T(8,128)(2,1)S(1)}, u32[]{:S(2)}, u32[]{:S(2)}) collective-permute-start(bf16[4,256,256]{2,1,0:T(8,128)(2,1)S(1)} %collective-permute-done.1.refs_2_), channel_id=1, source_target_pairs={{0,1},{1,0},{2,3},{3,2},{4,5},{5,4},{6,7},{7,6},{8,9},{9,8},{10,11... | collective-permute-start | bytes 1572872 | tf_op jit(solution)/shard_map/ppermute | solution.py:154
  35.1 1.9 %collective-permute-start.5 = (bf16[4,256,256]{2,1,0:T(8,128)(2,1)S(1)}, bf16[4,256,256]{2,1,0:T(8,128)(2,1)S(1)}, u32[]{:S(2)}, u32[]{:S(2)}) collective-permute-start(bf16[4,256,256]{2,1,0:T(8,128)(2,1)S(1)} %collective-permute-done.2.refs_3_), channel_id=1, source_target_pairs={{0,1},{1,0},{2,3},{3,2},{4,5},{5,4},{6,7},{7,6},{8,9},{9,8},{10,11... | collective-permute-start | bytes 1572872 | tf_op jit(solution)/shard_map/ppermute | solution.py:154
  37.0 1.7 %collective-permute-done.6.refs_6_ = bf16[4,256,256]{2,1,0:T(8,128)(2,1)S(1)} collective-permute-done((bf16[4,256,256]{2,1,0:T(8,128)(2,1)S(1)}, bf16[4,256,256]{2,1,0:T(8,128)(2,1)S(1)}, u32[]{:S(2)}, u32[]{:S(2)}) %collective-permute-start.6) | collective-permute-done | bytes 524320 | tf_op jit(solution)/shard_map/ppermute | solution.py:151
  38.7 2.0 %collective-permute-start.7 = (bf16[4,256,256]{2,1,0:T(8,128)(2,1)S(1)}, bf16[4,256,256]{2,1,0:T(8,128)(2,1)S(1)}, u32[]{:S(2)}, u32[]{:S(2)}) collective-permute-start(bf16[4,256,256]{2,1,0:T(8,128)(2,1)S(1)} %collective-permute-done.6.refs_6_), channel_id=1, source_target_pairs={{0,1},{1,0},{2,3},{3,2},{4,5},{5,4},{6,7},{7,6},{8,9},{9,8},{10,11... | collective-permute-start | bytes 1572872 | tf_op jit(solution)/shard_map/ppermute | solution.py:154
  40.7 0.0 collective-permute-done.3.refs_1_
  40.7 0.0 collective-permute-done.4.refs_4_
  40.7 0.0 collective-permute-done.5.refs_5_
  40.7 1.7 %collective-permute-done.7.refs_7_ = bf16[4,256,256]{2,1,0:T(8,128)(2,1)S(1)} collective-permute-done((bf16[4,256,256]{2,1,0:T(8,128)(2,1)S(1)}, bf16[4,256,256]{2,1,0:T(8,128)(2,1)S(1)}, u32[]{:S(2)}, u32[]{:S(2)}) %collective-permute-start.7) | collective-permute-done | bytes 524320 | tf_op jit(solution)/shard_map/ppermute | solution.py:154
  42.5 0.0 copy-start.2
  42.5 1.6 %copy-done.2 = bf16[16,256,256]{2,1,0:T(8,128)(2,1)S(1)} copy-done((bf16[16,256,256]{2,1,0:T(8,128)(2,1)S(1)}, bf16[16,256,256]{2,1,0:T(8,128)(2,1)}, u32[]{:S(2)}) %copy-start.2) | copy-done | bytes 2097176
  44.1 0.0 copy-start.3
  44.1 1.6 %copy-done.3 = bf16[16,256,256]{2,1,0:T(8,128)(2,1)S(1)} copy-done((bf16[16,256,256]{2,1,0:T(8,128)(2,1)S(1)}, bf16[16,256,256]{2,1,0:T(8,128)(2,1)}, u32[]{:S(2)}) %copy-start.3) | copy-done | bytes 2097176
  45.7 0.0 copy-start.4
  45.7 0.7 copy-done.4
  46.3 0.0 copy-start.5
  46.3 0.7 copy-done.5
  47.0 6.4 %terms.1 = bf16[4,8,64,256]{3,2,1,0:T(8,128)(2,1)S(1)} custom-call(s32[132]{0:T(256)S(1)} %copy-done.4, f32[132]{0:T(256)S(1)} %copy-done.5, s32[1]{0:T(128)} %get-tuple-element.20.count_ref, bf16[16,256,256]{2,1,0:T(8,128)(2,1)S(1)} %copy-done.2, bf16[16,256,256]{2,1,0:T(8,128)(2,1)S(1)} %copy-done.3, bf16[4,256,256]{2,1,0:T(8,128)(2,1)S(1)} %copy-done.1, ...), custom_call_target="tpu_custom_call" | custom-call | flops 2147483648 | bytes 10485760 | tf_op jit(solution)/shard_map/terms/pallas_call | solution.py:187
  53.4 0.0 copy-start.6
  53.4 18.7 %all_to_all.10.parts_ref = bf16[4,8,64,256]{3,2,1,0:T(8,128)(2,1)} all-to-all(bf16[4,8,64,256]{3,2,1,0:T(8,128)(2,1)S(1)} %terms.1), channel_id=1, replica_groups=mesh['z'=8,'x'=4,'y'=8,'core'=2] {'x'}, dimensions={0} | all-to-all | bytes 2097152 | tf_op jit(solution)/shard_map/all_to_all | solution.py:211
  72.1 2.1 %add.125 = bf16[8,64,256]{2,1,0:T(8,128)(2,1)} custom-call(bf16[4,8,64,256]{3,2,1,0:T(8,128)(2,1)} %all_to_all.10.parts_ref), custom_call_target="tpu_custom_call" | custom-call | tf_op jit(solution)/shard_map/add/pallas_call | solution.py:212
  74.1 10.8 %all-to-all-start.1 = ((bf16[8,64,256]{2,1,0:T(8,128)(2,1)}), bf16[8,64,256]{2,1,0:T(8,128)(2,1)S(1)}, u32[]{:S(2)}, u32[]{:S(2)}) async-start(bf16[8,64,256]{2,1,0:T(8,128)(2,1)} %add.125), calls=%async_computation.1 | async-start | bytes 524288 | tf_op jit(solution)/shard_map/all_to_all | solution.py:219
  85.0 10.7 %all-to-all-done.1 = bf16[8,64,256]{2,1,0:T(8,128)(2,1)S(1)} async-done(((bf16[8,64,256]{2,1,0:T(8,128)(2,1)}), bf16[8,64,256]{2,1,0:T(8,128)(2,1)S(1)}, u32[]{:S(2)}, u32[]{:S(2)}) %all-to-all-start.1) | async-done | bytes 262176 | tf_op jit(solution)/shard_map/all_to_all | solution.py:219
  95.8 3.5 %collective-permute-start.8 = (f32[4,8,256]{2,1,0:T(8,128)S(1)}, f32[4,8,256]{2,1,0:T(8,128)S(1)}, u32[]{:S(2)}, u32[]{:S(2)}) collective-permute-start(f32[4,8,256]{2,1,0:T(8,128)S(1)} %slice_bitcast_fusion), channel_id=1, source_target_pairs={{8,0},{9,1},{10,2},{11,3},{12,4},{13,5},{14,6},{15,7},{0,8},{1,9},... | collective-permute-start | bytes 98312 | tf_op jit(solution)/shard_map/ppermute | solution.py:151
  99.3 0.0 copy-done
  99.3 0.2 fusion.3
  99.5 6.0 %collective-permute-done.8 = f32[4,8,256]{2,1,0:T(8,128)S(1)} collective-permute-done((f32[4,8,256]{2,1,0:T(8,128)S(1)}, f32[4,8,256]{2,1,0:T(8,128)S(1)}, u32[]{:S(2)}, u32[]{:S(2)}) %collective-permute-start.8) | collective-permute-done | bytes 32800 | tf_op jit(solution)/shard_map/ppermute | solution.py:151
  105.5 0.0 copy-done.6
  105.5 0.8 fusion.1
  (3 shorter events, 0.1 us)
Async XLA Ops:
  0.0 99.3 %copy-start = (bf16[4,256,256]{2,1,0:T(8,128)(2,1)S(1)}, bf16[4,256,256]{2,1,0:T(8,128)(2,1)}, u32[]{:S(2)}) copy-start(bf16[4,256,256]{2,1,0:T(8,128)(2,1)} %param.14) | copy-start | bytes 1572868
  0.8 26.8 %collective-permute-start.1 = (bf16[4,256,256]{2,1,0:T(8,128)(2,1)}, bf16[4,256,256]{2,1,0:T(8,128)(2,1)S(1)}, u32[]{:S(2)}, u32[]{:S(2)}) collective-permute-start(bf16[4,256,256]{2,1,0:T(8,128)(2,1)} %refs_0_.1), channel_id=1, source_target_pairs={{2,0},{15,1},{4,2},{1,3},{6,4},{3,5},{8,6},{5,7},{10,8},{7,9},{12,... | collective-permute-start | bytes 1572872 | tf_op jit(solution)/shard_map/ppermute | solution.py:151
  8.5 19.1 %collective-permute-start.2 = (bf16[4,256,256]{2,1,0:T(8,128)(2,1)}, bf16[4,256,256]{2,1,0:T(8,128)(2,1)S(1)}, u32[]{:S(2)}, u32[]{:S(2)}) collective-permute-start(bf16[4,256,256]{2,1,0:T(8,128)(2,1)} %refs_0_.1), channel_id=1, source_target_pairs={{14,0},{3,1},{0,2},{5,3},{2,4},{7,5},{4,6},{9,7},{6,8},{11,9},{8,1... | collective-permute-start | bytes 1572872 | tf_op jit(solution)/shard_map/ppermute | solution.py:151
  10.4 10.3 %collective-permute-start = (s32[16,4]{0,1:T(4,128)S(1)}, s32[16,4]{0,1:T(4,128)S(1)}, u32[]{:S(2)}, u32[]{:S(2)}) collective-permute-start(s32[16,4]{0,1:T(4,128)S(1)} %compare_select_fusion.15), channel_id=1, source_target_pairs={{8,0},{9,1},{10,2},{11,3},{12,4},{13,5},{14,6},{15,7},{0,8},{1,9},... | collective-permute-start | bytes 776 | tf_op jit(solution)/shard_map/ppermute | solution.py:151
  21.5 9.2 %copy-start.1 = (bf16[4,256,256]{2,1,0:T(8,128)(2,1)S(1)}, bf16[4,256,256]{2,1,0:T(8,128)(2,1)}, u32[]{:S(2)}) copy-start(bf16[4,256,256]{2,1,0:T(8,128)(2,1)} %refs_0_.1) | copy-start | bytes 1572868
  27.6 11.1 %collective-permute-start.6 = (bf16[4,256,256]{2,1,0:T(8,128)(2,1)S(1)}, bf16[4,256,256]{2,1,0:T(8,128)(2,1)S(1)}, u32[]{:S(2)}, u32[]{:S(2)}) collective-permute-start(bf16[4,256,256]{2,1,0:T(8,128)(2,1)S(1)} %collective-permute-done.1.refs_2_), channel_id=1, source_target_pairs={{2,0},{15,1},{4,2},{1,3},{6,4},{3,5},{8,6},{5,7},{10,8},{7,9},{12,... | collective-permute-start | bytes 1572872 | tf_op jit(solution)/shard_map/ppermute | solution.py:151
  30.7 10.0 %collective-permute-start.3 = (bf16[4,256,256]{2,1,0:T(8,128)(2,1)S(1)}, bf16[4,256,256]{2,1,0:T(8,128)(2,1)S(1)}, u32[]{:S(2)}, u32[]{:S(2)}) collective-permute-start(bf16[4,256,256]{2,1,0:T(8,128)(2,1)S(1)} %copy-done.1), channel_id=1, source_target_pairs={{0,1},{1,0},{2,3},{3,2},{4,5},{5,4},{6,7},{7,6},{8,9},{9,8},{10,11... | collective-permute-start | bytes 1572872 | tf_op jit(solution)/shard_map/ppermute | solution.py:154
  32.7 8.0 %collective-permute-start.4 = (bf16[4,256,256]{2,1,0:T(8,128)(2,1)S(1)}, bf16[4,256,256]{2,1,0:T(8,128)(2,1)S(1)}, u32[]{:S(2)}, u32[]{:S(2)}) collective-permute-start(bf16[4,256,256]{2,1,0:T(8,128)(2,1)S(1)} %collective-permute-done.1.refs_2_), channel_id=1, source_target_pairs={{0,1},{1,0},{2,3},{3,2},{4,5},{5,4},{6,7},{7,6},{8,9},{9,8},{10,11... | collective-permute-start | bytes 1572872 | tf_op jit(solution)/shard_map/ppermute | solution.py:154
  35.1 5.6 %collective-permute-start.5 = (bf16[4,256,256]{2,1,0:T(8,128)(2,1)S(1)}, bf16[4,256,256]{2,1,0:T(8,128)(2,1)S(1)}, u32[]{:S(2)}, u32[]{:S(2)}) collective-permute-start(bf16[4,256,256]{2,1,0:T(8,128)(2,1)S(1)} %collective-permute-done.2.refs_3_), channel_id=1, source_target_pairs={{0,1},{1,0},{2,3},{3,2},{4,5},{5,4},{6,7},{7,6},{8,9},{9,8},{10,11... | collective-permute-start | bytes 1572872 | tf_op jit(solution)/shard_map/ppermute | solution.py:154
  38.7 3.8 %collective-permute-start.7 = (bf16[4,256,256]{2,1,0:T(8,128)(2,1)S(1)}, bf16[4,256,256]{2,1,0:T(8,128)(2,1)S(1)}, u32[]{:S(2)}, u32[]{:S(2)}) collective-permute-start(bf16[4,256,256]{2,1,0:T(8,128)(2,1)S(1)} %collective-permute-done.6.refs_6_), channel_id=1, source_target_pairs={{0,1},{1,0},{2,3},{3,2},{4,5},{5,4},{6,7},{7,6},{8,9},{9,8},{10,11... | collective-permute-start | bytes 1572872 | tf_op jit(solution)/shard_map/ppermute | solution.py:154
  42.5 1.6 %copy-start.2 = (bf16[16,256,256]{2,1,0:T(8,128)(2,1)S(1)}, bf16[16,256,256]{2,1,0:T(8,128)(2,1)}, u32[]{:S(2)}) copy-start(bf16[16,256,256]{2,1,0:T(8,128)(2,1)} %get-tuple-element.21.left_ref) | copy-start | bytes 6291460
  44.1 1.6 %copy-start.3 = (bf16[16,256,256]{2,1,0:T(8,128)(2,1)S(1)}, bf16[16,256,256]{2,1,0:T(8,128)(2,1)}, u32[]{:S(2)}) copy-start(bf16[16,256,256]{2,1,0:T(8,128)(2,1)} %get-tuple-element.22.right_ref) | copy-start | bytes 6291460
  45.7 0.7 copy-start.4
  46.3 0.7 copy-start.5
  53.4 52.1 %copy-start.6 = (bf16[4,256,256]{2,1,0:T(8,128)(2,1)S(1)}, bf16[4,256,256]{2,1,0:T(8,128)(2,1)}, u32[]{:S(2)}) copy-start(bf16[4,256,256]{2,1,0:T(8,128)(2,1)} %param.15) | copy-start | bytes 1572868
  74.1 21.6 %all-to-all-start.1 = ((bf16[8,64,256]{2,1,0:T(8,128)(2,1)}), bf16[8,64,256]{2,1,0:T(8,128)(2,1)S(1)}, u32[]{:S(2)}, u32[]{:S(2)}) async-start(bf16[8,64,256]{2,1,0:T(8,128)(2,1)} %add.125), calls=%async_computation.1 | async-start | bytes 524288 | tf_op jit(solution)/shard_map/all_to_all | solution.py:219
  95.8 9.7 %collective-permute-start.8 = (f32[4,8,256]{2,1,0:T(8,128)S(1)}, f32[4,8,256]{2,1,0:T(8,128)S(1)}, u32[]{:S(2)}, u32[]{:S(2)}) collective-permute-start(f32[4,8,256]{2,1,0:T(8,128)S(1)} %slice_bitcast_fusion), channel_id=1, source_target_pairs={{8,0},{9,1},{10,2},{11,3},{12,4},{13,5},{14,6},{15,7},{0,8},{1,9},... | collective-permute-start | bytes 98312 | tf_op jit(solution)/shard_map/ppermute | solution.py:151

commit v2 on v1

v2 whole, which is shorter than its diff:
```python
import functools

import jax
import jax.numpy as jnp
from jax import lax
from jax.experimental import pallas as pl
from jax.experimental.pallas import tpu as pltpu
from jax.sharding import Mesh, PartitionSpec as P

AXES = (8, 4, 2, 4, 2)
NAMES = ("z", "x", "half", "y", "core")
GROUP = 4

PLACES = ((0, 1, 0), (1, 4, 2), (-1, 5, 3), (2, 7, 6))
EARLY = 2


def places_of(codes, sec_dev, core, ring, length):
    source_core = (codes // sec_dev) % 2
    away = (codes // (2 * sec_dev) - ring) * jnp.where(source_core == 0, 1, -1)
    block = jnp.full_like(codes, -1)
    for far, other, own in PLACES:
        here = (away - far) % length == 0
        block = jnp.where(here, jnp.where(source_core == core, own, other), block)
    held = jnp.logical_and(codes >= 0, block >= 0)
    return jnp.where(held, block * sec_dev + codes % sec_dev, 2 * len(PLACES) * sec_dev)


def sorted_pairs(places):
    pairs = places.shape[0]
    pair = jnp.arange(pairs, dtype=jnp.int32)
    keys = places * pairs + pair
    rank = jnp.sum((keys[None, :] < keys[:, None]).astype(jnp.int32), axis=1)
    return jnp.sum(jnp.where(rank[None, :] == pair[:, None], keys[None, :], 0), axis=1)


def add_pairs(first, last, first_place, list_ref, coef_ref, left_ref, right_ref, blocks, tiles, sems, sums):
    targets = sums.shape[0]
    pairs = list_ref.shape[0]
    sec_dev = blocks[0].shape[0]

    def fetch(b):
        return pltpu.make_async_copy(
            blocks[b], tiles.at[pl.ds(b * sec_dev, sec_dev)], sems.at[b]
        )

    def step(g, ready):
        work = []
        for j in range(GROUP):
            at = first + g * GROUP + j
            valid = at < last
            code = list_ref[jnp.minimum(at, pairs - 1)]
            code = jnp.where(valid, code, pairs * first_place)
            pair = lax.rem(code, pairs)
            term = lax.div(pair, targets)
            weight = jnp.where(valid, coef_ref[term], 0.0)
            work.append((lax.div(code, pairs) - first_place, term, lax.rem(pair, targets), weight))
        needed = lax.div(functools.reduce(jnp.maximum, [w[0] for w in work]), sec_dev) + 1
        for b in range(len(blocks)):
            pl.when(jnp.logical_and(ready <= b, b < needed))(fetch(b).wait)
        images = []
        for place, term, target, weight in work:
            mixed = jnp.dot(
                left_ref[term], tiles[place], preferred_element_type=jnp.float32
            ).astype(jnp.bfloat16)
            image = jnp.dot(mixed, right_ref[term], preferred_element_type=jnp.float32)
            images.append((target, image * weight))
        for target, image in images:
            sums[target] += image
        return jnp.maximum(ready, needed)

    ready = lax.fori_loop(0, lax.div(last - first + GROUP - 1, GROUP), step, 0)
    for b in range(len(blocks)):
        pl.when(ready <= b)(fetch(b).wait)


def start_fetches(blocks, tiles, sems):
    sec_dev = blocks[0].shape[0]
    for b, block in enumerate(blocks):
        pltpu.make_async_copy(block, tiles.at[pl.ds(b * sec_dev, sec_dev)], sems.at[b]).start()


def early_kernel(list_ref, count_ref, coef_ref, left_hbm, right_hbm, *refs):
    blocks, (sums, left_ref, right_ref, tiles, sems, op_sems) = refs[:-6], refs[-6:]
    copies = [
        pltpu.make_async_copy(left_hbm, left_ref, op_sems.at[0]),
        pltpu.make_async_copy(right_hbm, right_ref, op_sems.at[1]),
    ]
    for copy in copies:
        copy.start()
    start_fetches(blocks, tiles, sems)
    sums[...] = jnp.zeros_like(sums)
    for copy in copies:
        copy.wait()
    add_pairs(0, count_ref[0], 0, list_ref, coef_ref, left_ref, right_ref, blocks, tiles, sems, sums)


def terms_kernel(list_ref, count_ref, coef_ref, left_ref, right_ref, early_ref, *refs):
    blocks, (out_ref, tiles, sums, sems) = refs[:-4], refs[-4:]
    n_x, n_z = out_ref.shape[:2]
    targets, tile, _ = sums.shape
    band = tile // (n_x * n_z)
    start_fetches(blocks, tiles, sems)
    sums[...] = early_ref[...]
    add_pairs(
        count_ref[0], count_ref[1], EARLY * blocks[0].shape[0],
        list_ref, coef_ref, left_ref, right_ref, blocks, tiles, sems, sums,
    )
    for t in range(0, targets, 2):
        two = [sums[t + i].reshape(n_z, n_x, band, tile) for i in range(2)]
        rows = jnp.concatenate(two, axis=2).astype(out_ref.dtype)
        for x in range(n_x):
            out_ref[x, :, pl.ds(t * band, 2 * band), :] = rows[:, x]


def add_kernel(parts_ref, out_ref):
    def add(i, carry):
        total = parts_ref[0, i].astype(jnp.float32)
        for part in range(1, parts_ref.shape[0]):
            total += parts_ref[part, i].astype(jnp.float32)
        out_ref[i] = total.astype(out_ref.dtype)
        return carry

    lax.fori_loop(0, out_ref.shape[0], add, 0)


def per_device(psi, left_ops, right_ops, coef, source, active, left_block, right_block):
    sec_dev, tile, _ = psi.shape
    term_dev = left_ops.shape[0]
    n_z, n_x, halves, half_y, cores = (lax.axis_size(name) for name in NAMES)
    n_ops, n_y = n_z * n_x, halves * half_y
    targets = halves * sec_dev
    pairs = term_dev * targets
    band = tile // n_ops
    ops_index = lax.axis_index("z") * n_x + lax.axis_index("x")
    core, half = lax.axis_index("core"), lax.axis_index("half")
    ring = half * half_y + lax.axis_index("y")
    smem = pl.BlockSpec(memory_space=pltpu.SMEM)
    vmem = pl.BlockSpec(memory_space=pltpu.VMEM)
    anywhere = pl.BlockSpec(memory_space=pl.ANY)

    def from_y(value, away):
        route = [(((y + a) % n_y) * 2 + c, y * 2 + c) for y in range(n_y) for c, a in ((0, away), (1, -away))]
        return lax.ppermute(value, ("half", "y", "core"), route)

    def from_core(value):
        return lax.ppermute(value, "core", [(0, 1), (1, 0)])

    far = from_y(psi, 2)
    near = [from_y(psi, 1), from_y(psi, -1)]
    their_psi = from_core(psi)

    code = jnp.where(active != 0, source, -1)
    other = from_y(code, n_y // 2)
    codes = jnp.concatenate(
        [jnp.where(half == 0, code, other), jnp.where(half == 0, other, code)], axis=1
    )
    places = places_of(codes, sec_dev, core, ring, n_y).reshape(pairs)
    pair_list = sorted_pairs(places)
    limits = jnp.array([EARLY, 2 * len(PLACES)], jnp.int32) * sec_dev
    counts = jnp.sum((places[None, :] < limits[:, None]).astype(jnp.int32), axis=1)

    early, left_near, right_near = pl.pallas_call(
        early_kernel,
        out_shape=(
            jax.ShapeDtypeStruct((targets, tile, tile), jnp.float32),
            jax.ShapeDtypeStruct(left_ops.shape, left_ops.dtype),
            jax.ShapeDtypeStruct(right_ops.shape, right_ops.dtype),
        ),
        in_specs=[smem] * 3 + [anywhere] * (2 + EARLY),
        out_specs=(vmem,) * 3,
        scratch_shapes=[
            pltpu.VMEM((EARLY * sec_dev, tile, tile), psi.dtype),
            pltpu.SemaphoreType.DMA((EARLY,)),
            pltpu.SemaphoreType.DMA((2,)),
        ],
        compiler_params=pltpu.CompilerParams(vmem_limit_bytes=16 * 2**20),
        name="early",
    )(pair_list, counts, coef, left_ops, right_ops, psi, their_psi)

    early, near = lax.optimization_barrier((early, near))
    mine = [psi, *near, far]
    theirs = [their_psi] + [from_core(block) for block in mine[1:]]
    blocks = [None] * (2 * len(PLACES))
    for (_, other, own), my_block, their_block in zip(PLACES, mine, theirs):
        blocks[own], blocks[other] = my_block, their_block
    blocks = blocks[EARLY:]

    partial_sum = pl.pallas_call(
        terms_kernel,
        out_shape=jax.ShapeDtypeStruct((n_x, n_z, targets * band, tile), jnp.bfloat16),
        in_specs=[smem] * 3 + [vmem] * 3 + [anywhere] * len(blocks),
        out_specs=vmem,
        scratch_shapes=[
            pltpu.VMEM((len(blocks) * sec_dev, tile, tile), psi.dtype),
            pltpu.VMEM((targets, tile, tile), jnp.float32),
            pltpu.SemaphoreType.DMA((len(blocks),)),
        ],
        compiler_params=pltpu.CompilerParams(vmem_limit_bytes=24 * 2**20),
        name="terms",
    )(pair_list, counts, coef, left_near, right_near, early, *blocks)

    local_rows = lax.dynamic_slice_in_dim(psi, ops_index * band, band, 1)
    block_rows = lax.dynamic_slice_in_dim(left_block, ops_index * band, band, 1)
    local_part = jnp.einsum("tij,tjl->til", block_rows, psi, preferred_element_type=jnp.float32)
    local_part = local_part + jnp.einsum(
        "tij,tjl->til", local_rows, right_block, preferred_element_type=jnp.float32
    )

    bands = lax.all_to_all(partial_sum, "x", 0, 0, tiled=True)
    bands = pl.pallas_call(
        add_kernel,
        out_shape=jax.ShapeDtypeStruct(bands.shape[1:], bands.dtype),
        in_specs=[vmem],
        out_specs=vmem,
        name="add",
    )(bands)
    bands = bands.reshape(n_z * halves, sec_dev * band, tile)
    bands = lax.all_to_all(bands, ("z", "half"), 0, 0, tiled=True)
    summed = jnp.sum(bands.astype(jnp.float32), axis=0).reshape(sec_dev, band, tile)
    return local_part + summed


def solution(mesh):
    full = Mesh(mesh.devices.reshape(AXES), NAMES)
    ops, sec = ("z", "x"), ("half", "y", "core")
    in_specs = (
        P(sec, None, None),
        P(ops, None, None),
        P(ops, None, None),
        P(ops),
        P(ops, sec),
        P(ops, sec),
        P(sec, None, None),
        P(sec, None, None),
    )
    return jax.shard_map(
        per_device, mesh=full, in_specs=in_specs, out_specs=P(sec, ops, None), check_vma=False
    )
```

time: 107 us -> 103 us (0.963)
  Pallas kernels: 14.5 us -> 6.62 us
  waiting for transfers between devices: 27.5 us -> 32.2 us
  starting transfers between devices: 38.4 us -> 36.6 us
    all_to_all x1, waiting for transfers between devices: 10.7 us -> 15.6 us  [per_device(): bands = lax.all_to_all(bands, ('z', 'half'), 0, 0, tiled=True)]
    pallas_call x1, Pallas kernels: 6.36 us -> 2.27 us  [per_device(): pl.pallas_call(terms_kernel, out_shape=jax.ShapeDtypeStruct((n_x, n_z, ta...]
    pallas_call x1, Pallas kernels: 6.08 us -> 2.26 us  [per_device(): pl.pallas_call(early_kernel, out_shape=(jax.ShapeDtypeStruct((targets, ti...]
    ppermute x5 -> x4, starting transfers between devices: 19.3 us -> 17 us  [from_y(): return lax.ppermute(value, ('half', 'y', 'core'), route)]
    reduce_sum x1 -> x4, other arithmetic: 0.04 us -> 1.17 us  [the longest x1 0.85 us: per_device(): jnp.sum((places[None, :] < limits[:, None]).astype(jnp.int32), axis=1)]
    unnamed x14 -> x16, local copies, waits for them, and re-layouts: 4.55 us -> 4.89 us
    ppermute x5 -> x4, waiting for transfers between devices: 15 us -> 14.7 us  [from_y(): return lax.ppermute(value, ('half', 'y', 'core'), route)]
  transfers between devices with their start and end apart: 10 -> 9, of which waited for: 5 -> 3; matrix products, arithmetic and copies ran while one was open for 1% -> 2% of each run, Pallas kernels for 6% -> 2%
where the time goes in v2:
time: 103 us; the launch traced here: 102 us
  starting transfers between devices  36.6 us (36%)
  waiting for transfers between devices  32.2 us (31%)
  blocking collectives  18.9 us (18%)
  Pallas kernels  6.62 us (6%)
  local copies, waits for them, and re-layouts  5.06 us (5%)
  other arithmetic  1.93 us (2%)
    all_to_all x1, blocking collectives, per_device(): bands = lax.all_to_all(partial_sum, 'x', 0, 0, tiled=True)  18.9 us
    ppermute x4, starting transfers between devices, from_y(): return lax.ppermute(value, ('half', 'y', 'core'), route)  17 us
    all_to_all x1, waiting for transfers between devices, per_device(): bands = lax.all_to_all(bands, ('z', 'half'), 0, 0, tiled=True)  15.6 us
    ppermute x4, waiting for transfers between devices, from_y(): return lax.ppermute(value, ('half', 'y', 'core'), route)  14.7 us
    all_to_all x1, starting transfers between devices, per_device(): bands = lax.all_to_all(bands, ('z', 'half'), 0, 0, tiled=True)  11.3 us
    ppermute x4, starting transfers between devices, from_core(): return lax.ppermute(value, 'core', [(0, 1), (1, 0)])  8.29 us
    unnamed x16, local copies, waits for them, and re-layouts  4.89 us
    pallas_call x1, Pallas kernels, per_device(): pl.pallas_call(terms_kernel, out_shape=jax.ShapeDtypeStruct((n_x, n_z, ta...  2.27 us
  transfers between devices with their start and end apart: 9, of which 3 were waited for; matrix products, arithmetic and copies ran while one was open for 2% of the time, Pallas kernels for 2%

profile of v2, /device:TPU:8, one launch (start us, length us, event | category | flops | bytes accessed | tf_op | source)
XLA Modules:
  0.0 102.5 jit_solution(14809547826687765636)
XLA Ops:
  0.0 0.0 copy-start
  0.0 2.0 %collective-permute-start.1 = (bf16[4,256,256]{2,1,0:T(8,128)(2,1)}, bf16[4,256,256]{2,1,0:T(8,128)(2,1)S(1)}, u32[]{:S(2)}, u32[]{:S(2)}) collective-permute-start(bf16[4,256,256]{2,1,0:T(8,128)(2,1)} %refs_0_.1), channel_id=1, source_target_pairs={{0,1},{1,0},{2,3},{3,2},{4,5},{5,4},{6,7},{7,6},{8,9},{9,8},{10,11... | collective-permute-start | bytes 1572872 | tf_op jit(solution)/shard_map/ppermute | solution.py:147
  2.1 7.7 %collective-permute-start.2 = (bf16[4,256,256]{2,1,0:T(8,128)(2,1)}, bf16[4,256,256]{2,1,0:T(8,128)(2,1)S(1)}, u32[]{:S(2)}, u32[]{:S(2)}) collective-permute-start(bf16[4,256,256]{2,1,0:T(8,128)(2,1)} %refs_0_.1), channel_id=1, source_target_pairs={{2,0},{15,1},{4,2},{1,3},{6,4},{3,5},{8,6},{5,7},{10,8},{7,9},{12,... | collective-permute-start | bytes 1572872 | tf_op jit(solution)/shard_map/ppermute | solution.py:144
  9.8 1.9 %collective-permute-start.3 = (bf16[4,256,256]{2,1,0:T(8,128)(2,1)}, bf16[4,256,256]{2,1,0:T(8,128)(2,1)S(1)}, u32[]{:S(2)}, u32[]{:S(2)}) collective-permute-start(bf16[4,256,256]{2,1,0:T(8,128)(2,1)} %refs_0_.1), channel_id=1, source_target_pairs={{14,0},{3,1},{0,2},{5,3},{2,4},{7,5},{4,6},{9,7},{6,8},{11,9},{8,1... | collective-permute-start | bytes 1572872 | tf_op jit(solution)/shard_map/ppermute | solution.py:144
  11.7 4.6 %collective-permute-start.6 = (bf16[4,256,256]{2,1,0:T(8,128)(2,1)}, bf16[4,256,256]{2,1,0:T(8,128)(2,1)S(1)}, u32[]{:S(2)}, u32[]{:S(2)}) collective-permute-start(bf16[4,256,256]{2,1,0:T(8,128)(2,1)} %refs_0_.1), channel_id=1, source_target_pairs={{4,0},{13,1},{6,2},{15,3},{8,4},{1,5},{10,6},{3,7},{12,8},{5,9},{1... | collective-permute-start | bytes 1572872 | tf_op jit(solution)/shard_map/ppermute | solution.py:144
  16.3 0.7 compare_select_fusion.15
  17.0 2.8 %collective-permute-start = (s32[16,4]{0,1:T(4,128)S(1)}, s32[16,4]{0,1:T(4,128)S(1)}, u32[]{:S(2)}, u32[]{:S(2)}) collective-permute-start(s32[16,4]{0,1:T(4,128)S(1)} %compare_select_fusion.15), channel_id=1, source_target_pairs={{8,0},{9,1},{10,2},{11,3},{12,4},{13,5},{14,6},{15,7},{0,8},{1,9},... | collective-permute-start | bytes 776 | tf_op jit(solution)/shard_map/ppermute | solution.py:144
  19.8 14.7 %collective-permute-done = s32[16,4]{0,1:T(4,128)S(1)} collective-permute-done((s32[16,4]{0,1:T(4,128)S(1)}, s32[16,4]{0,1:T(4,128)S(1)}, u32[]{:S(2)}, u32[]{:S(2)}) %collective-permute-start) | collective-permute-done | bytes 288 | tf_op jit(solution)/shard_map/ppermute | solution.py:144
  34.5 0.1 copy.12
  34.6 0.1 concatenate.6
  34.7 0.2 convert_reduce_fusion.1
  34.9 0.1 select_reduce_fusion.list_ref
  35.0 0.8 fusion.4.count_ref
  35.9 0.0 collective-permute-done.1.refs_1_
  35.9 0.0 copy-start.1
  35.9 1.0 %copy-done.1 = bf16[4,256,256]{2,1,0:T(8,128)(2,1)S(1)} copy-done((bf16[4,256,256]{2,1,0:T(8,128)(2,1)S(1)}, bf16[4,256,256]{2,1,0:T(8,128)(2,1)}, u32[]{:S(2)}) %copy-start.1) | copy-done | bytes 524312
  36.9 0.0 copy-start.3
  36.9 1.6 %copy-done.3 = bf16[16,256,256]{2,1,0:T(8,128)(2,1)S(1)} copy-done((bf16[16,256,256]{2,1,0:T(8,128)(2,1)S(1)}, bf16[16,256,256]{2,1,0:T(8,128)(2,1)}, u32[]{:S(2)}) %copy-start.3) | copy-done | bytes 2097176
  38.5 0.0 copy-start.4
  38.5 1.6 %copy-done.4 = bf16[16,256,256]{2,1,0:T(8,128)(2,1)S(1)} copy-done((bf16[16,256,256]{2,1,0:T(8,128)(2,1)S(1)}, bf16[16,256,256]{2,1,0:T(8,128)(2,1)}, u32[]{:S(2)}) %copy-start.4) | copy-done | bytes 2097176
  40.1 0.0 copy-start.5
  40.1 0.7 copy-done.5
  40.8 0.0 copy-start.6
  40.8 2.3 %early.1 = (f32[8,256,256]{2,1,0:T(8,128)S(1)}, bf16[16,256,256]{2,1,0:T(8,128)(2,1)S(1)}, bf16[16,256,256]{2,1,0:T(8,128)(2,1)S(1)}) custom-call(s32[128]{0:T(128)S(1)} %select_reduce_fusion.list_ref, s32[2]{0:T(128)S(1)} %fusion.4.count_ref, f32[16]{0:T(128)S(1)} %copy-done.5, bf16[16,256,256]{2,1,0:T(8,128)(2,1)S(1)} %copy-done.3, ...), custom_call_target="tpu_custom_call" | custom-call | tf_op jit(solution)/shard_map/early/pallas_call | solution.py:163
  43.0 0.0 collective-permute-done.2.refs_0_
  43.0 0.0 collective-permute-done.3.refs_1_
  43.1 1.9 %collective-permute-start.4 = (bf16[4,256,256]{2,1,0:T(8,128)(2,1)S(1)}, bf16[4,256,256]{2,1,0:T(8,128)(2,1)S(1)}, u32[]{:S(2)}, u32[]{:S(2)}) collective-permute-start(bf16[4,256,256]{2,1,0:T(8,128)(2,1)S(1)} %collective-permute-done.2.refs_0_), channel_id=1, source_target_pairs={{0,1},{1,0},{2,3},{3,2},{4,5},{5,4},{6,7},{7,6},{8,9},{9,8},{10,11... | collective-permute-start | bytes 1572872 | tf_op jit(solution)/shard_map/ppermute | solution.py:147
  45.0 2.4 %collective-permute-start.5 = (bf16[4,256,256]{2,1,0:T(8,128)(2,1)S(1)}, bf16[4,256,256]{2,1,0:T(8,128)(2,1)S(1)}, u32[]{:S(2)}, u32[]{:S(2)}) collective-permute-start(bf16[4,256,256]{2,1,0:T(8,128)(2,1)S(1)} %collective-permute-done.3.refs_1_), channel_id=1, source_target_pairs={{0,1},{1,0},{2,3},{3,2},{4,5},{5,4},{6,7},{7,6},{8,9},{9,8},{10,11... | collective-permute-start | bytes 1572872 | tf_op jit(solution)/shard_map/ppermute | solution.py:147
  47.4 0.0 collective-permute-done.6.refs_4_
  47.4 1.9 %collective-permute-start.7 = (bf16[4,256,256]{2,1,0:T(8,128)(2,1)S(1)}, bf16[4,256,256]{2,1,0:T(8,128)(2,1)S(1)}, u32[]{:S(2)}, u32[]{:S(2)}) collective-permute-start(bf16[4,256,256]{2,1,0:T(8,128)(2,1)S(1)} %collective-permute-done.6.refs_4_), channel_id=1, source_target_pairs={{0,1},{1,0},{2,3},{3,2},{4,5},{5,4},{6,7},{7,6},{8,9},{9,8},{10,11... | collective-permute-start | bytes 1572872 | tf_op jit(solution)/shard_map/ppermute | solution.py:147
  49.3 0.0 collective-permute-done.4.refs_2_
  49.3 0.0 collective-permute-done.5.refs_3_
  49.4 1.9 %collective-permute-done.7.refs_5_ = bf16[4,256,256]{2,1,0:T(8,128)(2,1)S(1)} collective-permute-done((bf16[4,256,256]{2,1,0:T(8,128)(2,1)S(1)}, bf16[4,256,256]{2,1,0:T(8,128)(2,1)S(1)}, u32[]{:S(2)}, u32[]{:S(2)}) %collective-permute-start.7) | collective-permute-done | bytes 524320 | tf_op jit(solution)/shard_map/ppermute | solution.py:147
  51.2 0.0 copy-done.6
  51.2 2.3 %terms.1 = bf16[4,8,64,256]{3,2,1,0:T(8,128)(2,1)S(1)} custom-call(s32[128]{0:T(128)S(1)} %select_reduce_fusion.list_ref, s32[2]{0:T(128)S(1)} %fusion.4.count_ref, f32[16]{0:T(128)S(1)} %copy-done.6, bf16[16,256,256]{2,1,0:T(8,128)(2,1)S(1)} %get-tuple-element.11.left_ref, bf16[16,256,256]{2,1,0:T(8,128)(2,1)S(1)} %get-tuple-element.12.right_ref, ...), custom_call_target="tpu_custom_call" | custom-call | tf_op jit(solution)/shard_map/terms/pallas_call | solution.py:189
  53.5 0.0 copy-start.2
  53.5 0.0 copy-start.7
  53.5 18.9 %all_to_all.10.parts_ref = bf16[4,8,64,256]{3,2,1,0:T(8,128)(2,1)} all-to-all(bf16[4,8,64,256]{3,2,1,0:T(8,128)(2,1)S(1)} %terms.1), channel_id=1, replica_groups=mesh['z'=8,'x'=4,'half'=2,'y'=4,'core'=2] {'x'}, dimensions={0} | all-to-all | bytes 2097152 | tf_op jit(solution)/shard_map/all_to_all | solution.py:210
  72.5 2.1 %add.272 = bf16[8,64,256]{2,1,0:T(8,128)(2,1)} custom-call(bf16[4,8,64,256]{3,2,1,0:T(8,128)(2,1)} %all_to_all.10.parts_ref), custom_call_target="tpu_custom_call" | custom-call | tf_op jit(solution)/shard_map/add/pallas_call | solution.py:211
  74.6 11.3 %all-to-all-start.1 = ((bf16[16,32,256]{2,1,0:T(8,128)(2,1)}), bf16[16,32,256]{2,1,0:T(8,128)(2,1)S(1)}, u32[]{:S(2)}, u32[]{:S(2)}) async-start(bf16[16,32,256]{2,1,0:T(8,128)(2,1)} %bitcast.5), calls=%async_computation.1 | async-start | bytes 524288 | tf_op jit(solution)/shard_map/all_to_all | solution.py:219
  85.8 0.0 copy-done
  85.8 0.0 copy-done.2
  85.8 0.2 fusion.2
  86.0 15.6 %all-to-all-done.1 = bf16[16,32,256]{2,1,0:T(8,128)(2,1)S(1)} async-done(((bf16[16,32,256]{2,1,0:T(8,128)(2,1)}), bf16[16,32,256]{2,1,0:T(8,128)(2,1)S(1)}, u32[]{:S(2)}, u32[]{:S(2)}) %all-to-all-start.1) | async-done | bytes 262176 | tf_op jit(solution)/shard_map/all_to_all | solution.py:219
  101.7 0.0 copy-done.7
  101.7 0.8 fusion
  (4 shorter events, 0.1 us)
Async XLA Ops:
  0.0 85.8 %copy-start = (bf16[4,256,256]{2,1,0:T(8,128)(2,1)S(1)}, bf16[4,256,256]{2,1,0:T(8,128)(2,1)}, u32[]{:S(2)}) copy-start(bf16[4,256,256]{2,1,0:T(8,128)(2,1)} %param.15) | copy-start | bytes 1572868
  0.0 35.9 %collective-permute-start.1 = (bf16[4,256,256]{2,1,0:T(8,128)(2,1)}, bf16[4,256,256]{2,1,0:T(8,128)(2,1)S(1)}, u32[]{:S(2)}, u32[]{:S(2)}) collective-permute-start(bf16[4,256,256]{2,1,0:T(8,128)(2,1)} %refs_0_.1), channel_id=1, source_target_pairs={{0,1},{1,0},{2,3},{3,2},{4,5},{5,4},{6,7},{7,6},{8,9},{9,8},{10,11... | collective-permute-start | bytes 1572872 | tf_op jit(solution)/shard_map/ppermute | solution.py:147
  2.1 41.0 %collective-permute-start.2 = (bf16[4,256,256]{2,1,0:T(8,128)(2,1)}, bf16[4,256,256]{2,1,0:T(8,128)(2,1)S(1)}, u32[]{:S(2)}, u32[]{:S(2)}) collective-permute-start(bf16[4,256,256]{2,1,0:T(8,128)(2,1)} %refs_0_.1), channel_id=1, source_target_pairs={{2,0},{15,1},{4,2},{1,3},{6,4},{3,5},{8,6},{5,7},{10,8},{7,9},{12,... | collective-permute-start | bytes 1572872 | tf_op jit(solution)/shard_map/ppermute | solution.py:144
  9.8 33.2 %collective-permute-start.3 = (bf16[4,256,256]{2,1,0:T(8,128)(2,1)}, bf16[4,256,256]{2,1,0:T(8,128)(2,1)S(1)}, u32[]{:S(2)}, u32[]{:S(2)}) collective-permute-start(bf16[4,256,256]{2,1,0:T(8,128)(2,1)} %refs_0_.1), channel_id=1, source_target_pairs={{14,0},{3,1},{0,2},{5,3},{2,4},{7,5},{4,6},{9,7},{6,8},{11,9},{8,1... | collective-permute-start | bytes 1572872 | tf_op jit(solution)/shard_map/ppermute | solution.py:144
  11.7 35.7 %collective-permute-start.6 = (bf16[4,256,256]{2,1,0:T(8,128)(2,1)}, bf16[4,256,256]{2,1,0:T(8,128)(2,1)S(1)}, u32[]{:S(2)}, u32[]{:S(2)}) collective-permute-start(bf16[4,256,256]{2,1,0:T(8,128)(2,1)} %refs_0_.1), channel_id=1, source_target_pairs={{4,0},{13,1},{6,2},{15,3},{8,4},{1,5},{10,6},{3,7},{12,8},{5,9},{1... | collective-permute-start | bytes 1572872 | tf_op jit(solution)/shard_map/ppermute | solution.py:144
  17.0 17.5 %collective-permute-start = (s32[16,4]{0,1:T(4,128)S(1)}, s32[16,4]{0,1:T(4,128)S(1)}, u32[]{:S(2)}, u32[]{:S(2)}) collective-permute-start(s32[16,4]{0,1:T(4,128)S(1)} %compare_select_fusion.15), channel_id=1, source_target_pairs={{8,0},{9,1},{10,2},{11,3},{12,4},{13,5},{14,6},{15,7},{0,8},{1,9},... | collective-permute-start | bytes 776 | tf_op jit(solution)/shard_map/ppermute | solution.py:144
  35.9 1.0 %copy-start.1 = (bf16[4,256,256]{2,1,0:T(8,128)(2,1)S(1)}, bf16[4,256,256]{2,1,0:T(8,128)(2,1)}, u32[]{:S(2)}) copy-start(bf16[4,256,256]{2,1,0:T(8,128)(2,1)} %refs_0_.1) | copy-start | bytes 1572868
  36.9 1.6 %copy-start.3 = (bf16[16,256,256]{2,1,0:T(8,128)(2,1)S(1)}, bf16[16,256,256]{2,1,0:T(8,128)(2,1)}, u32[]{:S(2)}) copy-start(bf16[16,256,256]{2,1,0:T(8,128)(2,1)} %left_hbm.1) | copy-start | bytes 6291460
  38.5 1.6 %copy-start.4 = (bf16[16,256,256]{2,1,0:T(8,128)(2,1)S(1)}, bf16[16,256,256]{2,1,0:T(8,128)(2,1)}, u32[]{:S(2)}) copy-start(bf16[16,256,256]{2,1,0:T(8,128)(2,1)} %right_hbm.1) | copy-start | bytes 6291460
  40.1 0.7 copy-start.5
  40.8 10.4 %copy-start.6 = (f32[16]{0:T(128)S(1)}, f32[16]{0:T(128)}, u32[]{:S(2)}) copy-start(f32[16]{0:T(128)} %coef_ref.3) | copy-start | bytes 196
  43.1 6.3 %collective-permute-start.4 = (bf16[4,256,256]{2,1,0:T(8,128)(2,1)S(1)}, bf16[4,256,256]{2,1,0:T(8,128)(2,1)S(1)}, u32[]{:S(2)}, u32[]{:S(2)}) collective-permute-start(bf16[4,256,256]{2,1,0:T(8,128)(2,1)S(1)} %collective-permute-done.2.refs_0_), channel_id=1, source_target_pairs={{0,1},{1,0},{2,3},{3,2},{4,5},{5,4},{6,7},{7,6},{8,9},{9,8},{10,11... | collective-permute-start | bytes 1572872 | tf_op jit(solution)/shard_map/ppermute | solution.py:147
  45.0 4.4 %collective-permute-start.5 = (bf16[4,256,256]{2,1,0:T(8,128)(2,1)S(1)}, bf16[4,256,256]{2,1,0:T(8,128)(2,1)S(1)}, u32[]{:S(2)}, u32[]{:S(2)}) collective-permute-start(bf16[4,256,256]{2,1,0:T(8,128)(2,1)S(1)} %collective-permute-done.3.refs_1_), channel_id=1, source_target_pairs={{0,1},{1,0},{2,3},{3,2},{4,5},{5,4},{6,7},{7,6},{8,9},{9,8},{10,11... | collective-permute-start | bytes 1572872 | tf_op jit(solution)/shard_map/ppermute | solution.py:147
  47.4 3.8 %collective-permute-start.7 = (bf16[4,256,256]{2,1,0:T(8,128)(2,1)S(1)}, bf16[4,256,256]{2,1,0:T(8,128)(2,1)S(1)}, u32[]{:S(2)}, u32[]{:S(2)}) collective-permute-start(bf16[4,256,256]{2,1,0:T(8,128)(2,1)S(1)} %collective-permute-done.6.refs_4_), channel_id=1, source_target_pairs={{0,1},{1,0},{2,3},{3,2},{4,5},{5,4},{6,7},{7,6},{8,9},{9,8},{10,11... | collective-permute-start | bytes 1572872 | tf_op jit(solution)/shard_map/ppermute | solution.py:147
  53.5 32.3 %copy-start.2 = (bf16[4,256,256]{2,1,0:T(8,128)(2,1)S(1)}, bf16[4,256,256]{2,1,0:T(8,128)(2,1)}, u32[]{:S(2)}) copy-start(bf16[4,256,256]{2,1,0:T(8,128)(2,1)} %refs_0_.1) | copy-start | bytes 1572868
  53.5 48.2 %copy-start.7 = (bf16[4,256,256]{2,1,0:T(8,128)(2,1)S(1)}, bf16[4,256,256]{2,1,0:T(8,128)(2,1)}, u32[]{:S(2)}) copy-start(bf16[4,256,256]{2,1,0:T(8,128)(2,1)} %param.16) | copy-start | bytes 1572868
  74.6 27.1 %all-to-all-start.1 = ((bf16[16,32,256]{2,1,0:T(8,128)(2,1)}), bf16[16,32,256]{2,1,0:T(8,128)(2,1)S(1)}, u32[]{:S(2)}, u32[]{:S(2)}) async-start(bf16[16,32,256]{2,1,0:T(8,128)(2,1)} %bitcast.5), calls=%async_computation.1 | async-start | bytes 524288 | tf_op jit(solution)/shard_map/all_to_all | solution.py:219

commit v3 on v2

v3 whole, which is shorter than its diff:
```python
import functools

import jax
import jax.numpy as jnp
from jax import lax
from jax.experimental import pallas as pl
from jax.experimental.pallas import tpu as pltpu
from jax.sharding import Mesh, PartitionSpec as P

AXES = (8, 4, 2, 4, 2)
NAMES = ("z", "x", "half", "y", "core")
GROUP = 4

PLACES = ((0, 1, 0), (1, 4, 2), (-1, 5, 3), (2, 7, 6))


def places_of(codes, sec_dev, core, ring, length):
    source_core = (codes // sec_dev) % 2
    away = (codes // (2 * sec_dev) - ring) * jnp.where(source_core == 0, 1, -1)
    block = jnp.full_like(codes, -1)
    for far, other, own in PLACES:
        here = (away - far) % length == 0
        block = jnp.where(here, jnp.where(source_core == core, own, other), block)
    held = jnp.logical_and(codes >= 0, block >= 0)
    return jnp.where(held, block * sec_dev + codes % sec_dev, 2 * len(PLACES) * sec_dev)


def sorted_pairs(places):
    pairs = places.shape[0]
    pair = jnp.arange(pairs, dtype=jnp.int32)
    keys = places * pairs + pair
    rank = jnp.sum((keys[None, :] < keys[:, None]).astype(jnp.int32), axis=1)
    return jnp.sum(jnp.where(rank[None, :] == pair[:, None], keys[None, :], 0), axis=1)


def add_pairs(last, list_ref, coef_ref, left_ref, right_ref, blocks, tiles, sems, sums):
    targets = sums.shape[0]
    pairs = list_ref.shape[0]
    sec_dev = blocks[0].shape[0]

    def fetch(b):
        return pltpu.make_async_copy(
            blocks[b], tiles.at[pl.ds(b * sec_dev, sec_dev)], sems.at[b]
        )

    def step(g, ready):
        work = []
        for j in range(GROUP):
            at = g * GROUP + j
            valid = at < last
            code = list_ref[jnp.minimum(at, pairs - 1)]
            code = jnp.where(valid, code, 0)
            pair = lax.rem(code, pairs)
            term = lax.div(pair, targets)
            weight = jnp.where(valid, coef_ref[term], 0.0)
            work.append((lax.div(code, pairs), term, lax.rem(pair, targets), weight))
        needed = lax.div(functools.reduce(jnp.maximum, [w[0] for w in work]), sec_dev) + 1
        for b in range(len(blocks)):
            pl.when(jnp.logical_and(ready <= b, b < needed))(fetch(b).wait)
        images = []
        for place, term, target, weight in work:
            mixed = jnp.dot(
                left_ref[term], tiles[place], preferred_element_type=jnp.float32
            ).astype(jnp.bfloat16)
            image = jnp.dot(mixed, right_ref[term], preferred_element_type=jnp.float32)
            images.append((target, image * weight))
        for target, image in images:
            sums[target] += image
        return jnp.maximum(ready, needed)

    ready = lax.fori_loop(0, lax.div(last + GROUP - 1, GROUP), step, 0)
    for b in range(len(blocks)):
        pl.when(ready <= b)(fetch(b).wait)


def start_fetches(blocks, tiles, sems):
    sec_dev = blocks[0].shape[0]
    for b, block in enumerate(blocks):
        pltpu.make_async_copy(block, tiles.at[pl.ds(b * sec_dev, sec_dev)], sems.at[b]).start()


def hold_kernel(left_hbm, right_hbm, left_ref, right_ref, sems):
    copies = [
        pltpu.make_async_copy(left_hbm, left_ref, sems.at[0]),
        pltpu.make_async_copy(right_hbm, right_ref, sems.at[1]),
    ]
    for copy in copies:
        copy.start()
    for copy in copies:
        copy.wait()


def terms_kernel(list_ref, count_ref, coef_ref, left_ref, right_ref, *refs):
    blocks, (out_ref, tiles, sums, sems) = refs[:-4], refs[-4:]
    n_x, n_z = out_ref.shape[:2]
    targets, tile, _ = sums.shape
    band = tile // (n_x * n_z)
    start_fetches(blocks, tiles, sems)
    sums[...] = jnp.zeros_like(sums)
    add_pairs(count_ref[0], list_ref, coef_ref, left_ref, right_ref, blocks, tiles, sems, sums)
    for t in range(0, targets, 2):
        two = [sums[t + i].reshape(n_z, n_x, band, tile) for i in range(2)]
        rows = jnp.concatenate(two, axis=2).astype(out_ref.dtype)
        for x in range(n_x):
            out_ref[x, :, pl.ds(t * band, 2 * band), :] = rows[:, x]


def per_device(psi, left_ops, right_ops, coef, source, active, left_block, right_block):
    sec_dev, tile, _ = psi.shape
    term_dev = left_ops.shape[0]
    n_z, n_x, halves, half_y, cores = (lax.axis_size(name) for name in NAMES)
    n_ops, n_y = n_z * n_x, halves * half_y
    targets = halves * sec_dev
    pairs = term_dev * targets
    band = tile // n_ops
    ops_index = lax.axis_index("z") * n_x + lax.axis_index("x")
    core, half = lax.axis_index("core"), lax.axis_index("half")
    ring = half * half_y + lax.axis_index("y")
    smem = pl.BlockSpec(memory_space=pltpu.SMEM)
    vmem = pl.BlockSpec(memory_space=pltpu.VMEM)
    anywhere = pl.BlockSpec(memory_space=pl.ANY)

    def from_y(value, away):
        route = [(((y + a) % n_y) * 2 + c, y * 2 + c) for y in range(n_y) for c, a in ((0, away), (1, -away))]
        return lax.ppermute(value, ("half", "y", "core"), route)

    def from_core(value):
        return lax.ppermute(value, "core", [(0, 1), (1, 0)])

    near = [from_y(psi, 1), from_y(psi, -1)]
    far = from_y(psi, 2)
    their_psi = from_core(psi)
    code = jnp.where(active != 0, source, -1)
    other = from_y(code, n_y // 2)
    held = pl.pallas_call(
        hold_kernel,
        out_shape=(
            jax.ShapeDtypeStruct(left_ops.shape, left_ops.dtype),
            jax.ShapeDtypeStruct(right_ops.shape, right_ops.dtype),
        ),
        in_specs=[anywhere] * 2,
        out_specs=(vmem,) * 2,
        scratch_shapes=[pltpu.SemaphoreType.DMA((2,))],
        compiler_params=pltpu.CompilerParams(vmem_limit_bytes=16 * 2**20),
        name="hold",
    )(left_ops, right_ops)

    local_rows = lax.dynamic_slice_in_dim(psi, ops_index * band, band, 1)
    block_rows = lax.dynamic_slice_in_dim(left_block, ops_index * band, band, 1)
    local_part = jnp.einsum("tij,tjl->til", block_rows, psi, preferred_element_type=jnp.float32)
    local_part = local_part + jnp.einsum(
        "tij,tjl->til", local_rows, right_block, preferred_element_type=jnp.float32
    )

    near, held, local_part = lax.optimization_barrier((near, held, local_part))
    theirs = [their_psi] + [from_core(block) for block in near]
    far, other, theirs = lax.optimization_barrier((far, other, theirs))
    theirs.append(from_core(far))
    blocks = [None] * (2 * len(PLACES))
    for (_, other_place, own), my_block, their_block in zip(PLACES, [psi, *near, far], theirs):
        blocks[own], blocks[other_place] = my_block, their_block

    codes = jnp.concatenate(
        [jnp.where(half == 0, code, other), jnp.where(half == 0, other, code)], axis=1
    )
    places = places_of(codes, sec_dev, core, ring, n_y).reshape(pairs)
    count = jnp.sum((places < len(blocks) * sec_dev).astype(jnp.int32)).reshape(1)

    partial_sum = pl.pallas_call(
        terms_kernel,
        out_shape=jax.ShapeDtypeStruct((n_x, n_z, targets * band, tile), jnp.bfloat16),
        in_specs=[smem] * 3 + [vmem] * 2 + [anywhere] * len(blocks),
        out_specs=vmem,
        scratch_shapes=[
            pltpu.VMEM((len(blocks) * sec_dev, tile, tile), psi.dtype),
            pltpu.VMEM((targets, tile, tile), jnp.float32),
            pltpu.SemaphoreType.DMA((len(blocks),)),
        ],
        compiler_params=pltpu.CompilerParams(vmem_limit_bytes=24 * 2**20),
        name="terms",
    )(sorted_pairs(places), count, coef, *held, *blocks)

    bands = lax.all_to_all(partial_sum, "x", 0, 0, tiled=True)
    bands = lax.optimization_barrier(jnp.sum(bands.astype(jnp.float32), axis=0))
    bands = bands.astype(partial_sum.dtype)
    bands = bands.reshape(n_z * halves, sec_dev * band, tile)
    bands = lax.all_to_all(bands, ("z", "half"), 0, 0, tiled=True)
    summed = jnp.sum(bands.astype(jnp.float32), axis=0).reshape(sec_dev, band, tile)
    return local_part + summed


def solution(mesh):
    full = Mesh(mesh.devices.reshape(AXES), NAMES)
    ops, sec = ("z", "x"), ("half", "y", "core")
    in_specs = (
        P(sec, None, None),
        P(ops, None, None),
        P(ops, None, None),
        P(ops),
        P(ops, sec),
        P(ops, sec),
        P(sec, None, None),
        P(sec, None, None),
    )
    return jax.shard_map(
        per_device, mesh=full, in_specs=in_specs, out_specs=P(sec, ops, None), check_vma=False
    )
```

time: 103 us -> 93 us (0.903)
  the two profiles are of different devices: /device:TPU:8 before, /device:TPU:2 now
where the time goes in v3:
time: 93 us; the launch traced here: 92.5 us
  blocking collectives  46.4 us (50%)
  starting transfers between devices  26.5 us (28%)
  local copies, waits for them, and re-layouts  6.29 us (7%)
  waiting for transfers between devices  5.61 us (6%)
  Pallas kernels  5.22 us (6%)
  other arithmetic  1.82 us (2%)
    all_to_all x1, blocking collectives, per_device(): bands = lax.all_to_all(partial_sum, 'x', 0, 0, tiled=True)  25.8 us
    all_to_all x1, blocking collectives, per_device(): bands = lax.all_to_all(bands, ('z', 'half'), 0, 0, tiled=True)  20.6 us
    ppermute x4, starting transfers between devices, from_y(): return lax.ppermute(value, ('half', 'y', 'core'), route)  18.4 us
    ppermute x4, starting transfers between devices, from_core(): return lax.ppermute(value, 'core', [(0, 1), (1, 0)])  8.16 us
    unnamed x20, local copies, waits for them, and re-layouts  6.14 us
    pallas_call x1, Pallas kernels, per_device(): pl.pallas_call(terms_kernel, out_shape=jax.ShapeDtypeStruct((n_x, n_z, ta...  4.92 us
    ppermute x4, waiting for transfers between devices, from_y(): return lax.ppermute(value, ('half', 'y', 'core'), route)  4.57 us
  transfers between devices with their start and end apart: 8, of which 3 were waited for; matrix products, arithmetic and copies ran while one was open for 2% of the time, Pallas kernels for 0%

profile of v3, /device:TPU:2, one launch (start us, length us, event | category | flops | bytes accessed | tf_op | source)
XLA Modules:
  0.0 92.5 jit_solution(9696542992396561135)
XLA Ops:
  0.0 0.0 copy-start
  0.0 3.6 %collective-permute-start.1 = (bf16[4,256,256]{2,1,0:T(8,128)(2,1)}, bf16[4,256,256]{2,1,0:T(8,128)(2,1)}, u32[]{:S(2)}, u32[]{:S(2)}) collective-permute-start(bf16[4,256,256]{2,1,0:T(8,128)(2,1)} %refs_0_.1), channel_id=1, source_target_pairs={{14,0},{3,1},{0,2},{5,3},{2,4},{7,5},{4,6},{9,7},{6,8},{11,9},{8,1... | collective-permute-start | bytes 1572872 | tf_op jit(solution)/shard_map/ppermute | solution.py:125
  3.6 3.8 %collective-permute-start = (bf16[4,256,256]{2,1,0:T(8,128)(2,1)}, bf16[4,256,256]{2,1,0:T(8,128)(2,1)}, u32[]{:S(2)}, u32[]{:S(2)}) collective-permute-start(bf16[4,256,256]{2,1,0:T(8,128)(2,1)} %refs_0_.1), channel_id=1, source_target_pairs={{2,0},{15,1},{4,2},{1,3},{6,4},{3,5},{8,6},{5,7},{10,8},{7,9},{12,... | collective-permute-start | bytes 1572872 | tf_op jit(solution)/shard_map/ppermute | solution.py:125
  7.4 4.7 %collective-permute-start.2 = (bf16[4,256,256]{2,1,0:T(8,128)(2,1)}, bf16[4,256,256]{2,1,0:T(8,128)(2,1)}, u32[]{:S(2)}, u32[]{:S(2)}) collective-permute-start(bf16[4,256,256]{2,1,0:T(8,128)(2,1)} %refs_0_.1), channel_id=1, source_target_pairs={{4,0},{13,1},{6,2},{15,3},{8,4},{1,5},{10,6},{3,7},{12,8},{5,9},{1... | collective-permute-start | bytes 1572872 | tf_op jit(solution)/shard_map/ppermute | solution.py:125
  12.2 1.9 %collective-permute-start.4 = (bf16[4,256,256]{2,1,0:T(8,128)(2,1)}, bf16[4,256,256]{2,1,0:T(8,128)(2,1)}, u32[]{:S(2)}, u32[]{:S(2)}) collective-permute-start(bf16[4,256,256]{2,1,0:T(8,128)(2,1)} %refs_0_.1), channel_id=1, source_target_pairs={{0,1},{1,0},{2,3},{3,2},{4,5},{5,4},{6,7},{7,6},{8,9},{9,8},{10,11... | collective-permute-start | bytes 1572872 | tf_op jit(solution)/shard_map/ppermute | solution.py:128
  14.1 0.0 copy-start.4
  14.1 1.6 %copy-done.4 = bf16[16,256,256]{2,1,0:T(8,128)(2,1)S(1)} copy-done((bf16[16,256,256]{2,1,0:T(8,128)(2,1)S(1)}, bf16[16,256,256]{2,1,0:T(8,128)(2,1)}, u32[]{:S(2)}) %copy-start.4) | copy-done | bytes 2097176
  15.7 0.0 copy-start.5
  15.7 1.6 %copy-done.5 = bf16[16,256,256]{2,1,0:T(8,128)(2,1)S(1)} copy-done((bf16[16,256,256]{2,1,0:T(8,128)(2,1)S(1)}, bf16[16,256,256]{2,1,0:T(8,128)(2,1)}, u32[]{:S(2)}) %copy-start.5) | copy-done | bytes 2097176
  17.3 0.0 copy-start.1
  17.3 0.0 copy-start.7
  17.3 0.0 copy-start.8
  17.3 0.0 copy-start.9
  17.3 0.0 copy-start.6
  17.3 0.3 hold.1
  17.6 0.0 copy-start.2
  17.6 1.3 %copy-done.2 = bf16[16,256,256]{2,1,0:T(8,128)(2,1)} copy-done((bf16[16,256,256]{2,1,0:T(8,128)(2,1)}, bf16[16,256,256]{2,1,0:T(8,128)(2,1)S(1)}, u32[]{:S(2)}) %copy-start.2) | copy-done | bytes 2097176
  19.0 0.0 copy-done
  19.0 0.0 copy-done.1
  19.0 0.2 fusion.1
  19.1 0.0 copy-done.7
  19.1 0.2 convolution_add_fusion
  19.3 0.0 collective-permute-done.1.refs_3_
  19.3 1.3 %collective-permute-done.refs_2_ = bf16[4,256,256]{2,1,0:T(8,128)(2,1)} collective-permute-done((bf16[4,256,256]{2,1,0:T(8,128)(2,1)}, bf16[4,256,256]{2,1,0:T(8,128)(2,1)}, u32[]{:S(2)}, u32[]{:S(2)}) %collective-permute-start) | collective-permute-done | bytes 524320 | tf_op jit(solution)/shard_map/ppermute | solution.py:125
  20.6 1.9 %collective-permute-start.5 = (bf16[4,256,256]{2,1,0:T(8,128)(2,1)}, bf16[4,256,256]{2,1,0:T(8,128)(2,1)}, u32[]{:S(2)}, u32[]{:S(2)}) collective-permute-start(bf16[4,256,256]{2,1,0:T(8,128)(2,1)} %collective-permute-done.refs_2_), channel_id=1, source_target_pairs={{0,1},{1,0},{2,3},{3,2},{4,5},{5,4},{6,7},{7,6},{8,9},{9,8},{10,11... | collective-permute-start | bytes 1572872 | tf_op jit(solution)/shard_map/ppermute | solution.py:128
  22.5 2.4 %collective-permute-start.6 = (bf16[4,256,256]{2,1,0:T(8,128)(2,1)}, bf16[4,256,256]{2,1,0:T(8,128)(2,1)}, u32[]{:S(2)}, u32[]{:S(2)}) collective-permute-start(bf16[4,256,256]{2,1,0:T(8,128)(2,1)} %collective-permute-done.1.refs_3_), channel_id=1, source_target_pairs={{0,1},{1,0},{2,3},{3,2},{4,5},{5,4},{6,7},{7,6},{8,9},{9,8},{10,11... | collective-permute-start | bytes 1572872 | tf_op jit(solution)/shard_map/ppermute | solution.py:128
  25.0 0.0 copy-done.8
  25.0 0.0 copy-done.9
  25.0 6.2 %collective-permute-start.3 = (s32[16,4]{0,1:T(4,128)S(1)}, s32[16,4]{0,1:T(4,128)S(1)}, u32[]{:S(2)}, u32[]{:S(2)}) collective-permute-start(s32[16,4]{0,1:T(4,128)S(1)} %compare_select_fusion.15), channel_id=1, source_target_pairs={{8,0},{9,1},{10,2},{11,3},{12,4},{13,5},{14,6},{15,7},{0,8},{1,9},... | collective-permute-start | bytes 776 | tf_op jit(solution)/shard_map/ppermute | solution.py:125
  31.3 3.3 %collective-permute-done.3 = s32[16,4]{0,1:T(4,128)S(1)} collective-permute-done((s32[16,4]{0,1:T(4,128)S(1)}, s32[16,4]{0,1:T(4,128)S(1)}, u32[]{:S(2)}, u32[]{:S(2)}) %collective-permute-start.3) | collective-permute-done | bytes 288 | tf_op jit(solution)/shard_map/ppermute | solution.py:125
  34.5 0.0 collective-permute-done.2.refs_6_
  34.5 0.0 collective-permute-done.4.refs_1_
  34.5 0.0 collective-permute-done.5.refs_4_
  34.5 0.0 collective-permute-done.6.refs_5_
  34.5 1.9 %collective-permute-start.7 = (bf16[4,256,256]{2,1,0:T(8,128)(2,1)}, bf16[4,256,256]{2,1,0:T(8,128)(2,1)}, u32[]{:S(2)}, u32[]{:S(2)}) collective-permute-start(bf16[4,256,256]{2,1,0:T(8,128)(2,1)} %collective-permute-done.2.refs_6_), channel_id=1, source_target_pairs={{0,1},{1,0},{2,3},{3,2},{4,5},{5,4},{6,7},{7,6},{8,9},{9,8},{10,11... | collective-permute-start | bytes 1572872 | tf_op jit(solution)/shard_map/ppermute | solution.py:128
  36.5 0.7 convert_reduce_fusion.3
  37.2 0.1 copy.11
  37.2 0.1 concatenate.6
  37.4 0.2 convert_reduce_fusion.2
  37.5 0.1 select_reduce_fusion.list_ref
  37.7 1.0 %collective-permute-done.7.refs_7_ = bf16[4,256,256]{2,1,0:T(8,128)(2,1)} collective-permute-done((bf16[4,256,256]{2,1,0:T(8,128)(2,1)}, bf16[4,256,256]{2,1,0:T(8,128)(2,1)}, u32[]{:S(2)}, u32[]{:S(2)}) %collective-permute-start.7) | collective-permute-done | bytes 524320 | tf_op jit(solution)/shard_map/ppermute | solution.py:128
  38.7 0.0 copy-done.6
  38.7 1.6 %copy-done.3 = bf16[16,256,256]{2,1,0:T(8,128)(2,1)S(1)} copy-done((bf16[16,256,256]{2,1,0:T(8,128)(2,1)S(1)}, bf16[16,256,256]{2,1,0:T(8,128)(2,1)}, u32[]{:S(2)}) %copy-start.3) | copy-done | bytes 2097176
  40.3 4.9 %terms.1 = bf16[4,8,64,256]{3,2,1,0:T(8,128)(2,1)S(1)} custom-call(s32[128]{0:T(128)S(1)} %select_reduce_fusion.list_ref, s32[1]{0:T(128)} %bitcast.count_ref, f32[16]{0:T(128)S(1)} %copy-done.6, bf16[16,256,256]{2,1,0:T(8,128)(2,1)S(1)} %get-tuple-element.23.left_ref, bf16[16,256,256]{2,1,0:T(8,128)(2,1)S(1)} %copy-done.3, ...), custom_call_target="tpu_custom_call" | custom-call | tf_op jit(solution)/shard_map/terms/pallas_call | solution.py:169
  45.2 25.8 %all_to_all.10 = bf16[4,8,64,256]{3,2,1,0:T(8,128)(2,1)S(1)} all-to-all(bf16[4,8,64,256]{3,2,1,0:T(8,128)(2,1)S(1)} %terms.1), channel_id=1, replica_groups=mesh['z'=8,'x'=4,'half'=2,'y'=4,'core'=2] {'x'}, dimensions={0} | all-to-all | bytes 2097152 | tf_op jit(solution)/shard_map/all_to_all | solution.py:183
  71.0 0.2 convert_reduce_fusion
  71.2 20.6 %all_to_all.11 = bf16[16,32,256]{2,1,0:T(8,128)(2,1)S(1)} all-to-all(bf16[16,32,256]{2,1,0:T(8,128)(2,1)S(1)} %bitcast.6), channel_id=1, replica_groups=mesh['z'=8,'x'=4,'half'=2,'y'=4,'core'=2] {'z','half'}, dimensions={0} | all-to-all | bytes 524288 | tf_op jit(solution)/shard_map/all_to_all | solution.py:187
  91.9 0.6 bitcast_add_fusion
  (5 shorter events, 0.1 us)
Async XLA Ops:
  0.0 19.0 %copy-start = (bf16[4,256,256]{2,1,0:T(8,128)(2,1)S(1)}, bf16[4,256,256]{2,1,0:T(8,128)(2,1)}, u32[]{:S(2)}) copy-start(bf16[4,256,256]{2,1,0:T(8,128)(2,1)} %param.14) | copy-start | bytes 1572868
  0.0 19.3 %collective-permute-start.1 = (bf16[4,256,256]{2,1,0:T(8,128)(2,1)}, bf16[4,256,256]{2,1,0:T(8,128)(2,1)}, u32[]{:S(2)}, u32[]{:S(2)}) collective-permute-start(bf16[4,256,256]{2,1,0:T(8,128)(2,1)} %refs_0_.1), channel_id=1, source_target_pairs={{14,0},{3,1},{0,2},{5,3},{2,4},{7,5},{4,6},{9,7},{6,8},{11,9},{8,1... | collective-permute-start | bytes 1572872 | tf_op jit(solution)/shard_map/ppermute | solution.py:125
  3.6 17.0 %collective-permute-start = (bf16[4,256,256]{2,1,0:T(8,128)(2,1)}, bf16[4,256,256]{2,1,0:T(8,128)(2,1)}, u32[]{:S(2)}, u32[]{:S(2)}) collective-permute-start(bf16[4,256,256]{2,1,0:T(8,128)(2,1)} %refs_0_.1), channel_id=1, source_target_pairs={{2,0},{15,1},{4,2},{1,3},{6,4},{3,5},{8,6},{5,7},{10,8},{7,9},{12,... | collective-permute-start | bytes 1572872 | tf_op jit(solution)/shard_map/ppermute | solution.py:125
  7.4 27.1 %collective-permute-start.2 = (bf16[4,256,256]{2,1,0:T(8,128)(2,1)}, bf16[4,256,256]{2,1,0:T(8,128)(2,1)}, u32[]{:S(2)}, u32[]{:S(2)}) collective-permute-start(bf16[4,256,256]{2,1,0:T(8,128)(2,1)} %refs_0_.1), channel_id=1, source_target_pairs={{4,0},{13,1},{6,2},{15,3},{8,4},{1,5},{10,6},{3,7},{12,8},{5,9},{1... | collective-permute-start | bytes 1572872 | tf_op jit(solution)/shard_map/ppermute | solution.py:125
  12.2 22.4 %collective-permute-start.4 = (bf16[4,256,256]{2,1,0:T(8,128)(2,1)}, bf16[4,256,256]{2,1,0:T(8,128)(2,1)}, u32[]{:S(2)}, u32[]{:S(2)}) collective-permute-start(bf16[4,256,256]{2,1,0:T(8,128)(2,1)} %refs_0_.1), channel_id=1, source_target_pairs={{0,1},{1,0},{2,3},{3,2},{4,5},{5,4},{6,7},{7,6},{8,9},{9,8},{10,11... | collective-permute-start | bytes 1572872 | tf_op jit(solution)/shard_map/ppermute | solution.py:128
  14.1 1.6 %copy-start.4 = (bf16[16,256,256]{2,1,0:T(8,128)(2,1)S(1)}, bf16[16,256,256]{2,1,0:T(8,128)(2,1)}, u32[]{:S(2)}) copy-start(bf16[16,256,256]{2,1,0:T(8,128)(2,1)} %left_hbm.1) | copy-start | bytes 6291460
  15.7 1.6 %copy-start.5 = (bf16[16,256,256]{2,1,0:T(8,128)(2,1)S(1)}, bf16[16,256,256]{2,1,0:T(8,128)(2,1)}, u32[]{:S(2)}) copy-start(bf16[16,256,256]{2,1,0:T(8,128)(2,1)} %right_hbm.1) | copy-start | bytes 6291460
  17.3 1.7 %copy-start.1 = (bf16[4,256,256]{2,1,0:T(8,128)(2,1)S(1)}, bf16[4,256,256]{2,1,0:T(8,128)(2,1)}, u32[]{:S(2)}) copy-start(bf16[4,256,256]{2,1,0:T(8,128)(2,1)} %refs_0_.1) | copy-start | bytes 1572868
  17.3 1.9 %copy-start.7 = (bf16[4,256,256]{2,1,0:T(8,128)(2,1)S(1)}, bf16[4,256,256]{2,1,0:T(8,128)(2,1)}, u32[]{:S(2)}) copy-start(bf16[4,256,256]{2,1,0:T(8,128)(2,1)} %param.15) | copy-start | bytes 1572868
  17.3 7.7 %copy-start.8 = (s32[16,4]{0,1:T(4,128)S(1)}, s32[16,4]{0,1:T(4,128)}, u32[]{:S(2)}) copy-start(s32[16,4]{0,1:T(4,128)} %param.12) | copy-start | bytes 772
  17.3 7.7 %copy-start.9 = (s32[16,4]{0,1:T(4,128)S(1)}, s32[16,4]{0,1:T(4,128)}, u32[]{:S(2)}) copy-start(s32[16,4]{0,1:T(4,128)} %param.13) | copy-start | bytes 772
  17.3 21.4 %copy-start.6 = (f32[16]{0:T(128)S(1)}, f32[16]{0:T(128)}, u32[]{:S(2)}) copy-start(f32[16]{0:T(128)} %coef_ref.1) | copy-start | bytes 196
  17.6 1.4 %copy-start.2 = (bf16[16,256,256]{2,1,0:T(8,128)(2,1)}, bf16[16,256,256]{2,1,0:T(8,128)(2,1)S(1)}, u32[]{:S(2)}) copy-start(bf16[16,256,256]{2,1,0:T(8,128)(2,1)S(1)} %get-tuple-element.24.right_ref) | copy-start | bytes 6291460
  20.6 13.9 %collective-permute-start.5 = (bf16[4,256,256]{2,1,0:T(8,128)(2,1)}, bf16[4,256,256]{2,1,0:T(8,128)(2,1)}, u32[]{:S(2)}, u32[]{:S(2)}) collective-permute-start(bf16[4,256,256]{2,1,0:T(8,128)(2,1)} %collective-permute-done.refs_2_), channel_id=1, source_target_pairs={{0,1},{1,0},{2,3},{3,2},{4,5},{5,4},{6,7},{7,6},{8,9},{9,8},{10,11... | collective-permute-start | bytes 1572872 | tf_op jit(solution)/shard_map/ppermute | solution.py:128
  22.5 12.0 %collective-permute-start.6 = (bf16[4,256,256]{2,1,0:T(8,128)(2,1)}, bf16[4,256,256]{2,1,0:T(8,128)(2,1)}, u32[]{:S(2)}, u32[]{:S(2)}) collective-permute-start(bf16[4,256,256]{2,1,0:T(8,128)(2,1)} %collective-permute-done.1.refs_3_), channel_id=1, source_target_pairs={{0,1},{1,0},{2,3},{3,2},{4,5},{5,4},{6,7},{7,6},{8,9},{9,8},{10,11... | collective-permute-start | bytes 1572872 | tf_op jit(solution)/shard_map/ppermute | solution.py:128
  25.0 9.5 %collective-permute-start.3 = (s32[16,4]{0,1:T(4,128)S(1)}, s32[16,4]{0,1:T(4,128)S(1)}, u32[]{:S(2)}, u32[]{:S(2)}) collective-permute-start(s32[16,4]{0,1:T(4,128)S(1)} %compare_select_fusion.15), channel_id=1, source_target_pairs={{8,0},{9,1},{10,2},{11,3},{12,4},{13,5},{14,6},{15,7},{0,8},{1,9},... | collective-permute-start | bytes 776 | tf_op jit(solution)/shard_map/ppermute | solution.py:125
  34.5 4.1 %collective-permute-start.7 = (bf16[4,256,256]{2,1,0:T(8,128)(2,1)}, bf16[4,256,256]{2,1,0:T(8,128)(2,1)}, u32[]{:S(2)}, u32[]{:S(2)}) collective-permute-start(bf16[4,256,256]{2,1,0:T(8,128)(2,1)} %collective-permute-done.2.refs_6_), channel_id=1, source_target_pairs={{0,1},{1,0},{2,3},{3,2},{4,5},{5,4},{6,7},{7,6},{8,9},{9,8},{10,11... | collective-permute-start | bytes 1572872 | tf_op jit(solution)/shard_map/ppermute | solution.py:128
  38.7 1.6 %copy-start.3 = (bf16[16,256,256]{2,1,0:T(8,128)(2,1)S(1)}, bf16[16,256,256]{2,1,0:T(8,128)(2,1)}, u32[]{:S(2)}) copy-start(bf16[16,256,256]{2,1,0:T(8,128)(2,1)} %copy-done.2) | copy-start | bytes 6291460

commit v4 on v3

--- a/solution.py
+++ b/solution.py
@@ -33,22 +33,42 @@
     return jnp.sum(jnp.where(rank[None, :] == pair[:, None], keys[None, :], 0), axis=1)
 
 
-def add_pairs(last, list_ref, coef_ref, left_ref, right_ref, blocks, tiles, sems, sums):
-    targets = sums.shape[0]
+def terms_kernel(list_ref, coef_ref, left_hbm, right_hbm, *refs):
+    blocks, (out_ref, left_ref, right_ref, tiles, sums, sems) = refs[:-6], refs[-6:]
+    n_x, n_z = out_ref.shape[:2]
+    targets, tile, _ = sums.shape
+    band = tile // (n_x * n_z)
     pairs = list_ref.shape[0]
     sec_dev = blocks[0].shape[0]
+    end = pairs * sec_dev * len(blocks)
 
     def fetch(b):
         return pltpu.make_async_copy(
             blocks[b], tiles.at[pl.ds(b * sec_dev, sec_dev)], sems.at[b]
         )
 
-    def step(g, ready):
+    operators = [
+        pltpu.make_async_copy(left_hbm, left_ref, sems.at[len(blocks)]),
+        pltpu.make_async_copy(right_hbm, right_ref, sems.at[len(blocks) + 1]),
+    ]
+    for copy in operators:
+        copy.start()
+    for b in range(len(blocks)):
+        fetch(b).start()
+    sums[...] = jnp.zeros_like(sums)
+    for copy in operators:
+        copy.wait()
+
+    def more(state):
+        at, _ = state
+        return jnp.logical_and(at < pairs, list_ref[jnp.minimum(at, pairs - 1)] < end)
+
+    def step(state):
+        at, ready = state
         work = []
         for j in range(GROUP):
-            at = g * GROUP + j
-            valid = at < last
-            code = list_ref[jnp.minimum(at, pairs - 1)]
+            code = list_ref[at + j]
+            valid = code < end
             code = jnp.where(valid, code, 0)
             pair = lax.rem(code, pairs)
             term = lax.div(pair, targets)
@@ -66,38 +86,11 @@
             images.append((target, image * weight))
         for target, image in images:
             sums[target] += image
-        return jnp.maximum(ready, needed)
+        return at + GROUP, jnp.maximum(ready, needed)
 
-    ready = lax.fori_loop(0, lax.div(last + GROUP - 1, GROUP), step, 0)
+    _, ready = lax.while_loop(more, step, (0, 0))
     for b in range(len(blocks)):
         pl.when(ready <= b)(fetch(b).wait)
-
-
-def start_fetches(blocks, tiles, sems):
-    sec_dev = blocks[0].shape[0]
-    for b, block in enumerate(blocks):
-        pltpu.make_async_copy(block, tiles.at[pl.ds(b * sec_dev, sec_dev)], sems.at[b]).start()
-
-
-def hold_kernel(left_hbm, right_hbm, left_ref, right_ref, sems):
-    copies = [
-        pltpu.make_async_copy(left_hbm, left_ref, sems.at[0]),
-        pltpu.make_async_copy(right_hbm, right_ref, sems.at[1]),
-    ]
-    for copy in copies:
-        copy.start()
-    for copy in copies:
-        copy.wait()
-
-
-def terms_kernel(list_ref, count_ref, coef_ref, left_ref, right_ref, *refs):
-    blocks, (out_ref, tiles, sums, sems) = refs[:-4], refs[-4:]
-    n_x, n_z = out_ref.shape[:2]
-    targets, tile, _ = sums.shape
-    band = tile // (n_x * n_z)
-    start_fetches(blocks, tiles, sems)
-    sums[...] = jnp.zeros_like(sums)
-    add_pairs(count_ref[0], list_ref, coef_ref, left_ref, right_ref, blocks, tiles, sems, sums)
     for t in range(0, targets, 2):
         two = [sums[t + i].reshape(n_z, n_x, band, tile) for i in range(2)]
         rows = jnp.concatenate(two, axis=2).astype(out_ref.dtype)
@@ -128,23 +121,9 @@
         return lax.ppermute(value, "core", [(0, 1), (1, 0)])
 
     near = [from_y(psi, 1), from_y(psi, -1)]
-    far = from_y(psi, 2)
     their_psi = from_core(psi)
     code = jnp.where(active != 0, source, -1)
     other = from_y(code, n_y // 2)
-    held = pl.pallas_call(
-        hold_kernel,
-        out_shape=(
-            jax.ShapeDtypeStruct(left_ops.shape, left_ops.dtype),
-            jax.ShapeDtypeStruct(right_ops.shape, right_ops.dtype),
-        ),
-        in_specs=[anywhere] * 2,
-        out_specs=(vmem,) * 2,
-        scratch_shapes=[pltpu.SemaphoreType.DMA((2,))],
-        compiler_params=pltpu.CompilerParams(vmem_limit_bytes=16 * 2**20),
-        name="hold",
-    )(left_ops, right_ops)
-
     local_rows = lax.dynamic_slice_in_dim(psi, ops_index * band, band, 1)
     block_rows = lax.dynamic_slice_in_dim(left_block, ops_index * band, band, 1)
     local_part = jnp.einsum("tij,tjl->til", block_rows, psi, preferred_element_type=jnp.float32)
@@ -152,33 +131,38 @@
         "tij,tjl->til", local_rows, right_block, preferred_element_type=jnp.float32
     )
 
-    near, held, local_part = lax.optimization_barrier((near, held, local_part))
+    near, other, local_part = lax.optimization_barrier((near[::-1], other, local_part))
+    near = near[::-1]
+    far = from_y(near[0], 1)
+
+    codes = jnp.concatenate(
+        [jnp.where(half == 0, code, other), jnp.where(half == 0, other, code)], axis=1
+    )
+    pair_list = sorted_pairs(places_of(codes, sec_dev, core, ring, n_y).reshape(pairs))
+
     theirs = [their_psi] + [from_core(block) for block in near]
-    far, other, theirs = lax.optimization_barrier((far, other, theirs))
+    theirs, far, pair_list = lax.optimization_barrier((theirs[::-1], far, pair_list))
+    theirs = theirs[::-1]
     theirs.append(from_core(far))
     blocks = [None] * (2 * len(PLACES))
     for (_, other_place, own), my_block, their_block in zip(PLACES, [psi, *near, far], theirs):
         blocks[own], blocks[other_place] = my_block, their_block
 
-    codes = jnp.concatenate(
-        [jnp.where(half == 0, code, other), jnp.where(half == 0, other, code)], axis=1
-    )
-    places = places_of(codes, sec_dev, core, ring, n_y).reshape(pairs)
-    count = jnp.sum((places < len(blocks) * sec_dev).astype(jnp.int32)).reshape(1)
-
     partial_sum = pl.pallas_call(
         terms_kernel,
         out_shape=jax.ShapeDtypeStruct((n_x, n_z, targets * band, tile), jnp.bfloat16),
-        in_specs=[smem] * 3 + [vmem] * 2 + [anywhere] * len(blocks),
+        in_specs=[smem] * 2 + [anywhere] * (2 + len(blocks)),
         out_specs=vmem,
         scratch_shapes=[
+            pltpu.VMEM(left_ops.shape, left_ops.dtype),
+            pltpu.VMEM(right_ops.shape, right_ops.dtype),
             pltpu.VMEM((len(blocks) * sec_dev, tile, tile), psi.dtype),
             pltpu.VMEM((targets, tile, tile), jnp.float32),
-            pltpu.SemaphoreType.DMA((len(blocks),)),
+            pltpu.SemaphoreType.DMA((len(blocks) + 2,)),
         ],
-        compiler_params=pltpu.CompilerParams(vmem_limit_bytes=24 * 2**20),
+        compiler_params=pltpu.CompilerParams(vmem_limit_bytes=48 * 2**20),
         name="terms",
-    )(sorted_pairs(places), count, coef, *held, *blocks)
+    )(pair_list, coef, left_ops, right_ops, *blocks)
 
     bands = lax.all_to_all(partial_sum, "x", 0, 0, tiled=True)
     bands = lax.optimization_barrier(jnp.sum(bands.astype(jnp.float32), axis=0))

time: 93 us -> 91.2 us (0.981)
  the two profiles are of different devices: /device:TPU:2 before, /device:TPU:1 now
where the time goes in v4:
time: 91.2 us; the launch traced here: 90.7 us
  blocking collectives  42.9 us (47%)
  starting transfers between devices  27.9 us (31%)
  waiting for transfers between devices  7.64 us (8%)
  Pallas kernels  5.87 us (6%)
  matrix products  2.46 us (3%)
  local copies, waits for them, and re-layouts  1.86 us (2%)
  other arithmetic  1.86 us (2%)
    all_to_all x1, blocking collectives, per_device(): bands = lax.all_to_all(bands, ('z', 'half'), 0, 0, tiled=True)  26.3 us
    all_to_all x1, blocking collectives, per_device(): bands = lax.all_to_all(partial_sum, 'x', 0, 0, tiled=True)  16.6 us
    ppermute x4, starting transfers between devices, from_core(): return lax.ppermute(value, 'core', [(0, 1), (1, 0)])  16 us
    ppermute x4, starting transfers between devices, from_y(): return lax.ppermute(value, ('half', 'y', 'core'), route)  11.9 us
    pallas_call x1, Pallas kernels, per_device(): pl.pallas_call(terms_kernel, out_shape=jax.ShapeDtypeStruct((n_x, n_z, ta...  5.87 us
    ppermute x4, waiting for transfers between devices, from_y(): return lax.ppermute(value, ('half', 'y', 'core'), route)  4.65 us
    ppermute x4, waiting for transfers between devices, from_core(): return lax.ppermute(value, 'core', [(0, 1), (1, 0)])  2.99 us
  transfers between devices with their start and end apart: 8, of which 4 were waited for; matrix products, arithmetic and copies ran while one was open for 4% of the time, Pallas kernels for 0%

profile of v4, /device:TPU:1, one launch (start us, length us, event | category | flops | bytes accessed | tf_op | source)
XLA Modules:
  0.0 90.7 jit_solution(3201516353309388850)
XLA Ops:
  0.0 0.0 copy-start
  0.0 4.2 %collective-permute-start.1 = (bf16[4,256,256]{2,1,0:T(8,128)(2,1)}, bf16[4,256,256]{2,1,0:T(8,128)(2,1)S(1)}, u32[]{:S(2)}, u32[]{:S(2)}) collective-permute-start(bf16[4,256,256]{2,1,0:T(8,128)(2,1)} %refs_0_.1), channel_id=1, source_target_pairs={{2,0},{15,1},{4,2},{1,3},{6,4},{3,5},{8,6},{5,7},{10,8},{7,9},{12,... | collective-permute-start | bytes 1572872 | tf_op jit(solution)/shard_map/ppermute | solution.py:118
  4.2 3.8 %collective-permute-start = (bf16[4,256,256]{2,1,0:T(8,128)(2,1)}, bf16[4,256,256]{2,1,0:T(8,128)(2,1)S(1)}, u32[]{:S(2)}, u32[]{:S(2)}) collective-permute-start(bf16[4,256,256]{2,1,0:T(8,128)(2,1)} %refs_0_.1), channel_id=1, source_target_pairs={{14,0},{3,1},{0,2},{5,3},{2,4},{7,5},{4,6},{9,7},{6,8},{11,9},{8,1... | collective-permute-start | bytes 1572872 | tf_op jit(solution)/shard_map/ppermute | solution.py:118
  8.0 6.8 %collective-permute-start.5 = (bf16[4,256,256]{2,1,0:T(8,128)(2,1)}, bf16[4,256,256]{2,1,0:T(8,128)(2,1)S(1)}, u32[]{:S(2)}, u32[]{:S(2)}) collective-permute-start(bf16[4,256,256]{2,1,0:T(8,128)(2,1)} %refs_0_.1), channel_id=1, source_target_pairs={{0,1},{1,0},{2,3},{3,2},{4,5},{5,4},{6,7},{7,6},{8,9},{9,8},{10,11... | collective-permute-start | bytes 1572872 | tf_op jit(solution)/shard_map/ppermute | solution.py:121
  14.8 0.7 compare_select_fusion.15
  15.5 2.1 %collective-permute-start.2 = (s32[16,4]{0,1:T(4,128)S(1)}, s32[16,4]{0,1:T(4,128)S(1)}, u32[]{:S(2)}, u32[]{:S(2)}) collective-permute-start(s32[16,4]{0,1:T(4,128)S(1)} %compare_select_fusion.15), channel_id=1, source_target_pairs={{8,0},{9,1},{10,2},{11,3},{12,4},{13,5},{14,6},{15,7},{0,8},{1,9},... | collective-permute-start | bytes 776 | tf_op jit(solution)/shard_map/ppermute | solution.py:118
  17.6 0.0 copy-done
  17.6 1.2 %fusion.1 = f32[4,8,256]{2,1,0:T(8,128)S(1)} fusion(bf16[4,256,256]{2,1,0:T(8,128)(2,1)} %refs_0_.1, bf16[4,256,256]{2,1,0:T(8,128)(2,1)S(1)} %copy-done, s32[]{:T(128)S(6)} %select_n.255), kind=kOutput, calls=%fused_computation.8 | convolution fusion | flops 4194304 | bytes 573444 | tf_op jit(solution)/shard_map/tij,tjl->til/dot_general | solution.py:129
  18.8 1.2 %convolution_add_fusion = f32[4,8,256]{2,1,0:T(8,128)S(1)} fusion(f32[4,8,256]{2,1,0:T(8,128)S(1)} %fusion.1, bf16[4,256,256]{2,1,0:T(8,128)(2,1)} %param.15, bf16[4,256,256]{2,1,0:T(8,128)(2,1)} %refs_0_.1, s32[]{:T(128)S(6)} %select_n.255), kind=kOutput, calls=%fused_computation.1 | convolution fusion | flops 4202496 | bytes 606212 | tf_op jit(solution)/shard_map/tij,tjl->til/dot_general | solution.py:130
  20.0 3.7 %collective-permute-done.2 = s32[16,4]{0,1:T(4,128)S(1)} collective-permute-done((s32[16,4]{0,1:T(4,128)S(1)}, s32[16,4]{0,1:T(4,128)S(1)}, u32[]{:S(2)}, u32[]{:S(2)}) %collective-permute-start.2) | collective-permute-done | bytes 288 | tf_op jit(solution)/shard_map/ppermute | solution.py:118
  23.7 0.0 collective-permute-done.1.refs_2_
  23.7 0.0 collective-permute-done.refs_3_
  23.7 1.9 %collective-permute-start.6 = (bf16[4,256,256]{2,1,0:T(8,128)(2,1)S(1)}, bf16[4,256,256]{2,1,0:T(8,128)(2,1)S(1)}, u32[]{:S(2)}, u32[]{:S(2)}) collective-permute-start(bf16[4,256,256]{2,1,0:T(8,128)(2,1)S(1)} %collective-permute-done.1.refs_2_), channel_id=1, source_target_pairs={{2,0},{15,1},{4,2},{1,3},{6,4},{3,5},{8,6},{5,7},{10,8},{7,9},{12,... | collective-permute-start | bytes 1572872 | tf_op jit(solution)/shard_map/ppermute | solution.py:118
  25.6 4.3 %collective-permute-start.4 = (bf16[4,256,256]{2,1,0:T(8,128)(2,1)S(1)}, bf16[4,256,256]{2,1,0:T(8,128)(2,1)S(1)}, u32[]{:S(2)}, u32[]{:S(2)}) collective-permute-start(bf16[4,256,256]{2,1,0:T(8,128)(2,1)S(1)} %collective-permute-done.1.refs_2_), channel_id=1, source_target_pairs={{0,1},{1,0},{2,3},{3,2},{4,5},{5,4},{6,7},{7,6},{8,9},{9,8},{10,11... | collective-permute-start | bytes 1572872 | tf_op jit(solution)/shard_map/ppermute | solution.py:121
  29.9 1.9 %collective-permute-start.3 = (bf16[4,256,256]{2,1,0:T(8,128)(2,1)S(1)}, bf16[4,256,256]{2,1,0:T(8,128)(2,1)}, u32[]{:S(2)}, u32[]{:S(2)}) collective-permute-start(bf16[4,256,256]{2,1,0:T(8,128)(2,1)S(1)} %collective-permute-done.refs_3_), channel_id=1, source_target_pairs={{0,1},{1,0},{2,3},{3,2},{4,5},{5,4},{6,7},{7,6},{8,9},{9,8},{10,11... | collective-permute-start | bytes 1572872 | tf_op jit(solution)/shard_map/ppermute | solution.py:121
  31.9 0.1 copy.11
  32.0 0.1 concatenate.6
  32.1 0.2 convert_reduce_fusion.2
  32.3 0.1 select_reduce_fusion.list_ref
  32.4 0.0 collective-permute-done.5.refs_1_
  32.4 1.5 %collective-permute-done.3.refs_5_ = bf16[4,256,256]{2,1,0:T(8,128)(2,1)} collective-permute-done((bf16[4,256,256]{2,1,0:T(8,128)(2,1)S(1)}, bf16[4,256,256]{2,1,0:T(8,128)(2,1)}, u32[]{:S(2)}, u32[]{:S(2)}) %collective-permute-start.3) | collective-permute-done | bytes 524320 | tf_op jit(solution)/shard_map/ppermute | solution.py:121
  33.9 1.0 %collective-permute-done.6.refs_6_ = bf16[4,256,256]{2,1,0:T(8,128)(2,1)S(1)} collective-permute-done((bf16[4,256,256]{2,1,0:T(8,128)(2,1)S(1)}, bf16[4,256,256]{2,1,0:T(8,128)(2,1)S(1)}, u32[]{:S(2)}, u32[]{:S(2)}) %collective-permute-start.6) | collective-permute-done | bytes 524320 | tf_op jit(solution)/shard_map/ppermute | solution.py:118
  34.8 0.0 collective-permute-done.4.refs_4_
  34.8 3.0 %collective-permute-start.7 = (bf16[4,256,256]{2,1,0:T(8,128)(2,1)S(1)}, bf16[4,256,256]{2,1,0:T(8,128)(2,1)S(1)}, u32[]{:S(2)}, u32[]{:S(2)}) collective-permute-start(bf16[4,256,256]{2,1,0:T(8,128)(2,1)S(1)} %collective-permute-done.6.refs_6_), channel_id=1, source_target_pairs={{0,1},{1,0},{2,3},{3,2},{4,5},{5,4},{6,7},{7,6},{8,9},{9,8},{10,11... | collective-permute-start | bytes 1572872 | tf_op jit(solution)/shard_map/ppermute | solution.py:121
  37.9 1.5 %collective-permute-done.7.refs_7_ = bf16[4,256,256]{2,1,0:T(8,128)(2,1)S(1)} collective-permute-done((bf16[4,256,256]{2,1,0:T(8,128)(2,1)S(1)}, bf16[4,256,256]{2,1,0:T(8,128)(2,1)S(1)}, u32[]{:S(2)}, u32[]{:S(2)}) %collective-permute-start.7) | collective-permute-done | bytes 524320 | tf_op jit(solution)/shard_map/ppermute | solution.py:121
  39.4 0.0 copy-start.1
  39.4 1.0 %copy-done.1 = bf16[4,256,256]{2,1,0:T(8,128)(2,1)S(1)} copy-done((bf16[4,256,256]{2,1,0:T(8,128)(2,1)S(1)}, bf16[4,256,256]{2,1,0:T(8,128)(2,1)}, u32[]{:S(2)}) %copy-start.1) | copy-done | bytes 524312
  40.4 0.0 copy-start.2
  40.4 0.7 copy-done.2
  41.1 5.9 %terms.1 = bf16[4,8,64,256]{3,2,1,0:T(8,128)(2,1)S(1)} custom-call(s32[128]{0:T(128)S(1)} %select_reduce_fusion.list_ref, f32[16]{0:T(128)S(1)} %copy-done.2, bf16[16,256,256]{2,1,0:T(8,128)(2,1)} %left_hbm.1, bf16[16,256,256]{2,1,0:T(8,128)(2,1)} %right_hbm.1, bf16[4,256,256]{2,1,0:T(8,128)(2,1)S(1)} %copy-done.1, ...), custom_call_target="tpu_custom_call" | custom-call | tf_op jit(solution)/shard_map/terms/pallas_call | solution.py:151
  46.9 16.6 %all_to_all.10 = bf16[4,8,64,256]{3,2,1,0:T(8,128)(2,1)S(1)} all-to-all(bf16[4,8,64,256]{3,2,1,0:T(8,128)(2,1)S(1)} %terms.1), channel_id=1, replica_groups=mesh['z'=8,'x'=4,'half'=2,'y'=4,'core'=2] {'x'}, dimensions={0} | all-to-all | bytes 2097152 | tf_op jit(solution)/shard_map/all_to_all | solution.py:167
  63.5 0.2 convert_reduce_fusion
  63.7 26.3 %all_to_all.11 = bf16[16,32,256]{2,1,0:T(8,128)(2,1)S(1)} all-to-all(bf16[16,32,256]{2,1,0:T(8,128)(2,1)S(1)} %bitcast.5), channel_id=1, replica_groups=mesh['z'=8,'x'=4,'half'=2,'y'=4,'core'=2] {'z','half'}, dimensions={0} | all-to-all | bytes 524288 | tf_op jit(solution)/shard_map/all_to_all | solution.py:171
  90.0 0.6 bitcast_add_fusion
  (4 shorter events, 0.1 us)
Async XLA Ops:
  0.0 17.6 %copy-start = (bf16[4,256,256]{2,1,0:T(8,128)(2,1)S(1)}, bf16[4,256,256]{2,1,0:T(8,128)(2,1)}, u32[]{:S(2)}) copy-start(bf16[4,256,256]{2,1,0:T(8,128)(2,1)} %param.14) | copy-start | bytes 1572868
  0.0 23.7 %collective-permute-start.1 = (bf16[4,256,256]{2,1,0:T(8,128)(2,1)}, bf16[4,256,256]{2,1,0:T(8,128)(2,1)S(1)}, u32[]{:S(2)}, u32[]{:S(2)}) collective-permute-start(bf16[4,256,256]{2,1,0:T(8,128)(2,1)} %refs_0_.1), channel_id=1, source_target_pairs={{2,0},{15,1},{4,2},{1,3},{6,4},{3,5},{8,6},{5,7},{10,8},{7,9},{12,... | collective-permute-start | bytes 1572872 | tf_op jit(solution)/shard_map/ppermute | solution.py:118
  4.2 19.5 %collective-permute-start = (bf16[4,256,256]{2,1,0:T(8,128)(2,1)}, bf16[4,256,256]{2,1,0:T(8,128)(2,1)S(1)}, u32[]{:S(2)}, u32[]{:S(2)}) collective-permute-start(bf16[4,256,256]{2,1,0:T(8,128)(2,1)} %refs_0_.1), channel_id=1, source_target_pairs={{14,0},{3,1},{0,2},{5,3},{2,4},{7,5},{4,6},{9,7},{6,8},{11,9},{8,1... | collective-permute-start | bytes 1572872 | tf_op jit(solution)/shard_map/ppermute | solution.py:118
  8.0 24.4 %collective-permute-start.5 = (bf16[4,256,256]{2,1,0:T(8,128)(2,1)}, bf16[4,256,256]{2,1,0:T(8,128)(2,1)S(1)}, u32[]{:S(2)}, u32[]{:S(2)}) collective-permute-start(bf16[4,256,256]{2,1,0:T(8,128)(2,1)} %refs_0_.1), channel_id=1, source_target_pairs={{0,1},{1,0},{2,3},{3,2},{4,5},{5,4},{6,7},{7,6},{8,9},{9,8},{10,11... | collective-permute-start | bytes 1572872 | tf_op jit(solution)/shard_map/ppermute | solution.py:121
  15.5 8.2 %collective-permute-start.2 = (s32[16,4]{0,1:T(4,128)S(1)}, s32[16,4]{0,1:T(4,128)S(1)}, u32[]{:S(2)}, u32[]{:S(2)}) collective-permute-start(s32[16,4]{0,1:T(4,128)S(1)} %compare_select_fusion.15), channel_id=1, source_target_pairs={{8,0},{9,1},{10,2},{11,3},{12,4},{13,5},{14,6},{15,7},{0,8},{1,9},... | collective-permute-start | bytes 776 | tf_op jit(solution)/shard_map/ppermute | solution.py:118
  23.7 11.1 %collective-permute-start.6 = (bf16[4,256,256]{2,1,0:T(8,128)(2,1)S(1)}, bf16[4,256,256]{2,1,0:T(8,128)(2,1)S(1)}, u32[]{:S(2)}, u32[]{:S(2)}) collective-permute-start(bf16[4,256,256]{2,1,0:T(8,128)(2,1)S(1)} %collective-permute-done.1.refs_2_), channel_id=1, source_target_pairs={{2,0},{15,1},{4,2},{1,3},{6,4},{3,5},{8,6},{5,7},{10,8},{7,9},{12,... | collective-permute-start | bytes 1572872 | tf_op jit(solution)/shard_map/ppermute | solution.py:118
  25.6 9.2 %collective-permute-start.4 = (bf16[4,256,256]{2,1,0:T(8,128)(2,1)S(1)}, bf16[4,256,256]{2,1,0:T(8,128)(2,1)S(1)}, u32[]{:S(2)}, u32[]{:S(2)}) collective-permute-start(bf16[4,256,256]{2,1,0:T(8,128)(2,1)S(1)} %collective-permute-done.1.refs_2_), channel_id=1, source_target_pairs={{0,1},{1,0},{2,3},{3,2},{4,5},{5,4},{6,7},{7,6},{8,9},{9,8},{10,11... | collective-permute-start | bytes 1572872 | tf_op jit(solution)/shard_map/ppermute | solution.py:121
  29.9 3.9 %collective-permute-start.3 = (bf16[4,256,256]{2,1,0:T(8,128)(2,1)S(1)}, bf16[4,256,256]{2,1,0:T(8,128)(2,1)}, u32[]{:S(2)}, u32[]{:S(2)}) collective-permute-start(bf16[4,256,256]{2,1,0:T(8,128)(2,1)S(1)} %collective-permute-done.refs_3_), channel_id=1, source_target_pairs={{0,1},{1,0},{2,3},{3,2},{4,5},{5,4},{6,7},{7,6},{8,9},{9,8},{10,11... | collective-permute-start | bytes 1572872 | tf_op jit(solution)/shard_map/ppermute | solution.py:121
  34.8 4.5 %collective-permute-start.7 = (bf16[4,256,256]{2,1,0:T(8,128)(2,1)S(1)}, bf16[4,256,256]{2,1,0:T(8,128)(2,1)S(1)}, u32[]{:S(2)}, u32[]{:S(2)}) collective-permute-start(bf16[4,256,256]{2,1,0:T(8,128)(2,1)S(1)} %collective-permute-done.6.refs_6_), channel_id=1, source_target_pairs={{0,1},{1,0},{2,3},{3,2},{4,5},{5,4},{6,7},{7,6},{8,9},{9,8},{10,11... | collective-permute-start | bytes 1572872 | tf_op jit(solution)/shard_map/ppermute | solution.py:121
  39.4 1.0 %copy-start.1 = (bf16[4,256,256]{2,1,0:T(8,128)(2,1)S(1)}, bf16[4,256,256]{2,1,0:T(8,128)(2,1)}, u32[]{:S(2)}) copy-start(bf16[4,256,256]{2,1,0:T(8,128)(2,1)} %refs_0_.1) | copy-start | bytes 1572868
  40.4 0.7 copy-start.2

commit v5 on v4

--- a/solution.py
+++ b/solution.py
@@ -25,15 +25,17 @@
     return jnp.where(held, block * sec_dev + codes % sec_dev, 2 * len(PLACES) * sec_dev)
 
 
-def sorted_pairs(places):
+def sorted_pairs(places, weights):
     pairs = places.shape[0]
     pair = jnp.arange(pairs, dtype=jnp.int32)
     keys = places * pairs + pair
     rank = jnp.sum((keys[None, :] < keys[:, None]).astype(jnp.int32), axis=1)
-    return jnp.sum(jnp.where(rank[None, :] == pair[:, None], keys[None, :], 0), axis=1)
+    here = rank[None, :] == pair[:, None]
+    listed = jnp.sum(jnp.where(here, keys[None, :], 0), axis=1)
+    return listed, jnp.sum(jnp.where(here, weights[None, :], 0.0), axis=1)
 
 
-def terms_kernel(list_ref, coef_ref, left_hbm, right_hbm, *refs):
+def terms_kernel(list_ref, weight_ref, left_hbm, right_hbm, *refs):
     blocks, (out_ref, left_ref, right_ref, tiles, sums, sems) = refs[:-6], refs[-6:]
     n_x, n_z = out_ref.shape[:2]
     targets, tile, _ = sums.shape
@@ -72,7 +74,7 @@
             code = jnp.where(valid, code, 0)
             pair = lax.rem(code, pairs)
             term = lax.div(pair, targets)
-            weight = jnp.where(valid, coef_ref[term], 0.0)
+            weight = jnp.where(valid, weight_ref[at + j], 0.0)
             work.append((lax.div(code, pairs), term, lax.rem(pair, targets), weight))
         needed = lax.div(functools.reduce(jnp.maximum, [w[0] for w in work]), sec_dev) + 1
         for b in range(len(blocks)):
@@ -121,7 +123,6 @@
         return lax.ppermute(value, "core", [(0, 1), (1, 0)])
 
     near = [from_y(psi, 1), from_y(psi, -1)]
-    their_psi = from_core(psi)
     code = jnp.where(active != 0, source, -1)
     other = from_y(code, n_y // 2)
     local_rows = lax.dynamic_slice_in_dim(psi, ops_index * band, band, 1)
@@ -131,17 +132,18 @@
         "tij,tjl->til", local_rows, right_block, preferred_element_type=jnp.float32
     )
 
-    near, other, local_part = lax.optimization_barrier((near[::-1], other, local_part))
+    near, other, local_part, psi = lax.optimization_barrier((near[::-1], other, local_part, psi))
     near = near[::-1]
     far = from_y(near[0], 1)
 
     codes = jnp.concatenate(
         [jnp.where(half == 0, code, other), jnp.where(half == 0, other, code)], axis=1
     )
-    pair_list = sorted_pairs(places_of(codes, sec_dev, core, ring, n_y).reshape(pairs))
+    places = places_of(codes, sec_dev, core, ring, n_y).reshape(pairs)
+    listed = sorted_pairs(places, jnp.repeat(coef, targets))
 
-    theirs = [their_psi] + [from_core(block) for block in near]
-    theirs, far, pair_list = lax.optimization_barrier((theirs[::-1], far, pair_list))
+    theirs = [from_core(block) for block in [psi, *near]]
+    theirs, far, listed = lax.optimization_barrier((theirs[::-1], far, listed))
     theirs = theirs[::-1]
     theirs.append(from_core(far))
     blocks = [None] * (2 * len(PLACES))
@@ -162,7 +164,7 @@
         ],
         compiler_params=pltpu.CompilerParams(vmem_limit_bytes=48 * 2**20),
         name="terms",
-    )(pair_list, coef, left_ops, right_ops, *blocks)
+    )(*listed, left_ops, right_ops, *blocks)
 
     bands = lax.all_to_all(partial_sum, "x", 0, 0, tiled=True)
     bands = lax.optimization_barrier(jnp.sum(bands.astype(jnp.float32), axis=0))

time: 91.2 us -> 89.6 us (0.982)
  the two profiles are of different devices: /device:TPU:1 before, /device:TPU:8 now
where the time goes in v5:
time: 89.6 us; the launch traced here: 89.1 us
  blocking collectives  45.2 us (50%)
  starting transfers between devices  24.7 us (28%)
  waiting for transfers between devices  6.68 us (7%)
  Pallas kernels  5.86 us (7%)
  matrix products  2.46 us (3%)
  local copies, waits for them, and re-layouts  2.02 us (2%)
  other arithmetic  1.97 us (2%)
    all_to_all x1, blocking collectives, per_device(): bands = lax.all_to_all(bands, ('z', 'half'), 0, 0, tiled=True)  27.7 us
    all_to_all x1, blocking collectives, per_device(): bands = lax.all_to_all(partial_sum, 'x', 0, 0, tiled=True)  17.5 us
    ppermute x4, starting transfers between devices, from_y(): return lax.ppermute(value, ('half', 'y', 'core'), route)  16.5 us
    ppermute x4, starting transfers between devices, from_core(): return lax.ppermute(value, 'core', [(0, 1), (1, 0)])  8.28 us
    pallas_call x1, Pallas kernels, per_device(): pl.pallas_call(terms_kernel, out_shape=jax.ShapeDtypeStruct((n_x, n_z, ta...  5.86 us
    ppermute x4, waiting for transfers between devices, from_core(): return lax.ppermute(value, 'core', [(0, 1), (1, 0)])  3.38 us
    ppermute x4, waiting for transfers between devices, from_y(): return lax.ppermute(value, ('half', 'y', 'core'), route)  3.29 us
  transfers between devices with their start and end apart: 8, of which 3 were waited for; matrix products, arithmetic and copies ran while one was open for 5% of the time, Pallas kernels for 0%

profile of v5, /device:TPU:8, one launch (start us, length us, event | category | flops | bytes accessed | tf_op | source)
XLA Modules:
  0.0 89.1 jit_solution(4154808456339702729)
XLA Ops:
  0.0 0.0 copy-start
  0.0 7.9 %collective-permute-start.1 = (bf16[4,256,256]{2,1,0:T(8,128)(2,1)}, bf16[4,256,256]{2,1,0:T(8,128)(2,1)S(1)}, u32[]{:S(2)}, u32[]{:S(2)}) collective-permute-start(bf16[4,256,256]{2,1,0:T(8,128)(2,1)} %refs_0_), channel_id=1, source_target_pairs={{2,0},{15,1},{4,2},{1,3},{6,4},{3,5},{8,6},{5,7},{10,8},{7,9},{12,... | collective-permute-start | bytes 1572872 | tf_op jit(solution)/shard_map/ppermute | solution.py:120
  7.9 1.9 %collective-permute-start = (bf16[4,256,256]{2,1,0:T(8,128)(2,1)}, bf16[4,256,256]{2,1,0:T(8,128)(2,1)S(1)}, u32[]{:S(2)}, u32[]{:S(2)}) collective-permute-start(bf16[4,256,256]{2,1,0:T(8,128)(2,1)} %refs_0_), channel_id=1, source_target_pairs={{14,0},{3,1},{0,2},{5,3},{2,4},{7,5},{4,6},{9,7},{6,8},{11,9},{8,1... | collective-permute-start | bytes 1572872 | tf_op jit(solution)/shard_map/ppermute | solution.py:120
  9.8 0.7 compare_select_fusion.15
  10.5 3.0 %collective-permute-start.2 = (s32[16,4]{0,1:T(4,128)S(1)}, s32[16,4]{0,1:T(4,128)S(1)}, u32[]{:S(2)}, u32[]{:S(2)}) collective-permute-start(s32[16,4]{0,1:T(4,128)S(1)} %compare_select_fusion.15), channel_id=1, source_target_pairs={{8,0},{9,1},{10,2},{11,3},{12,4},{13,5},{14,6},{15,7},{0,8},{1,9},... | collective-permute-start | bytes 776 | tf_op jit(solution)/shard_map/ppermute | solution.py:120
  13.5 0.0 copy-done
  13.5 1.2 %fusion.1 = f32[4,8,256]{2,1,0:T(8,128)S(1)} fusion(bf16[4,256,256]{2,1,0:T(8,128)(2,1)} %refs_0_, bf16[4,256,256]{2,1,0:T(8,128)(2,1)S(1)} %copy-done, s32[]{:T(128)S(6)} %select_n.259), kind=kOutput, calls=%fused_computation.9 | convolution fusion | flops 4194304 | bytes 573444 | tf_op jit(solution)/shard_map/tij,tjl->til/dot_general | solution.py:130
  14.8 1.2 %convolution_add_fusion = f32[4,8,256]{2,1,0:T(8,128)S(1)} fusion(f32[4,8,256]{2,1,0:T(8,128)S(1)} %fusion.1, bf16[4,256,256]{2,1,0:T(8,128)(2,1)} %param.15, bf16[4,256,256]{2,1,0:T(8,128)(2,1)} %refs_0_, s32[]{:T(128)S(6)} %select_n.259), kind=kOutput, calls=%fused_computation.1 | convolution fusion | flops 4202496 | bytes 606212 | tf_op jit(solution)/shard_map/tij,tjl->til/dot_general | solution.py:131
  16.0 0.7 broadcast_in_dim.61
  16.7 0.1 broadcast_in_dim.62
  16.8 3.3 %collective-permute-done.2 = s32[16,4]{0,1:T(4,128)S(1)} collective-permute-done((s32[16,4]{0,1:T(4,128)S(1)}, s32[16,4]{0,1:T(4,128)S(1)}, u32[]{:S(2)}, u32[]{:S(2)}) %collective-permute-start.2) | collective-permute-done | bytes 288 | tf_op jit(solution)/shard_map/ppermute | solution.py:120
  20.1 0.0 collective-permute-done.1.refs_2_
  20.1 0.0 collective-permute-done.refs_3_
  20.1 3.7 %collective-permute-start.6 = (bf16[4,256,256]{2,1,0:T(8,128)(2,1)S(1)}, bf16[4,256,256]{2,1,0:T(8,128)(2,1)S(1)}, u32[]{:S(2)}, u32[]{:S(2)}) collective-permute-start(bf16[4,256,256]{2,1,0:T(8,128)(2,1)S(1)} %collective-permute-done.1.refs_2_), channel_id=1, source_target_pairs={{2,0},{15,1},{4,2},{1,3},{6,4},{3,5},{8,6},{5,7},{10,8},{7,9},{12,... | collective-permute-start | bytes 1572872 | tf_op jit(solution)/shard_map/ppermute | solution.py:120
  23.8 1.9 %collective-permute-start.4 = (bf16[4,256,256]{2,1,0:T(8,128)(2,1)S(1)}, bf16[4,256,256]{2,1,0:T(8,128)(2,1)S(1)}, u32[]{:S(2)}, u32[]{:S(2)}) collective-permute-start(bf16[4,256,256]{2,1,0:T(8,128)(2,1)S(1)} %collective-permute-done.1.refs_2_), channel_id=1, source_target_pairs={{0,1},{1,0},{2,3},{3,2},{4,5},{5,4},{6,7},{7,6},{8,9},{9,8},{10,11... | collective-permute-start | bytes 1572872 | tf_op jit(solution)/shard_map/ppermute | solution.py:123
  25.8 0.1 copy.11
  25.8 0.1 concatenate.6
  25.9 2.4 %collective-permute-start.3 = (bf16[4,256,256]{2,1,0:T(8,128)(2,1)S(1)}, bf16[4,256,256]{2,1,0:T(8,128)(2,1)S(1)}, u32[]{:S(2)}, u32[]{:S(2)}) collective-permute-start(bf16[4,256,256]{2,1,0:T(8,128)(2,1)S(1)} %collective-permute-done.refs_3_), channel_id=1, source_target_pairs={{0,1},{1,0},{2,3},{3,2},{4,5},{5,4},{6,7},{7,6},{8,9},{9,8},{10,11... | collective-permute-start | bytes 1572872 | tf_op jit(solution)/shard_map/ppermute | solution.py:123
  28.3 1.9 %collective-permute-start.5 = (bf16[4,256,256]{2,1,0:T(8,128)(2,1)}, bf16[4,256,256]{2,1,0:T(8,128)(2,1)S(1)}, u32[]{:S(2)}, u32[]{:S(2)}) collective-permute-start(bf16[4,256,256]{2,1,0:T(8,128)(2,1)} %refs_0_), channel_id=1, source_target_pairs={{0,1},{1,0},{2,3},{3,2},{4,5},{5,4},{6,7},{7,6},{8,9},{9,8},{10,11... | collective-permute-start | bytes 1572872 | tf_op jit(solution)/shard_map/ppermute | solution.py:123
  30.3 0.2 convert_reduce_fusion.2
  30.5 0.1 select_reduce_fusion.1.list_ref
  30.6 0.1 select_reduce_fusion.weight_ref
  30.7 0.0 collective-permute-done.3.refs_5_
  30.7 1.6 %collective-permute-done.5.refs_1_ = bf16[4,256,256]{2,1,0:T(8,128)(2,1)S(1)} collective-permute-done((bf16[4,256,256]{2,1,0:T(8,128)(2,1)}, bf16[4,256,256]{2,1,0:T(8,128)(2,1)S(1)}, u32[]{:S(2)}, u32[]{:S(2)}) %collective-permute-start.5) | collective-permute-done | bytes 524320 | tf_op jit(solution)/shard_map/ppermute | solution.py:123
  32.4 0.0 collective-permute-done.6.refs_6_
  32.4 0.0 collective-permute-done.4.refs_4_
  32.4 2.0 %collective-permute-start.7 = (bf16[4,256,256]{2,1,0:T(8,128)(2,1)S(1)}, bf16[4,256,256]{2,1,0:T(8,128)(2,1)S(1)}, u32[]{:S(2)}, u32[]{:S(2)}) collective-permute-start(bf16[4,256,256]{2,1,0:T(8,128)(2,1)S(1)} %collective-permute-done.6.refs_6_), channel_id=1, source_target_pairs={{0,1},{1,0},{2,3},{3,2},{4,5},{5,4},{6,7},{7,6},{8,9},{9,8},{10,11... | collective-permute-start | bytes 1572872 | tf_op jit(solution)/shard_map/ppermute | solution.py:123
  34.4 1.8 %collective-permute-done.7.refs_7_ = bf16[4,256,256]{2,1,0:T(8,128)(2,1)S(1)} collective-permute-done((bf16[4,256,256]{2,1,0:T(8,128)(2,1)S(1)}, bf16[4,256,256]{2,1,0:T(8,128)(2,1)S(1)}, u32[]{:S(2)}, u32[]{:S(2)}) %collective-permute-start.7) | collective-permute-done | bytes 524320 | tf_op jit(solution)/shard_map/ppermute | solution.py:123
  36.2 0.0 copy-start.1
  36.2 1.0 %copy-done.1 = bf16[4,256,256]{2,1,0:T(8,128)(2,1)S(1)} copy-done((bf16[4,256,256]{2,1,0:T(8,128)(2,1)S(1)}, bf16[4,256,256]{2,1,0:T(8,128)(2,1)}, u32[]{:S(2)}) %copy-start.1) | copy-done | bytes 524312
  37.2 5.9 %terms.1 = bf16[4,8,64,256]{3,2,1,0:T(8,128)(2,1)S(1)} custom-call(s32[128]{0:T(128)S(1)} %select_reduce_fusion.1.list_ref, f32[128]{0:T(128)S(1)} %select_reduce_fusion.weight_ref, bf16[16,256,256]{2,1,0:T(8,128)(2,1)} %left_hbm.1, bf16[16,256,256]{2,1,0:T(8,128)(2,1)} %right_hbm.1, bf16[4,256,256]{2,1,0:T(8,128)(2,1)S(1)} %copy-done.1, ...), custom_call_target="tpu_custom_call" | custom-call | tf_op jit(solution)/shard_map/terms/pallas_call | solution.py:153
  43.1 17.5 %all_to_all.10 = bf16[4,8,64,256]{3,2,1,0:T(8,128)(2,1)S(1)} all-to-all(bf16[4,8,64,256]{3,2,1,0:T(8,128)(2,1)S(1)} %terms.1), channel_id=1, replica_groups=mesh['z'=8,'x'=4,'half'=2,'y'=4,'core'=2] {'x'}, dimensions={0} | all-to-all | bytes 2097152 | tf_op jit(solution)/shard_map/all_to_all | solution.py:169
  60.5 0.2 convert_reduce_fusion
  60.7 27.7 %all_to_all.11 = bf16[16,32,256]{2,1,0:T(8,128)(2,1)S(1)} all-to-all(bf16[16,32,256]{2,1,0:T(8,128)(2,1)S(1)} %bitcast.5), channel_id=1, replica_groups=mesh['z'=8,'x'=4,'half'=2,'y'=4,'core'=2] {'z','half'}, dimensions={0} | all-to-all | bytes 524288 | tf_op jit(solution)/shard_map/all_to_all | solution.py:173
  88.5 0.6 bitcast_add_fusion
  (4 shorter events, 0.1 us)
Async XLA Ops:
  0.0 13.5 %copy-start = (bf16[4,256,256]{2,1,0:T(8,128)(2,1)S(1)}, bf16[4,256,256]{2,1,0:T(8,128)(2,1)}, u32[]{:S(2)}) copy-start(bf16[4,256,256]{2,1,0:T(8,128)(2,1)} %param.14) | copy-start | bytes 1572868
  0.0 20.1 %collective-permute-start.1 = (bf16[4,256,256]{2,1,0:T(8,128)(2,1)}, bf16[4,256,256]{2,1,0:T(8,128)(2,1)S(1)}, u32[]{:S(2)}, u32[]{:S(2)}) collective-permute-start(bf16[4,256,256]{2,1,0:T(8,128)(2,1)} %refs_0_), channel_id=1, source_target_pairs={{2,0},{15,1},{4,2},{1,3},{6,4},{3,5},{8,6},{5,7},{10,8},{7,9},{12,... | collective-permute-start | bytes 1572872 | tf_op jit(solution)/shard_map/ppermute | solution.py:120
  7.9 12.3 %collective-permute-start = (bf16[4,256,256]{2,1,0:T(8,128)(2,1)}, bf16[4,256,256]{2,1,0:T(8,128)(2,1)S(1)}, u32[]{:S(2)}, u32[]{:S(2)}) collective-permute-start(bf16[4,256,256]{2,1,0:T(8,128)(2,1)} %refs_0_), channel_id=1, source_target_pairs={{14,0},{3,1},{0,2},{5,3},{2,4},{7,5},{4,6},{9,7},{6,8},{11,9},{8,1... | collective-permute-start | bytes 1572872 | tf_op jit(solution)/shard_map/ppermute | solution.py:120
  10.5 9.6 %collective-permute-start.2 = (s32[16,4]{0,1:T(4,128)S(1)}, s32[16,4]{0,1:T(4,128)S(1)}, u32[]{:S(2)}, u32[]{:S(2)}) collective-permute-start(s32[16,4]{0,1:T(4,128)S(1)} %compare_select_fusion.15), channel_id=1, source_target_pairs={{8,0},{9,1},{10,2},{11,3},{12,4},{13,5},{14,6},{15,7},{0,8},{1,9},... | collective-permute-start | bytes 776 | tf_op jit(solution)/shard_map/ppermute | solution.py:120
  20.1 12.2 %collective-permute-start.6 = (bf16[4,256,256]{2,1,0:T(8,128)(2,1)S(1)}, bf16[4,256,256]{2,1,0:T(8,128)(2,1)S(1)}, u32[]{:S(2)}, u32[]{:S(2)}) collective-permute-start(bf16[4,256,256]{2,1,0:T(8,128)(2,1)S(1)} %collective-permute-done.1.refs_2_), channel_id=1, source_target_pairs={{2,0},{15,1},{4,2},{1,3},{6,4},{3,5},{8,6},{5,7},{10,8},{7,9},{12,... | collective-permute-start | bytes 1572872 | tf_op jit(solution)/shard_map/ppermute | solution.py:120
  23.8 8.6 %collective-permute-start.4 = (bf16[4,256,256]{2,1,0:T(8,128)(2,1)S(1)}, bf16[4,256,256]{2,1,0:T(8,128)(2,1)S(1)}, u32[]{:S(2)}, u32[]{:S(2)}) collective-permute-start(bf16[4,256,256]{2,1,0:T(8,128)(2,1)S(1)} %collective-permute-done.1.refs_2_), channel_id=1, source_target_pairs={{0,1},{1,0},{2,3},{3,2},{4,5},{5,4},{6,7},{7,6},{8,9},{9,8},{10,11... | collective-permute-start | bytes 1572872 | tf_op jit(solution)/shard_map/ppermute | solution.py:123
  25.9 4.8 %collective-permute-start.3 = (bf16[4,256,256]{2,1,0:T(8,128)(2,1)S(1)}, bf16[4,256,256]{2,1,0:T(8,128)(2,1)S(1)}, u32[]{:S(2)}, u32[]{:S(2)}) collective-permute-start(bf16[4,256,256]{2,1,0:T(8,128)(2,1)S(1)} %collective-permute-done.refs_3_), channel_id=1, source_target_pairs={{0,1},{1,0},{2,3},{3,2},{4,5},{5,4},{6,7},{7,6},{8,9},{9,8},{10,11... | collective-permute-start | bytes 1572872 | tf_op jit(solution)/shard_map/ppermute | solution.py:123
  28.3 4.0 %collective-permute-start.5 = (bf16[4,256,256]{2,1,0:T(8,128)(2,1)}, bf16[4,256,256]{2,1,0:T(8,128)(2,1)S(1)}, u32[]{:S(2)}, u32[]{:S(2)}) collective-permute-start(bf16[4,256,256]{2,1,0:T(8,128)(2,1)} %refs_0_), channel_id=1, source_target_pairs={{0,1},{1,0},{2,3},{3,2},{4,5},{5,4},{6,7},{7,6},{8,9},{9,8},{10,11... | collective-permute-start | bytes 1572872 | tf_op jit(solution)/shard_map/ppermute | solution.py:123
  32.4 3.8 %collective-permute-start.7 = (bf16[4,256,256]{2,1,0:T(8,128)(2,1)S(1)}, bf16[4,256,256]{2,1,0:T(8,128)(2,1)S(1)}, u32[]{:S(2)}, u32[]{:S(2)}) collective-permute-start(bf16[4,256,256]{2,1,0:T(8,128)(2,1)S(1)} %collective-permute-done.6.refs_6_), channel_id=1, source_target_pairs={{0,1},{1,0},{2,3},{3,2},{4,5},{5,4},{6,7},{7,6},{8,9},{9,8},{10,11... | collective-permute-start | bytes 1572872 | tf_op jit(solution)/shard_map/ppermute | solution.py:123
  36.2 1.0 %copy-start.1 = (bf16[4,256,256]{2,1,0:T(8,128)(2,1)S(1)}, bf16[4,256,256]{2,1,0:T(8,128)(2,1)}, u32[]{:S(2)}) copy-start(bf16[4,256,256]{2,1,0:T(8,128)(2,1)} %refs_0_) | copy-start | bytes 1572868

commit v6 on v5

--- a/solution.py
+++ b/solution.py
@@ -122,7 +122,7 @@
     def from_core(value):
         return lax.ppermute(value, "core", [(0, 1), (1, 0)])
 
-    near = [from_y(psi, 1), from_y(psi, -1)]
+    first = from_y(psi, 1)
     code = jnp.where(active != 0, source, -1)
     other = from_y(code, n_y // 2)
     local_rows = lax.dynamic_slice_in_dim(psi, ops_index * band, band, 1)
@@ -132,9 +132,9 @@
         "tij,tjl->til", local_rows, right_block, preferred_element_type=jnp.float32
     )
 
-    near, other, local_part, psi = lax.optimization_barrier((near[::-1], other, local_part, psi))
-    near = near[::-1]
-    far = from_y(near[0], 1)
+    first, other, local_part, psi = lax.optimization_barrier((first, other, local_part, psi))
+    far = from_y(first, 1)
+    near = [first, from_y(psi, -1)]
 
     codes = jnp.concatenate(
         [jnp.where(half == 0, code, other), jnp.where(half == 0, other, code)], axis=1

time: 89.6 us -> 90.8 us (1.013)
  waiting for transfers between devices: 6.68 us -> 9.38 us
  blocking collectives: 45.2 us -> 43.8 us
    ppermute x4, waiting for transfers between devices: 3.29 us -> 7.29 us  [from_y(): return lax.ppermute(value, ('half', 'y', 'core'), route)]
    all_to_all x1, blocking collectives: 27.7 us -> 26 us  [per_device(): bands = lax.all_to_all(bands, ('z', 'half'), 0, 0, tiled=True)]
    ppermute x4, waiting for transfers between devices: 3.38 us -> 2.09 us  [from_core(): return lax.ppermute(value, 'core', [(0, 1), (1, 0)])]
  transfers between devices with their start and end apart: 8 -> 8, of which waited for: 3 -> 5; matrix products, arithmetic and copies ran while one was open for 5% -> 5% of each run, Pallas kernels for 0% -> 0%
where the time goes in v6:
time: 90.8 us; the launch traced here: 90.3 us
  blocking collectives  43.8 us (48%)
  starting transfers between devices  24.1 us (27%)
  waiting for transfers between devices  9.38 us (10%)
  Pallas kernels  6.45 us (7%)
  matrix products  2.46 us (3%)
  local copies, waits for them, and re-layouts  2.02 us (2%)
  other arithmetic  1.97 us (2%)
    all_to_all x1, blocking collectives, per_device(): bands = lax.all_to_all(bands, ('z', 'half'), 0, 0, tiled=True)  26 us
    all_to_all x1, blocking collectives, per_device(): bands = lax.all_to_all(partial_sum, 'x', 0, 0, tiled=True)  17.7 us
    ppermute x4, starting transfers between devices, from_y(): return lax.ppermute(value, ('half', 'y', 'core'), route)  16 us
    ppermute x4, starting transfers between devices, from_core(): return lax.ppermute(value, 'core', [(0, 1), (1, 0)])  8.04 us
    ppermute x4, waiting for transfers between devices, from_y(): return lax.ppermute(value, ('half', 'y', 'core'), route)  7.29 us
    pallas_call x1, Pallas kernels, per_device(): pl.pallas_call(terms_kernel, out_shape=jax.ShapeDtypeStruct((n_x, n_z, ta...  6.45 us
    ppermute x4, waiting for transfers between devices, from_core(): return lax.ppermute(value, 'core', [(0, 1), (1, 0)])  2.09 us
  transfers between devices with their start and end apart: 8, of which 5 were waited for; matrix products, arithmetic and copies ran while one was open for 5% of the time, Pallas kernels for 0%

profile of v6, /device:TPU:8, one launch (start us, length us, event | category | flops | bytes accessed | tf_op | source)
XLA Modules:
  0.0 90.3 jit_solution(3104041311872598731)
XLA Ops:
  0.0 0.0 copy-start
  0.0 7.9 %collective-permute-start = (bf16[4,256,256]{2,1,0:T(8,128)(2,1)}, bf16[4,256,256]{2,1,0:T(8,128)(2,1)S(1)}, u32[]{:S(2)}, u32[]{:S(2)}) collective-permute-start(bf16[4,256,256]{2,1,0:T(8,128)(2,1)} %refs_0_), channel_id=1, source_target_pairs={{2,0},{15,1},{4,2},{1,3},{6,4},{3,5},{8,6},{5,7},{10,8},{7,9},{12,... | collective-permute-start | bytes 1572872 | tf_op jit(solution)/shard_map/ppermute | solution.py:120
  7.9 0.7 compare_select_fusion.15
  8.6 2.3 %collective-permute-start.1 = (s32[16,4]{0,1:T(4,128)S(1)}, s32[16,4]{0,1:T(4,128)S(1)}, u32[]{:S(2)}, u32[]{:S(2)}) collective-permute-start(s32[16,4]{0,1:T(4,128)S(1)} %compare_select_fusion.15), channel_id=1, source_target_pairs={{8,0},{9,1},{10,2},{11,3},{12,4},{13,5},{14,6},{15,7},{0,8},{1,9},... | collective-permute-start | bytes 776 | tf_op jit(solution)/shard_map/ppermute | solution.py:120
  10.9 0.0 copy-done
  10.9 1.2 %fusion.1 = f32[4,8,256]{2,1,0:T(8,128)S(1)} fusion(bf16[4,256,256]{2,1,0:T(8,128)(2,1)} %refs_0_, bf16[4,256,256]{2,1,0:T(8,128)(2,1)S(1)} %copy-done, s32[]{:T(128)S(6)} %select_n.259), kind=kOutput, calls=%fused_computation.9 | convolution fusion | flops 4194304 | bytes 573444 | tf_op jit(solution)/shard_map/tij,tjl->til/dot_general | solution.py:130
  12.2 1.2 %convolution_add_fusion = f32[4,8,256]{2,1,0:T(8,128)S(1)} fusion(f32[4,8,256]{2,1,0:T(8,128)S(1)} %fusion.1, bf16[4,256,256]{2,1,0:T(8,128)(2,1)} %param.15, bf16[4,256,256]{2,1,0:T(8,128)(2,1)} %refs_0_, s32[]{:T(128)S(6)} %select_n.259), kind=kOutput, calls=%fused_computation.1 | convolution fusion | flops 4202496 | bytes 606212 | tf_op jit(solution)/shard_map/tij,tjl->til/dot_general | solution.py:131
  13.4 4.6 %collective-permute-done.1 = s32[16,4]{0,1:T(4,128)S(1)} collective-permute-done((s32[16,4]{0,1:T(4,128)S(1)}, s32[16,4]{0,1:T(4,128)S(1)}, u32[]{:S(2)}, u32[]{:S(2)}) %collective-permute-start.1) | collective-permute-done | bytes 288 | tf_op jit(solution)/shard_map/ppermute | solution.py:120
  18.0 0.0 collective-permute-done.refs_2_
  18.0 1.9 %collective-permute-start.2 = (bf16[4,256,256]{2,1,0:T(8,128)(2,1)}, bf16[4,256,256]{2,1,0:T(8,128)(2,1)S(1)}, u32[]{:S(2)}, u32[]{:S(2)}) collective-permute-start(bf16[4,256,256]{2,1,0:T(8,128)(2,1)} %refs_0_), channel_id=1, source_target_pairs={{14,0},{3,1},{0,2},{5,3},{2,4},{7,5},{4,6},{9,7},{6,8},{11,9},{8,1... | collective-permute-start | bytes 1572872 | tf_op jit(solution)/shard_map/ppermute | solution.py:120
  20.0 0.7 broadcast_in_dim.61
  20.7 0.1 broadcast_in_dim.62
  20.8 1.9 %collective-permute-start.5 = (bf16[4,256,256]{2,1,0:T(8,128)(2,1)}, bf16[4,256,256]{2,1,0:T(8,128)(2,1)S(1)}, u32[]{:S(2)}, u32[]{:S(2)}) collective-permute-start(bf16[4,256,256]{2,1,0:T(8,128)(2,1)} %refs_0_), channel_id=1, source_target_pairs={{0,1},{1,0},{2,3},{3,2},{4,5},{5,4},{6,7},{7,6},{8,9},{9,8},{10,11... | collective-permute-start | bytes 1572872 | tf_op jit(solution)/shard_map/ppermute | solution.py:123
  22.7 3.9 %collective-permute-start.6 = (bf16[4,256,256]{2,1,0:T(8,128)(2,1)S(1)}, bf16[4,256,256]{2,1,0:T(8,128)(2,1)S(1)}, u32[]{:S(2)}, u32[]{:S(2)}) collective-permute-start(bf16[4,256,256]{2,1,0:T(8,128)(2,1)S(1)} %collective-permute-done.refs_2_), channel_id=1, source_target_pairs={{2,0},{15,1},{4,2},{1,3},{6,4},{3,5},{8,6},{5,7},{10,8},{7,9},{12,... | collective-permute-start | bytes 1572872 | tf_op jit(solution)/shard_map/ppermute | solution.py:120
  26.7 1.9 %collective-permute-start.4 = (bf16[4,256,256]{2,1,0:T(8,128)(2,1)S(1)}, bf16[4,256,256]{2,1,0:T(8,128)(2,1)S(1)}, u32[]{:S(2)}, u32[]{:S(2)}) collective-permute-start(bf16[4,256,256]{2,1,0:T(8,128)(2,1)S(1)} %collective-permute-done.refs_2_), channel_id=1, source_target_pairs={{0,1},{1,0},{2,3},{3,2},{4,5},{5,4},{6,7},{7,6},{8,9},{9,8},{10,11... | collective-permute-start | bytes 1572872 | tf_op jit(solution)/shard_map/ppermute | solution.py:123
  28.6 0.1 copy.11
  28.7 0.1 concatenate.6
  28.8 1.8 %collective-permute-done.2.refs_3_ = bf16[4,256,256]{2,1,0:T(8,128)(2,1)S(1)} collective-permute-done((bf16[4,256,256]{2,1,0:T(8,128)(2,1)}, bf16[4,256,256]{2,1,0:T(8,128)(2,1)S(1)}, u32[]{:S(2)}, u32[]{:S(2)}) %collective-permute-start.2) | collective-permute-done | bytes 524320 | tf_op jit(solution)/shard_map/ppermute | solution.py:120
  30.6 1.9 %collective-permute-start.3 = (bf16[4,256,256]{2,1,0:T(8,128)(2,1)S(1)}, bf16[4,256,256]{2,1,0:T(8,128)(2,1)S(1)}, u32[]{:S(2)}, u32[]{:S(2)}) collective-permute-start(bf16[4,256,256]{2,1,0:T(8,128)(2,1)S(1)} %collective-permute-done.2.refs_3_), channel_id=1, source_target_pairs={{0,1},{1,0},{2,3},{3,2},{4,5},{5,4},{6,7},{7,6},{8,9},{9,8},{10,11... | collective-permute-start | bytes 1572872 | tf_op jit(solution)/shard_map/ppermute | solution.py:123
  32.5 0.2 convert_reduce_fusion.2
  32.7 0.1 select_reduce_fusion.1.list_ref
  32.8 0.1 select_reduce_fusion.weight_ref
  33.0 0.0 collective-permute-done.5.refs_1_
  33.0 0.8 collective-permute-done.6.refs_6_
  33.8 0.0 collective-permute-done.4.refs_4_
  33.8 0.6 collective-permute-done.3.refs_5_
  34.4 2.3 %collective-permute-start.7 = (bf16[4,256,256]{2,1,0:T(8,128)(2,1)S(1)}, bf16[4,256,256]{2,1,0:T(8,128)(2,1)S(1)}, u32[]{:S(2)}, u32[]{:S(2)}) collective-permute-start(bf16[4,256,256]{2,1,0:T(8,128)(2,1)S(1)} %collective-permute-done.6.refs_6_), channel_id=1, source_target_pairs={{0,1},{1,0},{2,3},{3,2},{4,5},{5,4},{6,7},{7,6},{8,9},{9,8},{10,11... | collective-permute-start | bytes 1572872 | tf_op jit(solution)/shard_map/ppermute | solution.py:123
  36.7 1.5 %collective-permute-done.7.refs_7_ = bf16[4,256,256]{2,1,0:T(8,128)(2,1)S(1)} collective-permute-done((bf16[4,256,256]{2,1,0:T(8,128)(2,1)S(1)}, bf16[4,256,256]{2,1,0:T(8,128)(2,1)S(1)}, u32[]{:S(2)}, u32[]{:S(2)}) %collective-permute-start.7) | collective-permute-done | bytes 524320 | tf_op jit(solution)/shard_map/ppermute | solution.py:123
  38.2 0.0 copy-start.1
  38.2 1.0 %copy-done.1 = bf16[4,256,256]{2,1,0:T(8,128)(2,1)S(1)} copy-done((bf16[4,256,256]{2,1,0:T(8,128)(2,1)S(1)}, bf16[4,256,256]{2,1,0:T(8,128)(2,1)}, u32[]{:S(2)}) %copy-start.1) | copy-done | bytes 524312
  39.2 6.4 %terms.1 = bf16[4,8,64,256]{3,2,1,0:T(8,128)(2,1)S(1)} custom-call(s32[128]{0:T(128)S(1)} %select_reduce_fusion.1.list_ref, f32[128]{0:T(128)S(1)} %select_reduce_fusion.weight_ref, bf16[16,256,256]{2,1,0:T(8,128)(2,1)} %left_hbm.1, bf16[16,256,256]{2,1,0:T(8,128)(2,1)} %right_hbm.1, bf16[4,256,256]{2,1,0:T(8,128)(2,1)S(1)} %copy-done.1, ...), custom_call_target="tpu_custom_call" | custom-call | tf_op jit(solution)/shard_map/terms/pallas_call | solution.py:153
  45.7 17.7 %all_to_all.10 = bf16[4,8,64,256]{3,2,1,0:T(8,128)(2,1)S(1)} all-to-all(bf16[4,8,64,256]{3,2,1,0:T(8,128)(2,1)S(1)} %terms.1), channel_id=1, replica_groups=mesh['z'=8,'x'=4,'half'=2,'y'=4,'core'=2] {'x'}, dimensions={0} | all-to-all | bytes 2097152 | tf_op jit(solution)/shard_map/all_to_all | solution.py:169
  63.4 0.2 convert_reduce_fusion
  63.6 26.0 %all_to_all.11 = bf16[16,32,256]{2,1,0:T(8,128)(2,1)S(1)} all-to-all(bf16[16,32,256]{2,1,0:T(8,128)(2,1)S(1)} %bitcast.5), channel_id=1, replica_groups=mesh['z'=8,'x'=4,'half'=2,'y'=4,'core'=2] {'z','half'}, dimensions={0} | all-to-all | bytes 524288 | tf_op jit(solution)/shard_map/all_to_all | solution.py:173
  89.7 0.6 bitcast_add_fusion
  (4 shorter events, 0.1 us)
Async XLA Ops:
  0.0 10.9 %copy-start = (bf16[4,256,256]{2,1,0:T(8,128)(2,1)S(1)}, bf16[4,256,256]{2,1,0:T(8,128)(2,1)}, u32[]{:S(2)}) copy-start(bf16[4,256,256]{2,1,0:T(8,128)(2,1)} %param.14) | copy-start | bytes 1572868
  0.0 18.0 %collective-permute-start = (bf16[4,256,256]{2,1,0:T(8,128)(2,1)}, bf16[4,256,256]{2,1,0:T(8,128)(2,1)S(1)}, u32[]{:S(2)}, u32[]{:S(2)}) collective-permute-start(bf16[4,256,256]{2,1,0:T(8,128)(2,1)} %refs_0_), channel_id=1, source_target_pairs={{2,0},{15,1},{4,2},{1,3},{6,4},{3,5},{8,6},{5,7},{10,8},{7,9},{12,... | collective-permute-start | bytes 1572872 | tf_op jit(solution)/shard_map/ppermute | solution.py:120
  8.6 9.5 %collective-permute-start.1 = (s32[16,4]{0,1:T(4,128)S(1)}, s32[16,4]{0,1:T(4,128)S(1)}, u32[]{:S(2)}, u32[]{:S(2)}) collective-permute-start(s32[16,4]{0,1:T(4,128)S(1)} %compare_select_fusion.15), channel_id=1, source_target_pairs={{8,0},{9,1},{10,2},{11,3},{12,4},{13,5},{14,6},{15,7},{0,8},{1,9},... | collective-permute-start | bytes 776 | tf_op jit(solution)/shard_map/ppermute | solution.py:120
  18.0 12.5 %collective-permute-start.2 = (bf16[4,256,256]{2,1,0:T(8,128)(2,1)}, bf16[4,256,256]{2,1,0:T(8,128)(2,1)S(1)}, u32[]{:S(2)}, u32[]{:S(2)}) collective-permute-start(bf16[4,256,256]{2,1,0:T(8,128)(2,1)} %refs_0_), channel_id=1, source_target_pairs={{14,0},{3,1},{0,2},{5,3},{2,4},{7,5},{4,6},{9,7},{6,8},{11,9},{8,1... | collective-permute-start | bytes 1572872 | tf_op jit(solution)/shard_map/ppermute | solution.py:120
  20.8 12.2 %collective-permute-start.5 = (bf16[4,256,256]{2,1,0:T(8,128)(2,1)}, bf16[4,256,256]{2,1,0:T(8,128)(2,1)S(1)}, u32[]{:S(2)}, u32[]{:S(2)}) collective-permute-start(bf16[4,256,256]{2,1,0:T(8,128)(2,1)} %refs_0_), channel_id=1, source_target_pairs={{0,1},{1,0},{2,3},{3,2},{4,5},{5,4},{6,7},{7,6},{8,9},{9,8},{10,11... | collective-permute-start | bytes 1572872 | tf_op jit(solution)/shard_map/ppermute | solution.py:123
  22.7 11.1 %collective-permute-start.6 = (bf16[4,256,256]{2,1,0:T(8,128)(2,1)S(1)}, bf16[4,256,256]{2,1,0:T(8,128)(2,1)S(1)}, u32[]{:S(2)}, u32[]{:S(2)}) collective-permute-start(bf16[4,256,256]{2,1,0:T(8,128)(2,1)S(1)} %collective-permute-done.refs_2_), channel_id=1, source_target_pairs={{2,0},{15,1},{4,2},{1,3},{6,4},{3,5},{8,6},{5,7},{10,8},{7,9},{12,... | collective-permute-start | bytes 1572872 | tf_op jit(solution)/shard_map/ppermute | solution.py:120
  26.7 7.1 %collective-permute-start.4 = (bf16[4,256,256]{2,1,0:T(8,128)(2,1)S(1)}, bf16[4,256,256]{2,1,0:T(8,128)(2,1)S(1)}, u32[]{:S(2)}, u32[]{:S(2)}) collective-permute-start(bf16[4,256,256]{2,1,0:T(8,128)(2,1)S(1)} %collective-permute-done.refs_2_), channel_id=1, source_target_pairs={{0,1},{1,0},{2,3},{3,2},{4,5},{5,4},{6,7},{7,6},{8,9},{9,8},{10,11... | collective-permute-start | bytes 1572872 | tf_op jit(solution)/shard_map/ppermute | solution.py:123
  30.6 3.8 %collective-permute-start.3 = (bf16[4,256,256]{2,1,0:T(8,128)(2,1)S(1)}, bf16[4,256,256]{2,1,0:T(8,128)(2,1)S(1)}, u32[]{:S(2)}, u32[]{:S(2)}) collective-permute-start(bf16[4,256,256]{2,1,0:T(8,128)(2,1)S(1)} %collective-permute-done.2.refs_3_), channel_id=1, source_target_pairs={{0,1},{1,0},{2,3},{3,2},{4,5},{5,4},{6,7},{7,6},{8,9},{9,8},{10,11... | collective-permute-start | bytes 1572872 | tf_op jit(solution)/shard_map/ppermute | solution.py:123
  34.4 3.8 %collective-permute-start.7 = (bf16[4,256,256]{2,1,0:T(8,128)(2,1)S(1)}, bf16[4,256,256]{2,1,0:T(8,128)(2,1)S(1)}, u32[]{:S(2)}, u32[]{:S(2)}) collective-permute-start(bf16[4,256,256]{2,1,0:T(8,128)(2,1)S(1)} %collective-permute-done.6.refs_6_), channel_id=1, source_target_pairs={{0,1},{1,0},{2,3},{3,2},{4,5},{5,4},{6,7},{7,6},{8,9},{9,8},{10,11... | collective-permute-start | bytes 1572872 | tf_op jit(solution)/shard_map/ppermute | solution.py:123
  38.2 1.0 %copy-start.1 = (bf16[4,256,256]{2,1,0:T(8,128)(2,1)S(1)}, bf16[4,256,256]{2,1,0:T(8,128)(2,1)}, u32[]{:S(2)}) copy-start(bf16[4,256,256]{2,1,0:T(8,128)(2,1)} %refs_0_) | copy-start | bytes 1572868

commit v7 on v5

--- a/solution.py
+++ b/solution.py
@@ -10,6 +10,7 @@
 AXES = (8, 4, 2, 4, 2)
 NAMES = ("z", "x", "half", "y", "core")
 GROUP = 4
+PARTS = 2
 
 PLACES = ((0, 1, 0), (1, 4, 2), (-1, 5, 3), (2, 7, 6))
 
@@ -105,8 +106,7 @@
     term_dev = left_ops.shape[0]
     n_z, n_x, halves, half_y, cores = (lax.axis_size(name) for name in NAMES)
     n_ops, n_y = n_z * n_x, halves * half_y
-    targets = halves * sec_dev
-    pairs = term_dev * targets
+    part = sec_dev // PARTS
     band = tile // n_ops
     ops_index = lax.axis_index("z") * n_x + lax.axis_index("x")
     core, half = lax.axis_index("core"), lax.axis_index("half")
@@ -139,8 +139,9 @@
     codes = jnp.concatenate(
         [jnp.where(half == 0, code, other), jnp.where(half == 0, other, code)], axis=1
     )
-    places = places_of(codes, sec_dev, core, ring, n_y).reshape(pairs)
-    listed = sorted_pairs(places, jnp.repeat(coef, targets))
+    places = places_of(codes, sec_dev, core, ring, n_y).reshape(term_dev, halves, PARTS, part)
+    weights = jnp.repeat(coef, halves * part)
+    listed = [sorted_pairs(places[:, :, p].reshape(-1), weights) for p in range(PARTS)]
 
     theirs = [from_core(block) for block in [psi, *near]]
     theirs, far, listed = lax.optimization_barrier((theirs[::-1], far, listed))
@@ -150,29 +151,33 @@
     for (_, other_place, own), my_block, their_block in zip(PLACES, [psi, *near, far], theirs):
         blocks[own], blocks[other_place] = my_block, their_block
 
-    partial_sum = pl.pallas_call(
-        terms_kernel,
-        out_shape=jax.ShapeDtypeStruct((n_x, n_z, targets * band, tile), jnp.bfloat16),
-        in_specs=[smem] * 2 + [anywhere] * (2 + len(blocks)),
-        out_specs=vmem,
-        scratch_shapes=[
-            pltpu.VMEM(left_ops.shape, left_ops.dtype),
-            pltpu.VMEM(right_ops.shape, right_ops.dtype),
-            pltpu.VMEM((len(blocks) * sec_dev, tile, tile), psi.dtype),
-            pltpu.VMEM((targets, tile, tile), jnp.float32),
-            pltpu.SemaphoreType.DMA((len(blocks) + 2,)),
-        ],
-        compiler_params=pltpu.CompilerParams(vmem_limit_bytes=48 * 2**20),
-        name="terms",
-    )(*listed, left_ops, right_ops, *blocks)
+    def sums_of(part_list):
+        return pl.pallas_call(
+            terms_kernel,
+            out_shape=jax.ShapeDtypeStruct((n_x, n_z, halves * part * band, tile), jnp.bfloat16),
+            in_specs=[smem] * 2 + [anywhere] * (2 + len(blocks)),
+            out_specs=vmem,
+            scratch_shapes=[
+                pltpu.VMEM(left_ops.shape, left_ops.dtype),
+                pltpu.VMEM(right_ops.shape, right_ops.dtype),
+                pltpu.VMEM((len(blocks) * sec_dev, tile, tile), psi.dtype),
+                pltpu.VMEM((halves * part, tile, tile), jnp.float32),
+                pltpu.SemaphoreType.DMA((len(blocks) + 2,)),
+            ],
+            compiler_params=pltpu.CompilerParams(vmem_limit_bytes=48 * 2**20),
+            name="terms",
+        )(*part_list, left_ops, right_ops, *blocks)
 
-    bands = lax.all_to_all(partial_sum, "x", 0, 0, tiled=True)
-    bands = lax.optimization_barrier(jnp.sum(bands.astype(jnp.float32), axis=0))
-    bands = bands.astype(partial_sum.dtype)
-    bands = bands.reshape(n_z * halves, sec_dev * band, tile)
-    bands = lax.all_to_all(bands, ("z", "half"), 0, 0, tiled=True)
-    summed = jnp.sum(bands.astype(jnp.float32), axis=0).reshape(sec_dev, band, tile)
-    return local_part + summed
+    sums = [sums_of(part_list) for part_list in listed]
+    along_x = [lax.all_to_all(part_sums, "x", 0, 0, tiled=True) for part_sums in sums]
+    along_x[0], _ = lax.optimization_barrier((along_x[0], sums[-1]))
+    done = []
+    for bands in along_x:
+        bands = lax.optimization_barrier(jnp.sum(bands.astype(jnp.float32), axis=0))
+        bands = bands.astype(jnp.bfloat16).reshape(n_z * halves, part * band, tile)
+        bands = lax.all_to_all(bands, ("z", "half"), 0, 0, tiled=True)
+        done.append(jnp.sum(bands.astype(jnp.float32), axis=0).reshape(part, band, tile))
+    return local_part + jnp.concatenate(done, axis=0)
 
 
 def solution(mesh):

time: 89.6 us -> 114 us (1.27)
  blocking collectives: 45.2 us -> 0 us
  waiting for transfers between devices: 6.68 us -> 40.6 us
  starting transfers between devices: 24.7 us -> 48.3 us
  local copies, waits for them, and re-layouts: 2.02 us -> 9.39 us
  other arithmetic: 1.97 us -> 4.5 us
  Pallas kernels: 5.86 us -> 8.11 us
    all_to_all x2 -> x0, blocking collectives: 45.2 us -> none  [the longest x1 27.7 us: per_device(): bands = lax.all_to_all(bands, ('z', 'half'), 0, 0, tiled=True)]
    all_to_all x0 -> x4, waiting for transfers between devices: none -> 34 us  [the longest x2 25.2 us: per_device(): bands = lax.all_to_all(bands, ('z', 'half'), 0, 0, tiled=True)]
    all_to_all x0 -> x4, starting transfers between devices: none -> 23.6 us  [the longest x2 15.2 us: per_device(): bands = lax.all_to_all(bands, ('z', 'half'), 0, 0, tiled=True)]
    unnamed x4 -> x22, local copies, waits for them, and re-layouts: 1.05 us -> 8.15 us
    reduce_sum x1 -> x2, other arithmetic: 0.15 us -> 2.51 us  [per_device(): bands = lax.optimization_barrier(jnp.sum(bands.astype(jnp.float32), axis=0))]
    pallas_call x1 -> x2, Pallas kernels: 5.86 us -> 8.11 us  [sums_of(): pl.pallas_call(terms_kernel, out_shape=jax.ShapeDtypeStruct((n_x, n_z, ha...]
  transfers between devices with their start and end apart: 8 -> 12, of which waited for: 3 -> 7; matrix products, arithmetic and copies ran while one was open for 5% -> 7% of each run, Pallas kernels for 0% -> 4%
where the time goes in v7:
time: 114 us
  starting transfers between devices  48.3 us (42%)
  waiting for transfers between devices  40.6 us (36%)
  local copies, waits for them, and re-layouts  9.39 us (8%)
  Pallas kernels  8.11 us (7%)
  other arithmetic  4.5 us (4%)
  matrix products  2.46 us (2%)
    all_to_all x2, waiting for transfers between devices, per_device(): bands = lax.all_to_all(bands, ('z', 'half'), 0, 0, tiled=True)  25.2 us
    ppermute x4, starting transfers between devices, from_y(): return lax.ppermute(value, ('half', 'y', 'core'), route)  16.5 us
    all_to_all x2, starting transfers between devices, per_device(): bands = lax.all_to_all(bands, ('z', 'half'), 0, 0, tiled=True)  15.2 us
    all_to_all x2, waiting for transfers between devices, per_device(): lax.all_to_all(part_sums, 'x', 0, 0, tiled=True)  8.79 us
    all_to_all x2, starting transfers between devices, per_device(): lax.all_to_all(part_sums, 'x', 0, 0, tiled=True)  8.36 us
    ppermute x4, starting transfers between devices, from_core(): return lax.ppermute(value, 'core', [(0, 1), (1, 0)])  8.28 us
    unnamed x22, local copies, waits for them, and re-layouts  8.15 us
    pallas_call x2, Pallas kernels, sums_of(): pl.pallas_call(terms_kernel, out_shape=jax.ShapeDtypeStruct((n_x, n_z, ha...  8.11 us
  transfers between devices with their start and end apart: 12, of which 7 were waited for; matrix products, arithmetic and copies ran while one was open for 7% of the time, Pallas kernels for 4%

profile of v7, /device:TPU:8, one launch (start us, length us, event | category | flops | bytes accessed | tf_op | source)
XLA Modules:
  0.0 113.6 jit_solution(12616684907293512050)
XLA Ops:
  0.0 7.9 %collective-permute-start.1 = (bf16[4,256,256]{2,1,0:T(8,128)(2,1)}, bf16[4,256,256]{2,1,0:T(8,128)(2,1)S(1)}, u32[]{:S(2)}, u32[]{:S(2)}) collective-permute-start(bf16[4,256,256]{2,1,0:T(8,128)(2,1)} %refs_0_.1), channel_id=1, source_target_pairs={{2,0},{15,1},{4,2},{1,3},{6,4},{3,5},{8,6},{5,7},{10,8},{7,9},{12,... | collective-permute-start | bytes 1572872 | tf_op jit(solution)/shard_map/ppermute | solution.py:120
  7.9 1.9 %collective-permute-start = (bf16[4,256,256]{2,1,0:T(8,128)(2,1)}, bf16[4,256,256]{2,1,0:T(8,128)(2,1)S(1)}, u32[]{:S(2)}, u32[]{:S(2)}) collective-permute-start(bf16[4,256,256]{2,1,0:T(8,128)(2,1)} %refs_0_.1), channel_id=1, source_target_pairs={{14,0},{3,1},{0,2},{5,3},{2,4},{7,5},{4,6},{9,7},{6,8},{11,9},{8,1... | collective-permute-start | bytes 1572872 | tf_op jit(solution)/shard_map/ppermute | solution.py:120
  9.8 0.7 compare_select_fusion.15
  10.5 3.0 %collective-permute-start.2 = (s32[16,4]{0,1:T(4,128)S(1)}, s32[16,4]{0,1:T(4,128)S(1)}, u32[]{:S(2)}, u32[]{:S(2)}) collective-permute-start(s32[16,4]{0,1:T(4,128)S(1)} %compare_select_fusion.15), channel_id=1, source_target_pairs={{8,0},{9,1},{10,2},{11,3},{12,4},{13,5},{14,6},{15,7},{0,8},{1,9},... | collective-permute-start | bytes 776 | tf_op jit(solution)/shard_map/ppermute | solution.py:120
  13.5 1.2 %fusion.1 = f32[4,8,256]{2,1,0:T(8,128)S(1)} fusion(bf16[4,256,256]{2,1,0:T(8,128)(2,1)} %refs_0_.1, bf16[4,256,256]{2,1,0:T(8,128)(2,1)S(1)} %copy-done, s32[]{:T(128)S(6)} %select_n.121), kind=kOutput, calls=%fused_computation.15 | convolution fusion | flops 4194304 | bytes 573444 | tf_op jit(solution)/shard_map/tij,tjl->til/dot_general | solution.py:130
  14.8 1.2 %convolution_add_fusion = f32[4,8,256]{2,1,0:T(8,128)S(1)} fusion(f32[4,8,256]{2,1,0:T(8,128)S(1)} %fusion.1, bf16[4,256,256]{2,1,0:T(8,128)(2,1)} %param.15, bf16[4,256,256]{2,1,0:T(8,128)(2,1)} %refs_0_.1, s32[]{:T(128)S(6)} %select_n.121), kind=kOutput, calls=%fused_computation | convolution fusion | flops 4202496 | bytes 606212 | tf_op jit(solution)/shard_map/tij,tjl->til/dot_general | solution.py:131
  16.0 0.7 broadcast_in_dim.74
  16.7 0.1 broadcast_in_dim.75
  16.8 3.3 %collective-permute-done.2 = s32[16,4]{0,1:T(4,128)S(1)} collective-permute-done((s32[16,4]{0,1:T(4,128)S(1)}, s32[16,4]{0,1:T(4,128)S(1)}, u32[]{:S(2)}, u32[]{:S(2)}) %collective-permute-start.2) | collective-permute-done | bytes 288 | tf_op jit(solution)/shard_map/ppermute | solution.py:120
  20.1 0.0 collective-permute-done.refs_3_
  20.1 3.7 %collective-permute-start.6 = (bf16[4,256,256]{2,1,0:T(8,128)(2,1)S(1)}, bf16[4,256,256]{2,1,0:T(8,128)(2,1)S(1)}, u32[]{:S(2)}, u32[]{:S(2)}) collective-permute-start(bf16[4,256,256]{2,1,0:T(8,128)(2,1)S(1)} %collective-permute-done.1.refs_2_), channel_id=1, source_target_pairs={{2,0},{15,1},{4,2},{1,3},{6,4},{3,5},{8,6},{5,7},{10,8},{7,9},{12,... | collective-permute-start | bytes 1572872 | tf_op jit(solution)/shard_map/ppermute | solution.py:120
  23.8 1.9 %collective-permute-start.4 = (bf16[4,256,256]{2,1,0:T(8,128)(2,1)S(1)}, bf16[4,256,256]{2,1,0:T(8,128)(2,1)S(1)}, u32[]{:S(2)}, u32[]{:S(2)}) collective-permute-start(bf16[4,256,256]{2,1,0:T(8,128)(2,1)S(1)} %collective-permute-done.1.refs_2_), channel_id=1, source_target_pairs={{0,1},{1,0},{2,3},{3,2},{4,5},{5,4},{6,7},{7,6},{8,9},{9,8},{10,11... | collective-permute-start | bytes 1572872 | tf_op jit(solution)/shard_map/ppermute | solution.py:123
  25.7 0.1 and_select_fusion.1
  25.8 0.1 copy.14
  25.9 0.1 mul.55
  26.1 0.1 copy.13
  26.2 0.1 mul.53
  26.3 2.4 %collective-permute-start.3 = (bf16[4,256,256]{2,1,0:T(8,128)(2,1)S(1)}, bf16[4,256,256]{2,1,0:T(8,128)(2,1)S(1)}, u32[]{:S(2)}, u32[]{:S(2)}) collective-permute-start(bf16[4,256,256]{2,1,0:T(8,128)(2,1)S(1)} %collective-permute-done.refs_3_), channel_id=1, source_target_pairs={{0,1},{1,0},{2,3},{3,2},{4,5},{5,4},{6,7},{7,6},{8,9},{9,8},{10,11... | collective-permute-start | bytes 1572872 | tf_op jit(solution)/shard_map/ppermute | solution.py:123
  28.7 1.9 %collective-permute-start.5 = (bf16[4,256,256]{2,1,0:T(8,128)(2,1)}, bf16[4,256,256]{2,1,0:T(8,128)(2,1)S(1)}, u32[]{:S(2)}, u32[]{:S(2)}) collective-permute-start(bf16[4,256,256]{2,1,0:T(8,128)(2,1)} %refs_0_.1), channel_id=1, source_target_pairs={{0,1},{1,0},{2,3},{3,2},{4,5},{5,4},{6,7},{7,6},{8,9},{9,8},{10,11... | collective-permute-start | bytes 1572872 | tf_op jit(solution)/shard_map/ppermute | solution.py:123
  30.6 0.2 convert_reduce_fusion.4
  30.8 0.1 select_reduce_fusion.1.list_ref
  30.9 0.1 select_reduce_fusion.3.list_ref
  31.0 0.1 select_reduce_fusion
  31.2 1.5 %collective-permute-done.5.refs_1_ = bf16[4,256,256]{2,1,0:T(8,128)(2,1)S(1)} collective-permute-done((bf16[4,256,256]{2,1,0:T(8,128)(2,1)}, bf16[4,256,256]{2,1,0:T(8,128)(2,1)S(1)}, u32[]{:S(2)}, u32[]{:S(2)}) %collective-permute-start.5) | collective-permute-done | bytes 524320 | tf_op jit(solution)/shard_map/ppermute | solution.py:123
  32.7 2.0 %collective-permute-start.7 = (bf16[4,256,256]{2,1,0:T(8,128)(2,1)S(1)}, bf16[4,256,256]{2,1,0:T(8,128)(2,1)S(1)}, u32[]{:S(2)}, u32[]{:S(2)}) collective-permute-start(bf16[4,256,256]{2,1,0:T(8,128)(2,1)S(1)} %collective-permute-done.6.refs_6_), channel_id=1, source_target_pairs={{0,1},{1,0},{2,3},{3,2},{4,5},{5,4},{6,7},{7,6},{8,9},{9,8},{10,11... | collective-permute-start | bytes 1572872 | tf_op jit(solution)/shard_map/ppermute | solution.py:123
  34.8 1.8 %collective-permute-done.7.refs_7_ = bf16[4,256,256]{2,1,0:T(8,128)(2,1)S(1)} collective-permute-done((bf16[4,256,256]{2,1,0:T(8,128)(2,1)S(1)}, bf16[4,256,256]{2,1,0:T(8,128)(2,1)S(1)}, u32[]{:S(2)}, u32[]{:S(2)}) %collective-permute-start.7) | collective-permute-done | bytes 524320 | tf_op jit(solution)/shard_map/ppermute | solution.py:123
  36.5 1.0 copy-done.1
  37.6 4.1 %terms.2 = bf16[4,8,32,256]{3,2,1,0:T(8,128)(2,1)S(1)} custom-call(s32[64]{0:T(128)S(1)} %select_reduce_fusion.3.list_ref, f32[64]{0:T(128)S(1)} %get-tuple-element.25.weight_ref, bf16[16,256,256]{2,1,0:T(8,128)(2,1)} %left_hbm.3, bf16[16,256,256]{2,1,0:T(8,128)(2,1)} %right_hbm.3, bf16[4,256,256]{2,1,0:T(8,128)(2,1)S(1)} %copy-done.1, ...), custom_call_target="tpu_custom_call" | custom-call | tf_op jit(solution)/shard_map/terms/pallas_call | solution.py:155
  41.6 0.8 copy-done.3
  42.4 0.8 copy-done.5
  43.2 0.8 copy-done.7
  44.0 0.8 copy-done.10
  44.8 4.5 %all-to-all-start = ((bf16[4,8,32,256]{3,2,1,0:T(8,128)(2,1)}), bf16[4,8,32,256]{3,2,1,0:T(8,128)(2,1)}, u32[]{:S(2)}, u32[]{:S(2)}) async-start(bf16[4,8,32,256]{3,2,1,0:T(8,128)(2,1)} %copy-done.10), calls=%async_computation | async-start | bytes 1048576 | tf_op jit(solution)/shard_map/all_to_all | solution.py:172
  49.3 1.0 copy-done.4
  50.3 1.0 copy-done.6
  51.4 1.0 copy-done.8
  52.4 4.1 %terms.3 = bf16[4,8,32,256]{3,2,1,0:T(8,128)(2,1)S(1)} custom-call(s32[64]{0:T(128)S(1)} %select_reduce_fusion.1.list_ref, f32[64]{0:T(128)S(1)} %get-tuple-element.31.weight_ref, bf16[16,256,256]{2,1,0:T(8,128)(2,1)} %left_hbm.3, bf16[16,256,256]{2,1,0:T(8,128)(2,1)} %right_hbm.3, bf16[4,256,256]{2,1,0:T(8,128)(2,1)S(1)} %copy-done.2, ...), custom_call_target="tpu_custom_call" | custom-call | tf_op jit(solution)/shard_map/terms/pallas_call | solution.py:155
  56.5 0.8 copy-done.9
  57.3 1.8 %all-to-all-done = bf16[4,8,32,256]{3,2,1,0:T(8,128)(2,1)} async-done(((bf16[4,8,32,256]{3,2,1,0:T(8,128)(2,1)}), bf16[4,8,32,256]{3,2,1,0:T(8,128)(2,1)}, u32[]{:S(2)}, u32[]{:S(2)}) %all-to-all-start) | async-done | bytes 524320 | tf_op jit(solution)/shard_map/all_to_all | solution.py:172
  59.0 3.9 %all-to-all-start.2 = ((bf16[4,8,32,256]{3,2,1,0:T(8,128)(2,1)}), bf16[4,8,32,256]{3,2,1,0:T(8,128)(2,1)S(1)}, u32[]{:S(2)}, u32[]{:S(2)}) async-start(bf16[4,8,32,256]{3,2,1,0:T(8,128)(2,1)} %copy-done.9), calls=%async_computation.2 | async-start | bytes 1048576 | tf_op jit(solution)/shard_map/all_to_all | solution.py:172
  62.9 1.8 %convert_reduce_fusion.1 = bf16[8,32,256]{2,1,0:T(8,128)(2,1)} fusion(bf16[4,8,32,256]{3,2,1,0:T(8,128)(2,1)} %all-to-all-done), kind=kLoop, calls=%fused_computation.2 | loop fusion | flops 458752 | bytes 655360 | tf_op jit(solution)/shard_map/reduce_sum | solution.py:176
  64.8 7.0 %all-to-all-done.2 = bf16[4,8,32,256]{3,2,1,0:T(8,128)(2,1)S(1)} async-done(((bf16[4,8,32,256]{3,2,1,0:T(8,128)(2,1)}), bf16[4,8,32,256]{3,2,1,0:T(8,128)(2,1)S(1)}, u32[]{:S(2)}, u32[]{:S(2)}) %all-to-all-start.2) | async-done | bytes 524320 | tf_op jit(solution)/shard_map/all_to_all | solution.py:172
  71.8 11.7 %all-to-all-start.1 = ((bf16[16,16,256]{2,1,0:T(8,128)(2,1)}), bf16[16,16,256]{2,1,0:T(8,128)(2,1)S(1)}, u32[]{:S(2)}, u32[]{:S(2)}) async-start(bf16[16,16,256]{2,1,0:T(8,128)(2,1)} %bitcast.2), calls=%async_computation.1 | async-start | bytes 262144 | tf_op jit(solution)/shard_map/all_to_all | solution.py:178
  83.5 0.7 convert_reduce_fusion
  84.2 12.3 %all-to-all-done.1 = bf16[16,16,256]{2,1,0:T(8,128)(2,1)S(1)} async-done(((bf16[16,16,256]{2,1,0:T(8,128)(2,1)}), bf16[16,16,256]{2,1,0:T(8,128)(2,1)S(1)}, u32[]{:S(2)}, u32[]{:S(2)}) %all-to-all-start.1) | async-done | bytes 131104 | tf_op jit(solution)/shard_map/all_to_all | solution.py:178
  96.5 3.5 %all-to-all-start.3 = ((bf16[16,16,256]{2,1,0:T(8,128)(2,1)}), bf16[16,16,256]{2,1,0:T(8,128)(2,1)S(1)}, u32[]{:S(2)}, u32[]{:S(2)}) async-start(bf16[16,16,256]{2,1,0:T(8,128)(2,1)} %bitcast.4), calls=%async_computation.3 | async-start | bytes 262144 | tf_op jit(solution)/shard_map/all_to_all | solution.py:178
  100.0 12.9 %all-to-all-done.3 = bf16[16,16,256]{2,1,0:T(8,128)(2,1)S(1)} async-done(((bf16[16,16,256]{2,1,0:T(8,128)(2,1)}), bf16[16,16,256]{2,1,0:T(8,128)(2,1)S(1)}, u32[]{:S(2)}, u32[]{:S(2)}) %all-to-all-start.3) | async-done | bytes 131104 | tf_op jit(solution)/shard_map/all_to_all | solution.py:178
  112.9 0.6 maximum_add_fusion
  (23 shorter events, 0.1 us)
Async XLA Ops:
  0.0 13.5 %copy-start = (bf16[4,256,256]{2,1,0:T(8,128)(2,1)S(1)}, bf16[4,256,256]{2,1,0:T(8,128)(2,1)}, u32[]{:S(2)}) copy-start(bf16[4,256,256]{2,1,0:T(8,128)(2,1)} %param.14) | copy-start | bytes 1572868
  0.0 20.1 %collective-permute-start.1 = (bf16[4,256,256]{2,1,0:T(8,128)(2,1)}, bf16[4,256,256]{2,1,0:T(8,128)(2,1)S(1)}, u32[]{:S(2)}, u32[]{:S(2)}) collective-permute-start(bf16[4,256,256]{2,1,0:T(8,128)(2,1)} %refs_0_.1), channel_id=1, source_target_pairs={{2,0},{15,1},{4,2},{1,3},{6,4},{3,5},{8,6},{5,7},{10,8},{7,9},{12,... | collective-permute-start | bytes 1572872 | tf_op jit(solution)/shard_map/ppermute | solution.py:120
  7.9 12.3 %collective-permute-start = (bf16[4,256,256]{2,1,0:T(8,128)(2,1)}, bf16[4,256,256]{2,1,0:T(8,128)(2,1)S(1)}, u32[]{:S(2)}, u32[]{:S(2)}) collective-permute-start(bf16[4,256,256]{2,1,0:T(8,128)(2,1)} %refs_0_.1), channel_id=1, source_target_pairs={{14,0},{3,1},{0,2},{5,3},{2,4},{7,5},{4,6},{9,7},{6,8},{11,9},{8,1... | collective-permute-start | bytes 1572872 | tf_op jit(solution)/shard_map/ppermute | solution.py:120
  10.5 9.6 %collective-permute-start.2 = (s32[16,4]{0,1:T(4,128)S(1)}, s32[16,4]{0,1:T(4,128)S(1)}, u32[]{:S(2)}, u32[]{:S(2)}) collective-permute-start(s32[16,4]{0,1:T(4,128)S(1)} %compare_select_fusion.15), channel_id=1, source_target_pairs={{8,0},{9,1},{10,2},{11,3},{12,4},{13,5},{14,6},{15,7},{0,8},{1,9},... | collective-permute-start | bytes 776 | tf_op jit(solution)/shard_map/ppermute | solution.py:120
  20.1 12.6 %collective-permute-start.6 = (bf16[4,256,256]{2,1,0:T(8,128)(2,1)S(1)}, bf16[4,256,256]{2,1,0:T(8,128)(2,1)S(1)}, u32[]{:S(2)}, u32[]{:S(2)}) collective-permute-start(bf16[4,256,256]{2,1,0:T(8,128)(2,1)S(1)} %collective-permute-done.1.refs_2_), channel_id=1, source_target_pairs={{2,0},{15,1},{4,2},{1,3},{6,4},{3,5},{8,6},{5,7},{10,8},{7,9},{12,... | collective-permute-start | bytes 1572872 | tf_op jit(solution)/shard_map/ppermute | solution.py:120
  23.8 8.9 %collective-permute-start.4 = (bf16[4,256,256]{2,1,0:T(8,128)(2,1)S(1)}, bf16[4,256,256]{2,1,0:T(8,128)(2,1)S(1)}, u32[]{:S(2)}, u32[]{:S(2)}) collective-permute-start(bf16[4,256,256]{2,1,0:T(8,128)(2,1)S(1)} %collective-permute-done.1.refs_2_), channel_id=1, source_target_pairs={{0,1},{1,0},{2,3},{3,2},{4,5},{5,4},{6,7},{7,6},{8,9},{9,8},{10,11... | collective-permute-start | bytes 1572872 | tf_op jit(solution)/shard_map/ppermute | solution.py:123
  26.3 4.9 %collective-permute-start.3 = (bf16[4,256,256]{2,1,0:T(8,128)(2,1)S(1)}, bf16[4,256,256]{2,1,0:T(8,128)(2,1)S(1)}, u32[]{:S(2)}, u32[]{:S(2)}) collective-permute-start(bf16[4,256,256]{2,1,0:T(8,128)(2,1)S(1)} %collective-permute-done.refs_3_), channel_id=1, source_target_pairs={{0,1},{1,0},{2,3},{3,2},{4,5},{5,4},{6,7},{7,6},{8,9},{9,8},{10,11... | collective-permute-start | bytes 1572872 | tf_op jit(solution)/shard_map/ppermute | solution.py:123
  28.7 4.0 %collective-permute-start.5 = (bf16[4,256,256]{2,1,0:T(8,128)(2,1)}, bf16[4,256,256]{2,1,0:T(8,128)(2,1)S(1)}, u32[]{:S(2)}, u32[]{:S(2)}) collective-permute-start(bf16[4,256,256]{2,1,0:T(8,128)(2,1)} %refs_0_.1), channel_id=1, source_target_pairs={{0,1},{1,0},{2,3},{3,2},{4,5},{5,4},{6,7},{7,6},{8,9},{9,8},{10,11... | collective-permute-start | bytes 1572872 | tf_op jit(solution)/shard_map/ppermute | solution.py:123
  32.7 3.8 %collective-permute-start.7 = (bf16[4,256,256]{2,1,0:T(8,128)(2,1)S(1)}, bf16[4,256,256]{2,1,0:T(8,128)(2,1)S(1)}, u32[]{:S(2)}, u32[]{:S(2)}) collective-permute-start(bf16[4,256,256]{2,1,0:T(8,128)(2,1)S(1)} %collective-permute-done.6.refs_6_), channel_id=1, source_target_pairs={{0,1},{1,0},{2,3},{3,2},{4,5},{5,4},{6,7},{7,6},{8,9},{9,8},{10,11... | collective-permute-start | bytes 1572872 | tf_op jit(solution)/shard_map/ppermute | solution.py:123
  36.5 1.0 copy-start.1
  37.6 11.7 %copy-start.2 = (bf16[4,256,256]{2,1,0:T(8,128)(2,1)S(1)}, bf16[4,256,256]{2,1,0:T(8,128)(2,1)}, u32[]{:S(2)}) copy-start(bf16[4,256,256]{2,1,0:T(8,128)(2,1)} %refs_0_.1) | copy-start | bytes 1572868
  41.6 0.8 copy-start.3
  42.4 0.8 copy-start.5
  43.2 0.8 copy-start.7
  44.0 0.8 copy-start.10
  44.8 14.2 %all-to-all-start = ((bf16[4,8,32,256]{3,2,1,0:T(8,128)(2,1)}), bf16[4,8,32,256]{3,2,1,0:T(8,128)(2,1)}, u32[]{:S(2)}, u32[]{:S(2)}) async-start(bf16[4,8,32,256]{3,2,1,0:T(8,128)(2,1)} %copy-done.10), calls=%async_computation | async-start | bytes 1048576 | tf_op jit(solution)/shard_map/all_to_all | solution.py:172
  49.3 1.0 copy-start.4
  50.3 1.0 copy-start.6
  51.4 1.0 copy-start.8
  56.5 0.8 copy-start.9
  59.0 12.7 %all-to-all-start.2 = ((bf16[4,8,32,256]{3,2,1,0:T(8,128)(2,1)}), bf16[4,8,32,256]{3,2,1,0:T(8,128)(2,1)S(1)}, u32[]{:S(2)}, u32[]{:S(2)}) async-start(bf16[4,8,32,256]{3,2,1,0:T(8,128)(2,1)} %copy-done.9), calls=%async_computation.2 | async-start | bytes 1048576 | tf_op jit(solution)/shard_map/all_to_all | solution.py:172
  71.8 24.7 %all-to-all-start.1 = ((bf16[16,16,256]{2,1,0:T(8,128)(2,1)}), bf16[16,16,256]{2,1,0:T(8,128)(2,1)S(1)}, u32[]{:S(2)}, u32[]{:S(2)}) async-start(bf16[16,16,256]{2,1,0:T(8,128)(2,1)} %bitcast.2), calls=%async_computation.1 | async-start | bytes 262144 | tf_op jit(solution)/shard_map/all_to_all | solution.py:178
  96.5 16.5 %all-to-all-start.3 = ((bf16[16,16,256]{2,1,0:T(8,128)(2,1)}), bf16[16,16,256]{2,1,0:T(8,128)(2,1)S(1)}, u32[]{:S(2)}, u32[]{:S(2)}) async-start(bf16[16,16,256]{2,1,0:T(8,128)(2,1)} %bitcast.4), calls=%async_computation.3 | async-start | bytes 262144 | tf_op jit(solution)/shard_map/all_to_all | solution.py:178

commit v8 on v5

--- a/solution.py
+++ b/solution.py
@@ -123,6 +123,7 @@
         return lax.ppermute(value, "core", [(0, 1), (1, 0)])
 
     near = [from_y(psi, 1), from_y(psi, -1)]
+    far = from_y(psi, 2)
     code = jnp.where(active != 0, source, -1)
     other = from_y(code, n_y // 2)
     local_rows = lax.dynamic_slice_in_dim(psi, ops_index * band, band, 1)
@@ -134,7 +135,6 @@
 
     near, other, local_part, psi = lax.optimization_barrier((near[::-1], other, local_part, psi))
     near = near[::-1]
-    far = from_y(near[0], 1)
 
     codes = jnp.concatenate(
         [jnp.where(half == 0, code, other), jnp.where(half == 0, other, code)], axis=1

time: 89.6 us -> 97.5 us (1.088)
  the two profiles are of different devices: /device:TPU:8 before, /device:TPU:16 now
where the time goes in v8:
time: 97.5 us; the launch traced here: 97 us
  blocking collectives  49.5 us (51%)
  starting transfers between devices  25 us (26%)
  waiting for transfers between devices  10.6 us (11%)
  Pallas kernels  5.27 us (5%)
  matrix products  2.46 us (3%)
  local copies, waits for them, and re-layouts  2.03 us (2%)
  other arithmetic  1.97 us (2%)
    all_to_all x1, blocking collectives, per_device(): bands = lax.all_to_all(bands, ('z', 'half'), 0, 0, tiled=True)  29.4 us
    all_to_all x1, blocking collectives, per_device(): bands = lax.all_to_all(partial_sum, 'x', 0, 0, tiled=True)  20.1 us
    ppermute x4, starting transfers between devices, from_y(): return lax.ppermute(value, ('half', 'y', 'core'), route)  15.9 us
    ppermute x4, starting transfers between devices, from_core(): return lax.ppermute(value, 'core', [(0, 1), (1, 0)])  9.1 us
    ppermute x4, waiting for transfers between devices, from_y(): return lax.ppermute(value, ('half', 'y', 'core'), route)  7.79 us
    pallas_call x1, Pallas kernels, per_device(): pl.pallas_call(terms_kernel, out_shape=jax.ShapeDtypeStruct((n_x, n_z, ta...  5.27 us
    ppermute x4, waiting for transfers between devices, from_core(): return lax.ppermute(value, 'core', [(0, 1), (1, 0)])  2.76 us
  transfers between devices with their start and end apart: 8, of which 4 were waited for; matrix products, arithmetic and copies ran while one was open for 5% of the time, Pallas kernels for 0%

profile of v8, /device:TPU:16, one launch (start us, length us, event | category | flops | bytes accessed | tf_op | source)
XLA Modules:
  0.0 97.0 jit_solution(4259860368043490249)
XLA Ops:
  0.0 0.0 copy-start
  0.0 2.5 %collective-permute-start.1 = (bf16[4,256,256]{2,1,0:T(8,128)(2,1)}, bf16[4,256,256]{2,1,0:T(8,128)(2,1)S(1)}, u32[]{:S(2)}, u32[]{:S(2)}) collective-permute-start(bf16[4,256,256]{2,1,0:T(8,128)(2,1)} %refs_0_), channel_id=1, source_target_pairs={{2,0},{15,1},{4,2},{1,3},{6,4},{3,5},{8,6},{5,7},{10,8},{7,9},{12,... | collective-permute-start | bytes 1572872 | tf_op jit(solution)/shard_map/ppermute | solution.py:120
  2.5 3.5 %collective-permute-start = (bf16[4,256,256]{2,1,0:T(8,128)(2,1)}, bf16[4,256,256]{2,1,0:T(8,128)(2,1)S(1)}, u32[]{:S(2)}, u32[]{:S(2)}) collective-permute-start(bf16[4,256,256]{2,1,0:T(8,128)(2,1)} %refs_0_), channel_id=1, source_target_pairs={{14,0},{3,1},{0,2},{5,3},{2,4},{7,5},{4,6},{9,7},{6,8},{11,9},{8,1... | collective-permute-start | bytes 1572872 | tf_op jit(solution)/shard_map/ppermute | solution.py:120
  6.0 7.6 %collective-permute-start.6 = (bf16[4,256,256]{2,1,0:T(8,128)(2,1)}, bf16[4,256,256]{2,1,0:T(8,128)(2,1)S(1)}, u32[]{:S(2)}, u32[]{:S(2)}) collective-permute-start(bf16[4,256,256]{2,1,0:T(8,128)(2,1)} %refs_0_), channel_id=1, source_target_pairs={{4,0},{13,1},{6,2},{15,3},{8,4},{1,5},{10,6},{3,7},{12,8},{5,9},{1... | collective-permute-start | bytes 1572872 | tf_op jit(solution)/shard_map/ppermute | solution.py:120
  13.6 0.7 compare_select_fusion.15
  14.3 2.3 %collective-permute-start.2 = (s32[16,4]{0,1:T(4,128)S(1)}, s32[16,4]{0,1:T(4,128)S(1)}, u32[]{:S(2)}, u32[]{:S(2)}) collective-permute-start(s32[16,4]{0,1:T(4,128)S(1)} %compare_select_fusion.15), channel_id=1, source_target_pairs={{8,0},{9,1},{10,2},{11,3},{12,4},{13,5},{14,6},{15,7},{0,8},{1,9},... | collective-permute-start | bytes 776 | tf_op jit(solution)/shard_map/ppermute | solution.py:120
  16.7 0.0 copy-done
  16.7 1.2 %fusion.1 = f32[4,8,256]{2,1,0:T(8,128)S(1)} fusion(bf16[4,256,256]{2,1,0:T(8,128)(2,1)} %refs_0_, bf16[4,256,256]{2,1,0:T(8,128)(2,1)S(1)} %copy-done, s32[]{:T(128)S(6)} %select_n.259), kind=kOutput, calls=%fused_computation.9 | convolution fusion | flops 4194304 | bytes 573444 | tf_op jit(solution)/shard_map/tij,tjl->til/dot_general | solution.py:131
  17.9 1.2 %convolution_add_fusion = f32[4,8,256]{2,1,0:T(8,128)S(1)} fusion(f32[4,8,256]{2,1,0:T(8,128)S(1)} %fusion.1, bf16[4,256,256]{2,1,0:T(8,128)(2,1)} %param.15, bf16[4,256,256]{2,1,0:T(8,128)(2,1)} %refs_0_, s32[]{:T(128)S(6)} %select_n.259), kind=kOutput, calls=%fused_computation.1 | convolution fusion | flops 4202496 | bytes 606212 | tf_op jit(solution)/shard_map/tij,tjl->til/dot_general | solution.py:132
  19.2 0.7 broadcast_in_dim.61
  19.9 0.1 broadcast_in_dim.62
  20.0 7.0 %collective-permute-done.2 = s32[16,4]{0,1:T(4,128)S(1)} collective-permute-done((s32[16,4]{0,1:T(4,128)S(1)}, s32[16,4]{0,1:T(4,128)S(1)}, u32[]{:S(2)}, u32[]{:S(2)}) %collective-permute-start.2) | collective-permute-done | bytes 288 | tf_op jit(solution)/shard_map/ppermute | solution.py:120
  27.0 0.0 collective-permute-done.1.refs_2_
  27.0 0.8 collective-permute-done.refs_3_
  27.8 0.1 copy.11
  27.9 0.1 concatenate.6
  28.0 2.5 %collective-permute-start.3 = (bf16[4,256,256]{2,1,0:T(8,128)(2,1)S(1)}, bf16[4,256,256]{2,1,0:T(8,128)(2,1)S(1)}, u32[]{:S(2)}, u32[]{:S(2)}) collective-permute-start(bf16[4,256,256]{2,1,0:T(8,128)(2,1)S(1)} %collective-permute-done.refs_3_), channel_id=1, source_target_pairs={{0,1},{1,0},{2,3},{3,2},{4,5},{5,4},{6,7},{7,6},{8,9},{9,8},{10,11... | collective-permute-start | bytes 1572872 | tf_op jit(solution)/shard_map/ppermute | solution.py:123
  30.5 1.9 %collective-permute-start.4 = (bf16[4,256,256]{2,1,0:T(8,128)(2,1)S(1)}, bf16[4,256,256]{2,1,0:T(8,128)(2,1)S(1)}, u32[]{:S(2)}, u32[]{:S(2)}) collective-permute-start(bf16[4,256,256]{2,1,0:T(8,128)(2,1)S(1)} %collective-permute-done.1.refs_2_), channel_id=1, source_target_pairs={{0,1},{1,0},{2,3},{3,2},{4,5},{5,4},{6,7},{7,6},{8,9},{9,8},{10,11... | collective-permute-start | bytes 1572872 | tf_op jit(solution)/shard_map/ppermute | solution.py:123
  32.4 2.4 %collective-permute-start.5 = (bf16[4,256,256]{2,1,0:T(8,128)(2,1)}, bf16[4,256,256]{2,1,0:T(8,128)(2,1)S(1)}, u32[]{:S(2)}, u32[]{:S(2)}) collective-permute-start(bf16[4,256,256]{2,1,0:T(8,128)(2,1)} %refs_0_), channel_id=1, source_target_pairs={{0,1},{1,0},{2,3},{3,2},{4,5},{5,4},{6,7},{7,6},{8,9},{9,8},{10,11... | collective-permute-start | bytes 1572872 | tf_op jit(solution)/shard_map/ppermute | solution.py:123
  34.8 0.2 convert_reduce_fusion.2
  35.0 0.1 select_reduce_fusion.1.list_ref
  35.1 0.1 select_reduce_fusion.weight_ref
  35.3 0.0 collective-permute-done.6.refs_6_
  35.3 0.0 collective-permute-done.3.refs_5_
  35.3 0.0 collective-permute-done.4.refs_4_
  35.3 1.2 %collective-permute-done.5.refs_1_ = bf16[4,256,256]{2,1,0:T(8,128)(2,1)S(1)} collective-permute-done((bf16[4,256,256]{2,1,0:T(8,128)(2,1)}, bf16[4,256,256]{2,1,0:T(8,128)(2,1)S(1)}, u32[]{:S(2)}, u32[]{:S(2)}) %collective-permute-start.5) | collective-permute-done | bytes 524320 | tf_op jit(solution)/shard_map/ppermute | solution.py:123
  36.5 2.3 %collective-permute-start.7 = (bf16[4,256,256]{2,1,0:T(8,128)(2,1)S(1)}, bf16[4,256,256]{2,1,0:T(8,128)(2,1)S(1)}, u32[]{:S(2)}, u32[]{:S(2)}) collective-permute-start(bf16[4,256,256]{2,1,0:T(8,128)(2,1)S(1)} %collective-permute-done.6.refs_6_), channel_id=1, source_target_pairs={{0,1},{1,0},{2,3},{3,2},{4,5},{5,4},{6,7},{7,6},{8,9},{9,8},{10,11... | collective-permute-start | bytes 1572872 | tf_op jit(solution)/shard_map/ppermute | solution.py:123
  38.8 1.5 %collective-permute-done.7.refs_7_ = bf16[4,256,256]{2,1,0:T(8,128)(2,1)S(1)} collective-permute-done((bf16[4,256,256]{2,1,0:T(8,128)(2,1)S(1)}, bf16[4,256,256]{2,1,0:T(8,128)(2,1)S(1)}, u32[]{:S(2)}, u32[]{:S(2)}) %collective-permute-start.7) | collective-permute-done | bytes 524320 | tf_op jit(solution)/shard_map/ppermute | solution.py:123
  40.3 0.0 copy-start.1
  40.3 1.0 %copy-done.1 = bf16[4,256,256]{2,1,0:T(8,128)(2,1)S(1)} copy-done((bf16[4,256,256]{2,1,0:T(8,128)(2,1)S(1)}, bf16[4,256,256]{2,1,0:T(8,128)(2,1)}, u32[]{:S(2)}) %copy-start.1) | copy-done | bytes 524312
  41.4 5.3 %terms.1 = bf16[4,8,64,256]{3,2,1,0:T(8,128)(2,1)S(1)} custom-call(s32[128]{0:T(128)S(1)} %select_reduce_fusion.1.list_ref, f32[128]{0:T(128)S(1)} %select_reduce_fusion.weight_ref, bf16[16,256,256]{2,1,0:T(8,128)(2,1)} %left_hbm.1, bf16[16,256,256]{2,1,0:T(8,128)(2,1)} %right_hbm.1, bf16[4,256,256]{2,1,0:T(8,128)(2,1)S(1)} %copy-done.1, ...), custom_call_target="tpu_custom_call" | custom-call | tf_op jit(solution)/shard_map/terms/pallas_call | solution.py:153
  46.6 20.1 %all_to_all.10 = bf16[4,8,64,256]{3,2,1,0:T(8,128)(2,1)S(1)} all-to-all(bf16[4,8,64,256]{3,2,1,0:T(8,128)(2,1)S(1)} %terms.1), channel_id=1, replica_groups=mesh['z'=8,'x'=4,'half'=2,'y'=4,'core'=2] {'x'}, dimensions={0} | all-to-all | bytes 2097152 | tf_op jit(solution)/shard_map/all_to_all | solution.py:169
  66.8 0.2 convert_reduce_fusion
  66.9 29.4 %all_to_all.11 = bf16[16,32,256]{2,1,0:T(8,128)(2,1)S(1)} all-to-all(bf16[16,32,256]{2,1,0:T(8,128)(2,1)S(1)} %bitcast.5), channel_id=1, replica_groups=mesh['z'=8,'x'=4,'half'=2,'y'=4,'core'=2] {'z','half'}, dimensions={0} | all-to-all | bytes 524288 | tf_op jit(solution)/shard_map/all_to_all | solution.py:173
  96.4 0.6 bitcast_add_fusion
  (4 shorter events, 0.1 us)
Async XLA Ops:
  0.0 16.7 %copy-start = (bf16[4,256,256]{2,1,0:T(8,128)(2,1)S(1)}, bf16[4,256,256]{2,1,0:T(8,128)(2,1)}, u32[]{:S(2)}) copy-start(bf16[4,256,256]{2,1,0:T(8,128)(2,1)} %param.14) | copy-start | bytes 1572868
  0.0 27.0 %collective-permute-start.1 = (bf16[4,256,256]{2,1,0:T(8,128)(2,1)}, bf16[4,256,256]{2,1,0:T(8,128)(2,1)S(1)}, u32[]{:S(2)}, u32[]{:S(2)}) collective-permute-start(bf16[4,256,256]{2,1,0:T(8,128)(2,1)} %refs_0_), channel_id=1, source_target_pairs={{2,0},{15,1},{4,2},{1,3},{6,4},{3,5},{8,6},{5,7},{10,8},{7,9},{12,... | collective-permute-start | bytes 1572872 | tf_op jit(solution)/shard_map/ppermute | solution.py:120
  2.5 25.3 %collective-permute-start = (bf16[4,256,256]{2,1,0:T(8,128)(2,1)}, bf16[4,256,256]{2,1,0:T(8,128)(2,1)S(1)}, u32[]{:S(2)}, u32[]{:S(2)}) collective-permute-start(bf16[4,256,256]{2,1,0:T(8,128)(2,1)} %refs_0_), channel_id=1, source_target_pairs={{14,0},{3,1},{0,2},{5,3},{2,4},{7,5},{4,6},{9,7},{6,8},{11,9},{8,1... | collective-permute-start | bytes 1572872 | tf_op jit(solution)/shard_map/ppermute | solution.py:120
  6.0 29.3 %collective-permute-start.6 = (bf16[4,256,256]{2,1,0:T(8,128)(2,1)}, bf16[4,256,256]{2,1,0:T(8,128)(2,1)S(1)}, u32[]{:S(2)}, u32[]{:S(2)}) collective-permute-start(bf16[4,256,256]{2,1,0:T(8,128)(2,1)} %refs_0_), channel_id=1, source_target_pairs={{4,0},{13,1},{6,2},{15,3},{8,4},{1,5},{10,6},{3,7},{12,8},{5,9},{1... | collective-permute-start | bytes 1572872 | tf_op jit(solution)/shard_map/ppermute | solution.py:120
  14.3 12.7 %collective-permute-start.2 = (s32[16,4]{0,1:T(4,128)S(1)}, s32[16,4]{0,1:T(4,128)S(1)}, u32[]{:S(2)}, u32[]{:S(2)}) collective-permute-start(s32[16,4]{0,1:T(4,128)S(1)} %compare_select_fusion.15), channel_id=1, source_target_pairs={{8,0},{9,1},{10,2},{11,3},{12,4},{13,5},{14,6},{15,7},{0,8},{1,9},... | collective-permute-start | bytes 776 | tf_op jit(solution)/shard_map/ppermute | solution.py:120
  28.0 7.3 %collective-permute-start.3 = (bf16[4,256,256]{2,1,0:T(8,128)(2,1)S(1)}, bf16[4,256,256]{2,1,0:T(8,128)(2,1)S(1)}, u32[]{:S(2)}, u32[]{:S(2)}) collective-permute-start(bf16[4,256,256]{2,1,0:T(8,128)(2,1)S(1)} %collective-permute-done.refs_3_), channel_id=1, source_target_pairs={{0,1},{1,0},{2,3},{3,2},{4,5},{5,4},{6,7},{7,6},{8,9},{9,8},{10,11... | collective-permute-start | bytes 1572872 | tf_op jit(solution)/shard_map/ppermute | solution.py:123
  30.5 4.8 %collective-permute-start.4 = (bf16[4,256,256]{2,1,0:T(8,128)(2,1)S(1)}, bf16[4,256,256]{2,1,0:T(8,128)(2,1)S(1)}, u32[]{:S(2)}, u32[]{:S(2)}) collective-permute-start(bf16[4,256,256]{2,1,0:T(8,128)(2,1)S(1)} %collective-permute-done.1.refs_2_), channel_id=1, source_target_pairs={{0,1},{1,0},{2,3},{3,2},{4,5},{5,4},{6,7},{7,6},{8,9},{9,8},{10,11... | collective-permute-start | bytes 1572872 | tf_op jit(solution)/shard_map/ppermute | solution.py:123
  32.4 4.1 %collective-permute-start.5 = (bf16[4,256,256]{2,1,0:T(8,128)(2,1)}, bf16[4,256,256]{2,1,0:T(8,128)(2,1)S(1)}, u32[]{:S(2)}, u32[]{:S(2)}) collective-permute-start(bf16[4,256,256]{2,1,0:T(8,128)(2,1)} %refs_0_), channel_id=1, source_target_pairs={{0,1},{1,0},{2,3},{3,2},{4,5},{5,4},{6,7},{7,6},{8,9},{9,8},{10,11... | collective-permute-start | bytes 1572872 | tf_op jit(solution)/shard_map/ppermute | solution.py:123
  36.5 3.8 %collective-permute-start.7 = (bf16[4,256,256]{2,1,0:T(8,128)(2,1)S(1)}, bf16[4,256,256]{2,1,0:T(8,128)(2,1)S(1)}, u32[]{:S(2)}, u32[]{:S(2)}) collective-permute-start(bf16[4,256,256]{2,1,0:T(8,128)(2,1)S(1)} %collective-permute-done.6.refs_6_), channel_id=1, source_target_pairs={{0,1},{1,0},{2,3},{3,2},{4,5},{5,4},{6,7},{7,6},{8,9},{9,8},{10,11... | collective-permute-start | bytes 1572872 | tf_op jit(solution)/shard_map/ppermute | solution.py:123
  40.3 1.0 %copy-start.1 = (bf16[4,256,256]{2,1,0:T(8,128)(2,1)S(1)}, bf16[4,256,256]{2,1,0:T(8,128)(2,1)}, u32[]{:S(2)}) copy-start(bf16[4,256,256]{2,1,0:T(8,128)(2,1)} %refs_0_) | copy-start | bytes 1572868

commit v9 on v5

--- a/solution.py
+++ b/solution.py
@@ -33,6 +33,12 @@
     here = rank[None, :] == pair[:, None]
     listed = jnp.sum(jnp.where(here, keys[None, :], 0), axis=1)
     return listed, jnp.sum(jnp.where(here, weights[None, :], 0.0), axis=1)
+
+
+def keep_kernel(block, kept_ref, sem):
+    copy = pltpu.make_async_copy(block, kept_ref, sem)
+    copy.start()
+    copy.wait()
 
 
 def terms_kernel(list_ref, weight_ref, left_hbm, right_hbm, *refs):
@@ -132,7 +138,17 @@
         "tij,tjl->til", local_rows, right_block, preferred_element_type=jnp.float32
     )
 
-    near, other, local_part, psi = lax.optimization_barrier((near[::-1], other, local_part, psi))
+    own = pl.pallas_call(
+        keep_kernel,
+        out_shape=jax.ShapeDtypeStruct(psi.shape, psi.dtype),
+        in_specs=[anywhere],
+        out_specs=vmem,
+        scratch_shapes=[pltpu.SemaphoreType.DMA],
+        compiler_params=pltpu.CompilerParams(vmem_limit_bytes=48 * 2**20),
+        name="keep",
+    )(psi)
+
+    near, other, local_part, psi = lax.optimization_barrier((near[::-1], other, local_part, own))
     near = near[::-1]
     far = from_y(near[0], 1)
 

time: 89.6 us -> 87.7 us (0.979)
  the two profiles are of different devices: /device:TPU:8 before, /device:TPU:2 now
where the time goes in v9:
time: 87.7 us; the launch traced here: 87.2 us
  blocking collectives  46.1 us (53%)
  starting transfers between devices  26.1 us (30%)
  waiting for transfers between devices  4.83 us (6%)
  Pallas kernels  4.15 us (5%)
  matrix products  2.46 us (3%)
  other arithmetic  1.97 us (2%)
  local copies, waits for them, and re-layouts  1.37 us (2%)
    all_to_all x1, blocking collectives, per_device(): bands = lax.all_to_all(bands, ('z', 'half'), 0, 0, tiled=True)  26.1 us
    all_to_all x1, blocking collectives, per_device(): bands = lax.all_to_all(partial_sum, 'x', 0, 0, tiled=True)  20 us
    ppermute x4, starting transfers between devices, from_y(): return lax.ppermute(value, ('half', 'y', 'core'), route)  16.2 us
    ppermute x4, starting transfers between devices, from_core(): return lax.ppermute(value, 'core', [(0, 1), (1, 0)])  9.96 us
    pallas_call x1, Pallas kernels, per_device(): pl.pallas_call(terms_kernel, out_shape=jax.ShapeDtypeStruct((n_x, n_z, ta...  4.1 us
    ppermute x4, waiting for transfers between devices, from_core(): return lax.ppermute(value, 'core', [(0, 1), (1, 0)])  2.57 us
    ppermute x4, waiting for transfers between devices, from_y(): return lax.ppermute(value, ('half', 'y', 'core'), route)  2.26 us
  transfers between devices with their start and end apart: 8, of which 3 were waited for; matrix products, arithmetic and copies ran while one was open for 5% of the time, Pallas kernels for 0%

profile of v9, /device:TPU:2, one launch (start us, length us, event | category | flops | bytes accessed | tf_op | source)
XLA Modules:
  0.0 87.2 jit_solution(16812042550084918013)
XLA Ops:
  0.0 0.0 copy-start
  0.0 0.0 copy-start.2
  0.0 5.5 %collective-permute-start.1 = (bf16[4,256,256]{2,1,0:T(8,128)(2,1)}, bf16[4,256,256]{2,1,0:T(8,128)(2,1)S(1)}, u32[]{:S(2)}, u32[]{:S(2)}) collective-permute-start(bf16[4,256,256]{2,1,0:T(8,128)(2,1)} %block.1), channel_id=1, source_target_pairs={{2,0},{15,1},{4,2},{1,3},{6,4},{3,5},{8,6},{5,7},{10,8},{7,9},{12,... | collective-permute-start | bytes 1572872 | tf_op jit(solution)/shard_map/ppermute | solution.py:126
  5.5 1.9 %collective-permute-start = (bf16[4,256,256]{2,1,0:T(8,128)(2,1)}, bf16[4,256,256]{2,1,0:T(8,128)(2,1)S(1)}, u32[]{:S(2)}, u32[]{:S(2)}) collective-permute-start(bf16[4,256,256]{2,1,0:T(8,128)(2,1)} %block.1), channel_id=1, source_target_pairs={{14,0},{3,1},{0,2},{5,3},{2,4},{7,5},{4,6},{9,7},{6,8},{11,9},{8,1... | collective-permute-start | bytes 1572872 | tf_op jit(solution)/shard_map/ppermute | solution.py:126
  7.4 0.7 compare_select_fusion.15
  8.1 6.3 %collective-permute-start.2 = (s32[16,4]{0,1:T(4,128)S(1)}, s32[16,4]{0,1:T(4,128)S(1)}, u32[]{:S(2)}, u32[]{:S(2)}) collective-permute-start(s32[16,4]{0,1:T(4,128)S(1)} %compare_select_fusion.15), channel_id=1, source_target_pairs={{8,0},{9,1},{10,2},{11,3},{12,4},{13,5},{14,6},{15,7},{0,8},{1,9},... | collective-permute-start | bytes 776 | tf_op jit(solution)/shard_map/ppermute | solution.py:126
  14.4 0.0 copy-start.1
  14.4 1.0 %copy-done.1 = bf16[4,256,256]{2,1,0:T(8,128)(2,1)S(1)} copy-done((bf16[4,256,256]{2,1,0:T(8,128)(2,1)S(1)}, bf16[4,256,256]{2,1,0:T(8,128)(2,1)}, u32[]{:S(2)}) %copy-start.1) | copy-done | bytes 524312
  15.5 0.0 copy-done
  15.5 1.2 %fusion.1 = f32[4,8,256]{2,1,0:T(8,128)S(1)} fusion(bf16[4,256,256]{2,1,0:T(8,128)(2,1)} %block.1, bf16[4,256,256]{2,1,0:T(8,128)(2,1)S(1)} %copy-done, s32[]{:T(128)S(6)} %select_n.259), kind=kOutput, calls=%fused_computation.9 | convolution fusion | flops 4194304 | bytes 573444 | tf_op jit(solution)/shard_map/tij,tjl->til/dot_general | solution.py:136
  16.8 1.2 %convolution_add_fusion = f32[4,8,256]{2,1,0:T(8,128)S(1)} fusion(f32[4,8,256]{2,1,0:T(8,128)S(1)} %fusion.1, bf16[4,256,256]{2,1,0:T(8,128)(2,1)} %param.15, bf16[4,256,256]{2,1,0:T(8,128)(2,1)} %block.1, s32[]{:T(128)S(6)} %select_n.259), kind=kOutput, calls=%fused_computation.1 | convolution fusion | flops 4202496 | bytes 606212 | tf_op jit(solution)/shard_map/tij,tjl->til/dot_general | solution.py:137
  18.0 0.0 copy-done.2
  18.0 0.1 broadcast_in_dim.61
  18.1 0.1 broadcast_in_dim.62
  18.2 2.3 %collective-permute-done.2 = s32[16,4]{0,1:T(4,128)S(1)} collective-permute-done((s32[16,4]{0,1:T(4,128)S(1)}, s32[16,4]{0,1:T(4,128)S(1)}, u32[]{:S(2)}, u32[]{:S(2)}) %collective-permute-start.2) | collective-permute-done | bytes 288 | tf_op jit(solution)/shard_map/ppermute | solution.py:126
  20.4 0.0 collective-permute-done.1.refs_2_
  20.4 0.0 collective-permute-done.refs_3_
  20.4 2.5 %collective-permute-start.6 = (bf16[4,256,256]{2,1,0:T(8,128)(2,1)S(1)}, bf16[4,256,256]{2,1,0:T(8,128)(2,1)S(1)}, u32[]{:S(2)}, u32[]{:S(2)}) collective-permute-start(bf16[4,256,256]{2,1,0:T(8,128)(2,1)S(1)} %collective-permute-done.1.refs_2_), channel_id=1, source_target_pairs={{2,0},{15,1},{4,2},{1,3},{6,4},{3,5},{8,6},{5,7},{10,8},{7,9},{12,... | collective-permute-start | bytes 1572872 | tf_op jit(solution)/shard_map/ppermute | solution.py:126
  22.9 3.4 %collective-permute-start.4 = (bf16[4,256,256]{2,1,0:T(8,128)(2,1)S(1)}, bf16[4,256,256]{2,1,0:T(8,128)(2,1)S(1)}, u32[]{:S(2)}, u32[]{:S(2)}) collective-permute-start(bf16[4,256,256]{2,1,0:T(8,128)(2,1)S(1)} %collective-permute-done.1.refs_2_), channel_id=1, source_target_pairs={{0,1},{1,0},{2,3},{3,2},{4,5},{5,4},{6,7},{7,6},{8,9},{9,8},{10,11... | collective-permute-start | bytes 1572872 | tf_op jit(solution)/shard_map/ppermute | solution.py:129
  26.3 0.1 copy.11
  26.4 0.1 concatenate.6
  26.5 1.9 %collective-permute-start.3 = (bf16[4,256,256]{2,1,0:T(8,128)(2,1)S(1)}, bf16[4,256,256]{2,1,0:T(8,128)(2,1)S(1)}, u32[]{:S(2)}, u32[]{:S(2)}) collective-permute-start(bf16[4,256,256]{2,1,0:T(8,128)(2,1)S(1)} %collective-permute-done.refs_3_), channel_id=1, source_target_pairs={{0,1},{1,0},{2,3},{3,2},{4,5},{5,4},{6,7},{7,6},{8,9},{9,8},{10,11... | collective-permute-start | bytes 1572872 | tf_op jit(solution)/shard_map/ppermute | solution.py:129
  28.4 2.4 %collective-permute-start.5 = (bf16[4,256,256]{2,1,0:T(8,128)(2,1)S(1)}, bf16[4,256,256]{2,1,0:T(8,128)(2,1)S(1)}, u32[]{:S(2)}, u32[]{:S(2)}) collective-permute-start(bf16[4,256,256]{2,1,0:T(8,128)(2,1)S(1)} %keep.1.refs_0_), channel_id=1, source_target_pairs={{0,1},{1,0},{2,3},{3,2},{4,5},{5,4},{6,7},{7,6},{8,9},{9,8},{10,11... | collective-permute-start | bytes 1572872 | tf_op jit(solution)/shard_map/ppermute | solution.py:129
  30.9 0.2 convert_reduce_fusion.2
  31.0 0.1 select_reduce_fusion.1.list_ref
  31.2 0.1 select_reduce_fusion.weight_ref
  31.3 0.0 collective-permute-done.3.refs_5_
  31.3 1.1 %collective-permute-done.5.refs_1_ = bf16[4,256,256]{2,1,0:T(8,128)(2,1)S(1)} collective-permute-done((bf16[4,256,256]{2,1,0:T(8,128)(2,1)S(1)}, bf16[4,256,256]{2,1,0:T(8,128)(2,1)S(1)}, u32[]{:S(2)}, u32[]{:S(2)}) %collective-permute-start.5) | collective-permute-done | bytes 524320 | tf_op jit(solution)/shard_map/ppermute | solution.py:129
  32.3 0.0 collective-permute-done.6.refs_6_
  32.3 0.0 collective-permute-done.4.refs_4_
  32.3 2.3 %collective-permute-start.7 = (bf16[4,256,256]{2,1,0:T(8,128)(2,1)S(1)}, bf16[4,256,256]{2,1,0:T(8,128)(2,1)S(1)}, u32[]{:S(2)}, u32[]{:S(2)}) collective-permute-start(bf16[4,256,256]{2,1,0:T(8,128)(2,1)S(1)} %collective-permute-done.6.refs_6_), channel_id=1, source_target_pairs={{0,1},{1,0},{2,3},{3,2},{4,5},{5,4},{6,7},{7,6},{8,9},{9,8},{10,11... | collective-permute-start | bytes 1572872 | tf_op jit(solution)/shard_map/ppermute | solution.py:129
  34.6 1.5 %collective-permute-done.7.refs_7_ = bf16[4,256,256]{2,1,0:T(8,128)(2,1)S(1)} collective-permute-done((bf16[4,256,256]{2,1,0:T(8,128)(2,1)S(1)}, bf16[4,256,256]{2,1,0:T(8,128)(2,1)S(1)}, u32[]{:S(2)}, u32[]{:S(2)}) %collective-permute-start.7) | collective-permute-done | bytes 524320 | tf_op jit(solution)/shard_map/ppermute | solution.py:129
  36.1 4.1 %terms.1 = bf16[4,8,64,256]{3,2,1,0:T(8,128)(2,1)S(1)} custom-call(s32[128]{0:T(128)S(1)} %select_reduce_fusion.1.list_ref, f32[128]{0:T(128)S(1)} %select_reduce_fusion.weight_ref, bf16[16,256,256]{2,1,0:T(8,128)(2,1)} %left_hbm.1, bf16[16,256,256]{2,1,0:T(8,128)(2,1)} %right_hbm.1, bf16[4,256,256]{2,1,0:T(8,128)(2,1)S(1)} %keep.1.refs_0_, ...), custom_call_target="tpu_custom_call" | custom-call | tf_op jit(solution)/shard_map/terms/pallas_call | solution.py:169
  40.3 20.0 %all_to_all.10 = bf16[4,8,64,256]{3,2,1,0:T(8,128)(2,1)S(1)} all-to-all(bf16[4,8,64,256]{3,2,1,0:T(8,128)(2,1)S(1)} %terms.1), channel_id=1, replica_groups=mesh['z'=8,'x'=4,'half'=2,'y'=4,'core'=2] {'x'}, dimensions={0} | all-to-all | bytes 2097152 | tf_op jit(solution)/shard_map/all_to_all | solution.py:185
  60.2 0.2 convert_reduce_fusion
  60.4 26.1 %all_to_all.11 = bf16[16,32,256]{2,1,0:T(8,128)(2,1)S(1)} all-to-all(bf16[16,32,256]{2,1,0:T(8,128)(2,1)S(1)} %bitcast.5), channel_id=1, replica_groups=mesh['z'=8,'x'=4,'half'=2,'y'=4,'core'=2] {'z','half'}, dimensions={0} | all-to-all | bytes 524288 | tf_op jit(solution)/shard_map/all_to_all | solution.py:189
  86.6 0.6 bitcast_add_fusion
  (5 shorter events, 0.1 us)
Async XLA Ops:
  0.0 15.5 %copy-start = (bf16[4,256,256]{2,1,0:T(8,128)(2,1)S(1)}, bf16[4,256,256]{2,1,0:T(8,128)(2,1)}, u32[]{:S(2)}) copy-start(bf16[4,256,256]{2,1,0:T(8,128)(2,1)} %param.14) | copy-start | bytes 1572868
  0.0 18.0 %copy-start.2 = (f32[16]{0:T(128)S(1)}, f32[16]{0:T(128)}, u32[]{:S(2)}) copy-start(f32[16]{0:T(128)} %param.11) | copy-start | bytes 196
  0.0 20.4 %collective-permute-start.1 = (bf16[4,256,256]{2,1,0:T(8,128)(2,1)}, bf16[4,256,256]{2,1,0:T(8,128)(2,1)S(1)}, u32[]{:S(2)}, u32[]{:S(2)}) collective-permute-start(bf16[4,256,256]{2,1,0:T(8,128)(2,1)} %block.1), channel_id=1, source_target_pairs={{2,0},{15,1},{4,2},{1,3},{6,4},{3,5},{8,6},{5,7},{10,8},{7,9},{12,... | collective-permute-start | bytes 1572872 | tf_op jit(solution)/shard_map/ppermute | solution.py:126
  5.5 14.9 %collective-permute-start = (bf16[4,256,256]{2,1,0:T(8,128)(2,1)}, bf16[4,256,256]{2,1,0:T(8,128)(2,1)S(1)}, u32[]{:S(2)}, u32[]{:S(2)}) collective-permute-start(bf16[4,256,256]{2,1,0:T(8,128)(2,1)} %block.1), channel_id=1, source_target_pairs={{14,0},{3,1},{0,2},{5,3},{2,4},{7,5},{4,6},{9,7},{6,8},{11,9},{8,1... | collective-permute-start | bytes 1572872 | tf_op jit(solution)/shard_map/ppermute | solution.py:126
  8.1 12.3 %collective-permute-start.2 = (s32[16,4]{0,1:T(4,128)S(1)}, s32[16,4]{0,1:T(4,128)S(1)}, u32[]{:S(2)}, u32[]{:S(2)}) collective-permute-start(s32[16,4]{0,1:T(4,128)S(1)} %compare_select_fusion.15), channel_id=1, source_target_pairs={{8,0},{9,1},{10,2},{11,3},{12,4},{13,5},{14,6},{15,7},{0,8},{1,9},... | collective-permute-start | bytes 776 | tf_op jit(solution)/shard_map/ppermute | solution.py:126
  14.4 1.0 %copy-start.1 = (bf16[4,256,256]{2,1,0:T(8,128)(2,1)S(1)}, bf16[4,256,256]{2,1,0:T(8,128)(2,1)}, u32[]{:S(2)}) copy-start(bf16[4,256,256]{2,1,0:T(8,128)(2,1)} %block.1) | copy-start | bytes 1572868
  20.4 11.9 %collective-permute-start.6 = (bf16[4,256,256]{2,1,0:T(8,128)(2,1)S(1)}, bf16[4,256,256]{2,1,0:T(8,128)(2,1)S(1)}, u32[]{:S(2)}, u32[]{:S(2)}) collective-permute-start(bf16[4,256,256]{2,1,0:T(8,128)(2,1)S(1)} %collective-permute-done.1.refs_2_), channel_id=1, source_target_pairs={{2,0},{15,1},{4,2},{1,3},{6,4},{3,5},{8,6},{5,7},{10,8},{7,9},{12,... | collective-permute-start | bytes 1572872 | tf_op jit(solution)/shard_map/ppermute | solution.py:126
  22.9 9.4 %collective-permute-start.4 = (bf16[4,256,256]{2,1,0:T(8,128)(2,1)S(1)}, bf16[4,256,256]{2,1,0:T(8,128)(2,1)S(1)}, u32[]{:S(2)}, u32[]{:S(2)}) collective-permute-start(bf16[4,256,256]{2,1,0:T(8,128)(2,1)S(1)} %collective-permute-done.1.refs_2_), channel_id=1, source_target_pairs={{0,1},{1,0},{2,3},{3,2},{4,5},{5,4},{6,7},{7,6},{8,9},{9,8},{10,11... | collective-permute-start | bytes 1572872 | tf_op jit(solution)/shard_map/ppermute | solution.py:129
  26.5 4.8 %collective-permute-start.3 = (bf16[4,256,256]{2,1,0:T(8,128)(2,1)S(1)}, bf16[4,256,256]{2,1,0:T(8,128)(2,1)S(1)}, u32[]{:S(2)}, u32[]{:S(2)}) collective-permute-start(bf16[4,256,256]{2,1,0:T(8,128)(2,1)S(1)} %collective-permute-done.refs_3_), channel_id=1, source_target_pairs={{0,1},{1,0},{2,3},{3,2},{4,5},{5,4},{6,7},{7,6},{8,9},{9,8},{10,11... | collective-permute-start | bytes 1572872 | tf_op jit(solution)/shard_map/ppermute | solution.py:129
  28.4 3.9 %collective-permute-start.5 = (bf16[4,256,256]{2,1,0:T(8,128)(2,1)S(1)}, bf16[4,256,256]{2,1,0:T(8,128)(2,1)S(1)}, u32[]{:S(2)}, u32[]{:S(2)}) collective-permute-start(bf16[4,256,256]{2,1,0:T(8,128)(2,1)S(1)} %keep.1.refs_0_), channel_id=1, source_target_pairs={{0,1},{1,0},{2,3},{3,2},{4,5},{5,4},{6,7},{7,6},{8,9},{9,8},{10,11... | collective-permute-start | bytes 1572872 | tf_op jit(solution)/shard_map/ppermute | solution.py:129
  32.3 3.8 %collective-permute-start.7 = (bf16[4,256,256]{2,1,0:T(8,128)(2,1)S(1)}, bf16[4,256,256]{2,1,0:T(8,128)(2,1)S(1)}, u32[]{:S(2)}, u32[]{:S(2)}) collective-permute-start(bf16[4,256,256]{2,1,0:T(8,128)(2,1)S(1)} %collective-permute-done.6.refs_6_), channel_id=1, source_target_pairs={{0,1},{1,0},{2,3},{3,2},{4,5},{5,4},{6,7},{7,6},{8,9},{9,8},{10,11... | collective-permute-start | bytes 1572872 | tf_op jit(solution)/shard_map/ppermute | solution.py:129

commit v10 on v9

--- a/solution.py
+++ b/solution.py
@@ -85,15 +85,15 @@
         needed = lax.div(functools.reduce(jnp.maximum, [w[0] for w in work]), sec_dev) + 1
         for b in range(len(blocks)):
             pl.when(jnp.logical_and(ready <= b, b < needed))(fetch(b).wait)
-        images = []
-        for place, term, target, weight in work:
-            mixed = jnp.dot(
-                left_ref[term], tiles[place], preferred_element_type=jnp.float32
-            ).astype(jnp.bfloat16)
-            image = jnp.dot(mixed, right_ref[term], preferred_element_type=jnp.float32)
-            images.append((target, image * weight))
-        for target, image in images:
-            sums[target] += image
+        mixed = [
+            jnp.dot(left_ref[term], tiles[place], preferred_element_type=jnp.float32)
+            for place, term, _, _ in work
+        ]
+        for value, (_, term, target, weight) in zip(mixed, work):
+            image = jnp.dot(
+                value.astype(jnp.bfloat16), right_ref[term], preferred_element_type=jnp.float32
+            )
+            sums[target] += image * weight
         return at + GROUP, jnp.maximum(ready, needed)
 
     _, ready = lax.while_loop(more, step, (0, 0))

time: 87.7 us -> 87.7 us (level)
  the two profiles are of different devices: /device:TPU:2 before, /device:TPU:16 now
where the time goes in v10:
time: 87.7 us; the launch traced here: 87.2 us
  blocking collectives  46.8 us (53%)
  starting transfers between devices  24 us (27%)
  waiting for transfers between devices  5.45 us (6%)
  Pallas kernels  5.01 us (6%)
  matrix products  2.46 us (3%)
  other arithmetic  1.97 us (2%)
  local copies, waits for them, and re-layouts  1.37 us (2%)
    all_to_all x1, blocking collectives, per_device(): bands = lax.all_to_all(bands, ('z', 'half'), 0, 0, tiled=True)  26.8 us
    all_to_all x1, blocking collectives, per_device(): bands = lax.all_to_all(partial_sum, 'x', 0, 0, tiled=True)  20 us
    ppermute x4, starting transfers between devices, from_y(): return lax.ppermute(value, ('half', 'y', 'core'), route)  15.6 us
    ppermute x4, starting transfers between devices, from_core(): return lax.ppermute(value, 'core', [(0, 1), (1, 0)])  8.37 us
    pallas_call x1, Pallas kernels, per_device(): pl.pallas_call(terms_kernel, out_shape=jax.ShapeDtypeStruct((n_x, n_z, ta...  4.96 us
    ppermute x4, waiting for transfers between devices, from_core(): return lax.ppermute(value, 'core', [(0, 1), (1, 0)])  3.08 us
    ppermute x4, waiting for transfers between devices, from_y(): return lax.ppermute(value, ('half', 'y', 'core'), route)  2.36 us
  transfers between devices with their start and end apart: 8, of which 3 were waited for; matrix products, arithmetic and copies ran while one was open for 5% of the time, Pallas kernels for 0%

profile of v10, /device:TPU:16, one launch (start us, length us, event | category | flops | bytes accessed | tf_op | source)
XLA Modules:
  0.0 87.2 jit_solution(17233105412765947533)
XLA Ops:
  0.0 0.0 copy-start
  0.0 0.0 copy-start.2
  0.0 2.5 %collective-permute-start.1 = (bf16[4,256,256]{2,1,0:T(8,128)(2,1)}, bf16[4,256,256]{2,1,0:T(8,128)(2,1)S(1)}, u32[]{:S(2)}, u32[]{:S(2)}) collective-permute-start(bf16[4,256,256]{2,1,0:T(8,128)(2,1)} %block.1), channel_id=1, source_target_pairs={{2,0},{15,1},{4,2},{1,3},{6,4},{3,5},{8,6},{5,7},{10,8},{7,9},{12,... | collective-permute-start | bytes 1572872 | tf_op jit(solution)/shard_map/ppermute | solution.py:126
  2.5 3.5 %collective-permute-start = (bf16[4,256,256]{2,1,0:T(8,128)(2,1)}, bf16[4,256,256]{2,1,0:T(8,128)(2,1)S(1)}, u32[]{:S(2)}, u32[]{:S(2)}) collective-permute-start(bf16[4,256,256]{2,1,0:T(8,128)(2,1)} %block.1), channel_id=1, source_target_pairs={{14,0},{3,1},{0,2},{5,3},{2,4},{7,5},{4,6},{9,7},{6,8},{11,9},{8,1... | collective-permute-start | bytes 1572872 | tf_op jit(solution)/shard_map/ppermute | solution.py:126
  6.0 0.7 compare_select_fusion.15
  6.7 5.9 %collective-permute-start.2 = (s32[16,4]{0,1:T(4,128)S(1)}, s32[16,4]{0,1:T(4,128)S(1)}, u32[]{:S(2)}, u32[]{:S(2)}) collective-permute-start(s32[16,4]{0,1:T(4,128)S(1)} %compare_select_fusion.15), channel_id=1, source_target_pairs={{8,0},{9,1},{10,2},{11,3},{12,4},{13,5},{14,6},{15,7},{0,8},{1,9},... | collective-permute-start | bytes 776 | tf_op jit(solution)/shard_map/ppermute | solution.py:126
  12.6 0.0 copy-start.1
  12.6 1.0 %copy-done.1 = bf16[4,256,256]{2,1,0:T(8,128)(2,1)S(1)} copy-done((bf16[4,256,256]{2,1,0:T(8,128)(2,1)S(1)}, bf16[4,256,256]{2,1,0:T(8,128)(2,1)}, u32[]{:S(2)}) %copy-start.1) | copy-done | bytes 524312
  13.7 0.0 copy-done
  13.7 1.2 %fusion.1 = f32[4,8,256]{2,1,0:T(8,128)S(1)} fusion(bf16[4,256,256]{2,1,0:T(8,128)(2,1)} %block.1, bf16[4,256,256]{2,1,0:T(8,128)(2,1)S(1)} %copy-done, s32[]{:T(128)S(6)} %select_n.259), kind=kOutput, calls=%fused_computation.9 | convolution fusion | flops 4194304 | bytes 573444 | tf_op jit(solution)/shard_map/tij,tjl->til/dot_general | solution.py:136
  15.0 1.2 %convolution_add_fusion = f32[4,8,256]{2,1,0:T(8,128)S(1)} fusion(f32[4,8,256]{2,1,0:T(8,128)S(1)} %fusion.1, bf16[4,256,256]{2,1,0:T(8,128)(2,1)} %param.15, bf16[4,256,256]{2,1,0:T(8,128)(2,1)} %block.1, s32[]{:T(128)S(6)} %select_n.259), kind=kOutput, calls=%fused_computation.1 | convolution fusion | flops 4202496 | bytes 606212 | tf_op jit(solution)/shard_map/tij,tjl->til/dot_general | solution.py:137
  16.2 0.0 copy-done.2
  16.2 0.1 broadcast_in_dim.61
  16.3 0.1 broadcast_in_dim.62
  16.4 2.4 %collective-permute-done.2 = s32[16,4]{0,1:T(4,128)S(1)} collective-permute-done((s32[16,4]{0,1:T(4,128)S(1)}, s32[16,4]{0,1:T(4,128)S(1)}, u32[]{:S(2)}, u32[]{:S(2)}) %collective-permute-start.2) | collective-permute-done | bytes 288 | tf_op jit(solution)/shard_map/ppermute | solution.py:126
  18.7 0.0 collective-permute-done.1.refs_2_
  18.7 0.0 collective-permute-done.refs_3_
  18.8 3.7 %collective-permute-start.6 = (bf16[4,256,256]{2,1,0:T(8,128)(2,1)S(1)}, bf16[4,256,256]{2,1,0:T(8,128)(2,1)S(1)}, u32[]{:S(2)}, u32[]{:S(2)}) collective-permute-start(bf16[4,256,256]{2,1,0:T(8,128)(2,1)S(1)} %collective-permute-done.1.refs_2_), channel_id=1, source_target_pairs={{2,0},{15,1},{4,2},{1,3},{6,4},{3,5},{8,6},{5,7},{10,8},{7,9},{12,... | collective-permute-start | bytes 1572872 | tf_op jit(solution)/shard_map/ppermute | solution.py:126
  22.5 2.0 %collective-permute-start.4 = (bf16[4,256,256]{2,1,0:T(8,128)(2,1)S(1)}, bf16[4,256,256]{2,1,0:T(8,128)(2,1)S(1)}, u32[]{:S(2)}, u32[]{:S(2)}) collective-permute-start(bf16[4,256,256]{2,1,0:T(8,128)(2,1)S(1)} %collective-permute-done.1.refs_2_), channel_id=1, source_target_pairs={{0,1},{1,0},{2,3},{3,2},{4,5},{5,4},{6,7},{7,6},{8,9},{9,8},{10,11... | collective-permute-start | bytes 1572872 | tf_op jit(solution)/shard_map/ppermute | solution.py:129
  24.5 0.1 copy.11
  24.6 0.1 concatenate.6
  24.7 2.3 %collective-permute-start.3 = (bf16[4,256,256]{2,1,0:T(8,128)(2,1)S(1)}, bf16[4,256,256]{2,1,0:T(8,128)(2,1)S(1)}, u32[]{:S(2)}, u32[]{:S(2)}) collective-permute-start(bf16[4,256,256]{2,1,0:T(8,128)(2,1)S(1)} %collective-permute-done.refs_3_), channel_id=1, source_target_pairs={{0,1},{1,0},{2,3},{3,2},{4,5},{5,4},{6,7},{7,6},{8,9},{9,8},{10,11... | collective-permute-start | bytes 1572872 | tf_op jit(solution)/shard_map/ppermute | solution.py:129
  27.0 2.0 %collective-permute-start.5 = (bf16[4,256,256]{2,1,0:T(8,128)(2,1)S(1)}, bf16[4,256,256]{2,1,0:T(8,128)(2,1)S(1)}, u32[]{:S(2)}, u32[]{:S(2)}) collective-permute-start(bf16[4,256,256]{2,1,0:T(8,128)(2,1)S(1)} %keep.1.refs_0_), channel_id=1, source_target_pairs={{0,1},{1,0},{2,3},{3,2},{4,5},{5,4},{6,7},{7,6},{8,9},{9,8},{10,11... | collective-permute-start | bytes 1572872 | tf_op jit(solution)/shard_map/ppermute | solution.py:129
  29.1 0.2 convert_reduce_fusion.2
  29.2 0.1 select_reduce_fusion.1.list_ref
  29.4 0.1 select_reduce_fusion.weight_ref
  29.5 0.0 collective-permute-done.3.refs_5_
  29.5 1.3 %collective-permute-done.5.refs_1_ = bf16[4,256,256]{2,1,0:T(8,128)(2,1)S(1)} collective-permute-done((bf16[4,256,256]{2,1,0:T(8,128)(2,1)S(1)}, bf16[4,256,256]{2,1,0:T(8,128)(2,1)S(1)}, u32[]{:S(2)}, u32[]{:S(2)}) %collective-permute-start.5) | collective-permute-done | bytes 524320 | tf_op jit(solution)/shard_map/ppermute | solution.py:129
  30.8 0.0 collective-permute-done.6.refs_6_
  30.8 0.0 collective-permute-done.4.refs_4_
  30.8 2.0 %collective-permute-start.7 = (bf16[4,256,256]{2,1,0:T(8,128)(2,1)S(1)}, bf16[4,256,256]{2,1,0:T(8,128)(2,1)S(1)}, u32[]{:S(2)}, u32[]{:S(2)}) collective-permute-start(bf16[4,256,256]{2,1,0:T(8,128)(2,1)S(1)} %collective-permute-done.6.refs_6_), channel_id=1, source_target_pairs={{0,1},{1,0},{2,3},{3,2},{4,5},{5,4},{6,7},{7,6},{8,9},{9,8},{10,11... | collective-permute-start | bytes 1572872 | tf_op jit(solution)/shard_map/ppermute | solution.py:129
  32.9 1.8 %collective-permute-done.7.refs_7_ = bf16[4,256,256]{2,1,0:T(8,128)(2,1)S(1)} collective-permute-done((bf16[4,256,256]{2,1,0:T(8,128)(2,1)S(1)}, bf16[4,256,256]{2,1,0:T(8,128)(2,1)S(1)}, u32[]{:S(2)}, u32[]{:S(2)}) %collective-permute-start.7) | collective-permute-done | bytes 524320 | tf_op jit(solution)/shard_map/ppermute | solution.py:129
  34.6 5.0 %terms.1 = bf16[4,8,64,256]{3,2,1,0:T(8,128)(2,1)S(1)} custom-call(s32[128]{0:T(128)S(1)} %select_reduce_fusion.1.list_ref, f32[128]{0:T(128)S(1)} %select_reduce_fusion.weight_ref, bf16[16,256,256]{2,1,0:T(8,128)(2,1)} %left_hbm.1, bf16[16,256,256]{2,1,0:T(8,128)(2,1)} %right_hbm.1, bf16[4,256,256]{2,1,0:T(8,128)(2,1)S(1)} %keep.1.refs_0_, ...), custom_call_target="tpu_custom_call" | custom-call | tf_op jit(solution)/shard_map/terms/pallas_call | solution.py:169
  39.6 20.0 %all_to_all.10 = bf16[4,8,64,256]{3,2,1,0:T(8,128)(2,1)S(1)} all-to-all(bf16[4,8,64,256]{3,2,1,0:T(8,128)(2,1)S(1)} %terms.1), channel_id=1, replica_groups=mesh['z'=8,'x'=4,'half'=2,'y'=4,'core'=2] {'x'}, dimensions={0} | all-to-all | bytes 2097152 | tf_op jit(solution)/shard_map/all_to_all | solution.py:185
  59.6 0.2 convert_reduce_fusion
  59.7 26.8 %all_to_all.11 = bf16[16,32,256]{2,1,0:T(8,128)(2,1)S(1)} all-to-all(bf16[16,32,256]{2,1,0:T(8,128)(2,1)S(1)} %bitcast.5), channel_id=1, replica_groups=mesh['z'=8,'x'=4,'half'=2,'y'=4,'core'=2] {'z','half'}, dimensions={0} | all-to-all | bytes 524288 | tf_op jit(solution)/shard_map/all_to_all | solution.py:189
  86.6 0.6 bitcast_add_fusion
  (5 shorter events, 0.1 us)
Async XLA Ops:
  0.0 13.7 %copy-start = (bf16[4,256,256]{2,1,0:T(8,128)(2,1)S(1)}, bf16[4,256,256]{2,1,0:T(8,128)(2,1)}, u32[]{:S(2)}) copy-start(bf16[4,256,256]{2,1,0:T(8,128)(2,1)} %param.14) | copy-start | bytes 1572868
  0.0 16.2 %copy-start.2 = (f32[16]{0:T(128)S(1)}, f32[16]{0:T(128)}, u32[]{:S(2)}) copy-start(f32[16]{0:T(128)} %param.11) | copy-start | bytes 196
  0.0 18.7 %collective-permute-start.1 = (bf16[4,256,256]{2,1,0:T(8,128)(2,1)}, bf16[4,256,256]{2,1,0:T(8,128)(2,1)S(1)}, u32[]{:S(2)}, u32[]{:S(2)}) collective-permute-start(bf16[4,256,256]{2,1,0:T(8,128)(2,1)} %block.1), channel_id=1, source_target_pairs={{2,0},{15,1},{4,2},{1,3},{6,4},{3,5},{8,6},{5,7},{10,8},{7,9},{12,... | collective-permute-start | bytes 1572872 | tf_op jit(solution)/shard_map/ppermute | solution.py:126
  2.5 16.3 %collective-permute-start = (bf16[4,256,256]{2,1,0:T(8,128)(2,1)}, bf16[4,256,256]{2,1,0:T(8,128)(2,1)S(1)}, u32[]{:S(2)}, u32[]{:S(2)}) collective-permute-start(bf16[4,256,256]{2,1,0:T(8,128)(2,1)} %block.1), channel_id=1, source_target_pairs={{14,0},{3,1},{0,2},{5,3},{2,4},{7,5},{4,6},{9,7},{6,8},{11,9},{8,1... | collective-permute-start | bytes 1572872 | tf_op jit(solution)/shard_map/ppermute | solution.py:126
  6.7 12.1 %collective-permute-start.2 = (s32[16,4]{0,1:T(4,128)S(1)}, s32[16,4]{0,1:T(4,128)S(1)}, u32[]{:S(2)}, u32[]{:S(2)}) collective-permute-start(s32[16,4]{0,1:T(4,128)S(1)} %compare_select_fusion.15), channel_id=1, source_target_pairs={{8,0},{9,1},{10,2},{11,3},{12,4},{13,5},{14,6},{15,7},{0,8},{1,9},... | collective-permute-start | bytes 776 | tf_op jit(solution)/shard_map/ppermute | solution.py:126
  12.6 1.0 %copy-start.1 = (bf16[4,256,256]{2,1,0:T(8,128)(2,1)S(1)}, bf16[4,256,256]{2,1,0:T(8,128)(2,1)}, u32[]{:S(2)}) copy-start(bf16[4,256,256]{2,1,0:T(8,128)(2,1)} %block.1) | copy-start | bytes 1572868
  18.8 12.1 %collective-permute-start.6 = (bf16[4,256,256]{2,1,0:T(8,128)(2,1)S(1)}, bf16[4,256,256]{2,1,0:T(8,128)(2,1)S(1)}, u32[]{:S(2)}, u32[]{:S(2)}) collective-permute-start(bf16[4,256,256]{2,1,0:T(8,128)(2,1)S(1)} %collective-permute-done.1.refs_2_), channel_id=1, source_target_pairs={{2,0},{15,1},{4,2},{1,3},{6,4},{3,5},{8,6},{5,7},{10,8},{7,9},{12,... | collective-permute-start | bytes 1572872 | tf_op jit(solution)/shard_map/ppermute | solution.py:126
  22.5 8.3 %collective-permute-start.4 = (bf16[4,256,256]{2,1,0:T(8,128)(2,1)S(1)}, bf16[4,256,256]{2,1,0:T(8,128)(2,1)S(1)}, u32[]{:S(2)}, u32[]{:S(2)}) collective-permute-start(bf16[4,256,256]{2,1,0:T(8,128)(2,1)S(1)} %collective-permute-done.1.refs_2_), channel_id=1, source_target_pairs={{0,1},{1,0},{2,3},{3,2},{4,5},{5,4},{6,7},{7,6},{8,9},{9,8},{10,11... | collective-permute-start | bytes 1572872 | tf_op jit(solution)/shard_map/ppermute | solution.py:129
  24.7 4.8 %collective-permute-start.3 = (bf16[4,256,256]{2,1,0:T(8,128)(2,1)S(1)}, bf16[4,256,256]{2,1,0:T(8,128)(2,1)S(1)}, u32[]{:S(2)}, u32[]{:S(2)}) collective-permute-start(bf16[4,256,256]{2,1,0:T(8,128)(2,1)S(1)} %collective-permute-done.refs_3_), channel_id=1, source_target_pairs={{0,1},{1,0},{2,3},{3,2},{4,5},{5,4},{6,7},{7,6},{8,9},{9,8},{10,11... | collective-permute-start | bytes 1572872 | tf_op jit(solution)/shard_map/ppermute | solution.py:129
  27.0 3.8 %collective-permute-start.5 = (bf16[4,256,256]{2,1,0:T(8,128)(2,1)S(1)}, bf16[4,256,256]{2,1,0:T(8,128)(2,1)S(1)}, u32[]{:S(2)}, u32[]{:S(2)}) collective-permute-start(bf16[4,256,256]{2,1,0:T(8,128)(2,1)S(1)} %keep.1.refs_0_), channel_id=1, source_target_pairs={{0,1},{1,0},{2,3},{3,2},{4,5},{5,4},{6,7},{7,6},{8,9},{9,8},{10,11... | collective-permute-start | bytes 1572872 | tf_op jit(solution)/shard_map/ppermute | solution.py:129
  30.8 3.8 %collective-permute-start.7 = (bf16[4,256,256]{2,1,0:T(8,128)(2,1)S(1)}, bf16[4,256,256]{2,1,0:T(8,128)(2,1)S(1)}, u32[]{:S(2)}, u32[]{:S(2)}) collective-permute-start(bf16[4,256,256]{2,1,0:T(8,128)(2,1)S(1)} %collective-permute-done.6.refs_6_), channel_id=1, source_target_pairs={{0,1},{1,0},{2,3},{3,2},{4,5},{5,4},{6,7},{7,6},{8,9},{9,8},{10,11... | collective-permute-start | bytes 1572872 | tf_op jit(solution)/shard_map/ppermute | solution.py:129

commit v11 on v9

--- a/solution.py
+++ b/solution.py
@@ -85,15 +85,17 @@
         needed = lax.div(functools.reduce(jnp.maximum, [w[0] for w in work]), sec_dev) + 1
         for b in range(len(blocks)):
             pl.when(jnp.logical_and(ready <= b, b < needed))(fetch(b).wait)
-        images = []
-        for place, term, target, weight in work:
-            mixed = jnp.dot(
+        def mix(place, term):
+            return jnp.dot(
                 left_ref[term], tiles[place], preferred_element_type=jnp.float32
             ).astype(jnp.bfloat16)
+
+        mixed = mix(*work[0][:2])
+        for j, (_, term, target, weight) in enumerate(work):
+            later = mix(*work[j + 1][:2]) if j + 1 < GROUP else None
             image = jnp.dot(mixed, right_ref[term], preferred_element_type=jnp.float32)
-            images.append((target, image * weight))
-        for target, image in images:
-            sums[target] += image
+            sums[target] += image * weight
+            mixed = later
         return at + GROUP, jnp.maximum(ready, needed)
 
     _, ready = lax.while_loop(more, step, (0, 0))

time: 87.7 us -> 90.2 us (1.029)
  the two profiles are of different devices: /device:TPU:2 before, /device:TPU:8 now
where the time goes in v11:
time: 90.2 us; the launch traced here: 89.3 us
  blocking collectives  46.2 us (51%)
  starting transfers between devices  24.7 us (27%)
  Pallas kernels  6.38 us (7%)
  waiting for transfers between devices  6.01 us (7%)
  matrix products  2.46 us (3%)
  other arithmetic  1.97 us (2%)
  local copies, waits for them, and re-layouts  1.37 us (2%)
    all_to_all x1, blocking collectives, per_device(): bands = lax.all_to_all(bands, ('z', 'half'), 0, 0, tiled=True)  27.9 us
    all_to_all x1, blocking collectives, per_device(): bands = lax.all_to_all(partial_sum, 'x', 0, 0, tiled=True)  18.4 us
    ppermute x4, starting transfers between devices, from_y(): return lax.ppermute(value, ('half', 'y', 'core'), route)  16.5 us
    ppermute x4, starting transfers between devices, from_core(): return lax.ppermute(value, 'core', [(0, 1), (1, 0)])  8.28 us
    pallas_call x1, Pallas kernels, per_device(): pl.pallas_call(terms_kernel, out_shape=jax.ShapeDtypeStruct((n_x, n_z, ta...  6.33 us
    ppermute x4, waiting for transfers between devices, from_core(): return lax.ppermute(value, 'core', [(0, 1), (1, 0)])  3.17 us
    ppermute x4, waiting for transfers between devices, from_y(): return lax.ppermute(value, ('half', 'y', 'core'), route)  2.84 us
  transfers between devices with their start and end apart: 8, of which 3 were waited for; matrix products, arithmetic and copies ran while one was open for 4% of the time, Pallas kernels for 0%

profile of v11, /device:TPU:8, one launch (start us, length us, event | category | flops | bytes accessed | tf_op | source)
XLA Modules:
  0.0 89.3 jit_solution(2860678907246888966)
XLA Ops:
  0.0 0.0 copy-start
  0.0 0.0 copy-start.2
  0.0 7.9 %collective-permute-start.1 = (bf16[4,256,256]{2,1,0:T(8,128)(2,1)}, bf16[4,256,256]{2,1,0:T(8,128)(2,1)S(1)}, u32[]{:S(2)}, u32[]{:S(2)}) collective-permute-start(bf16[4,256,256]{2,1,0:T(8,128)(2,1)} %block.1), channel_id=1, source_target_pairs={{2,0},{15,1},{4,2},{1,3},{6,4},{3,5},{8,6},{5,7},{10,8},{7,9},{12,... | collective-permute-start | bytes 1572872 | tf_op jit(solution)/shard_map/ppermute | solution.py:128
  7.9 1.9 %collective-permute-start = (bf16[4,256,256]{2,1,0:T(8,128)(2,1)}, bf16[4,256,256]{2,1,0:T(8,128)(2,1)S(1)}, u32[]{:S(2)}, u32[]{:S(2)}) collective-permute-start(bf16[4,256,256]{2,1,0:T(8,128)(2,1)} %block.1), channel_id=1, source_target_pairs={{14,0},{3,1},{0,2},{5,3},{2,4},{7,5},{4,6},{9,7},{6,8},{11,9},{8,1... | collective-permute-start | bytes 1572872 | tf_op jit(solution)/shard_map/ppermute | solution.py:128
  9.8 0.7 compare_select_fusion.15
  10.5 3.0 %collective-permute-start.2 = (s32[16,4]{0,1:T(4,128)S(1)}, s32[16,4]{0,1:T(4,128)S(1)}, u32[]{:S(2)}, u32[]{:S(2)}) collective-permute-start(s32[16,4]{0,1:T(4,128)S(1)} %compare_select_fusion.15), channel_id=1, source_target_pairs={{8,0},{9,1},{10,2},{11,3},{12,4},{13,5},{14,6},{15,7},{0,8},{1,9},... | collective-permute-start | bytes 776 | tf_op jit(solution)/shard_map/ppermute | solution.py:128
  13.5 0.0 copy-start.1
  13.5 1.0 %copy-done.1 = bf16[4,256,256]{2,1,0:T(8,128)(2,1)S(1)} copy-done((bf16[4,256,256]{2,1,0:T(8,128)(2,1)S(1)}, bf16[4,256,256]{2,1,0:T(8,128)(2,1)}, u32[]{:S(2)}) %copy-start.1) | copy-done | bytes 524312
  14.6 0.0 copy-done
  14.6 1.2 %fusion.1 = f32[4,8,256]{2,1,0:T(8,128)S(1)} fusion(bf16[4,256,256]{2,1,0:T(8,128)(2,1)} %block.1, bf16[4,256,256]{2,1,0:T(8,128)(2,1)S(1)} %copy-done, s32[]{:T(128)S(6)} %select_n.259), kind=kOutput, calls=%fused_computation.9 | convolution fusion | flops 4194304 | bytes 573444 | tf_op jit(solution)/shard_map/tij,tjl->til/dot_general | solution.py:138
  15.9 1.2 %convolution_add_fusion = f32[4,8,256]{2,1,0:T(8,128)S(1)} fusion(f32[4,8,256]{2,1,0:T(8,128)S(1)} %fusion.1, bf16[4,256,256]{2,1,0:T(8,128)(2,1)} %param.15, bf16[4,256,256]{2,1,0:T(8,128)(2,1)} %block.1, s32[]{:T(128)S(6)} %select_n.259), kind=kOutput, calls=%fused_computation.1 | convolution fusion | flops 4202496 | bytes 606212 | tf_op jit(solution)/shard_map/tij,tjl->til/dot_general | solution.py:139
  17.1 0.0 copy-done.2
  17.1 0.1 broadcast_in_dim.61
  17.2 0.1 broadcast_in_dim.62
  17.3 2.8 %collective-permute-done.2 = s32[16,4]{0,1:T(4,128)S(1)} collective-permute-done((s32[16,4]{0,1:T(4,128)S(1)}, s32[16,4]{0,1:T(4,128)S(1)}, u32[]{:S(2)}, u32[]{:S(2)}) %collective-permute-start.2) | collective-permute-done | bytes 288 | tf_op jit(solution)/shard_map/ppermute | solution.py:128
  20.1 0.0 collective-permute-done.1.refs_2_
  20.1 0.0 collective-permute-done.refs_3_
  20.1 3.7 %collective-permute-start.6 = (bf16[4,256,256]{2,1,0:T(8,128)(2,1)S(1)}, bf16[4,256,256]{2,1,0:T(8,128)(2,1)S(1)}, u32[]{:S(2)}, u32[]{:S(2)}) collective-permute-start(bf16[4,256,256]{2,1,0:T(8,128)(2,1)S(1)} %collective-permute-done.1.refs_2_), channel_id=1, source_target_pairs={{2,0},{15,1},{4,2},{1,3},{6,4},{3,5},{8,6},{5,7},{10,8},{7,9},{12,... | collective-permute-start | bytes 1572872 | tf_op jit(solution)/shard_map/ppermute | solution.py:128
  23.8 1.9 %collective-permute-start.4 = (bf16[4,256,256]{2,1,0:T(8,128)(2,1)S(1)}, bf16[4,256,256]{2,1,0:T(8,128)(2,1)S(1)}, u32[]{:S(2)}, u32[]{:S(2)}) collective-permute-start(bf16[4,256,256]{2,1,0:T(8,128)(2,1)S(1)} %collective-permute-done.1.refs_2_), channel_id=1, source_target_pairs={{0,1},{1,0},{2,3},{3,2},{4,5},{5,4},{6,7},{7,6},{8,9},{9,8},{10,11... | collective-permute-start | bytes 1572872 | tf_op jit(solution)/shard_map/ppermute | solution.py:131
  25.8 0.1 copy.11
  25.8 0.1 concatenate.6
  25.9 2.4 %collective-permute-start.3 = (bf16[4,256,256]{2,1,0:T(8,128)(2,1)S(1)}, bf16[4,256,256]{2,1,0:T(8,128)(2,1)S(1)}, u32[]{:S(2)}, u32[]{:S(2)}) collective-permute-start(bf16[4,256,256]{2,1,0:T(8,128)(2,1)S(1)} %collective-permute-done.refs_3_), channel_id=1, source_target_pairs={{0,1},{1,0},{2,3},{3,2},{4,5},{5,4},{6,7},{7,6},{8,9},{9,8},{10,11... | collective-permute-start | bytes 1572872 | tf_op jit(solution)/shard_map/ppermute | solution.py:131
  28.3 1.9 %collective-permute-start.5 = (bf16[4,256,256]{2,1,0:T(8,128)(2,1)S(1)}, bf16[4,256,256]{2,1,0:T(8,128)(2,1)S(1)}, u32[]{:S(2)}, u32[]{:S(2)}) collective-permute-start(bf16[4,256,256]{2,1,0:T(8,128)(2,1)S(1)} %keep.1.refs_0_), channel_id=1, source_target_pairs={{0,1},{1,0},{2,3},{3,2},{4,5},{5,4},{6,7},{7,6},{8,9},{9,8},{10,11... | collective-permute-start | bytes 1572872 | tf_op jit(solution)/shard_map/ppermute | solution.py:131
  30.3 0.2 convert_reduce_fusion.2
  30.5 0.1 select_reduce_fusion.1.list_ref
  30.6 0.1 select_reduce_fusion.weight_ref
  30.7 0.0 collective-permute-done.3.refs_5_
  30.7 1.4 %collective-permute-done.5.refs_1_ = bf16[4,256,256]{2,1,0:T(8,128)(2,1)S(1)} collective-permute-done((bf16[4,256,256]{2,1,0:T(8,128)(2,1)S(1)}, bf16[4,256,256]{2,1,0:T(8,128)(2,1)S(1)}, u32[]{:S(2)}, u32[]{:S(2)}) %collective-permute-start.5) | collective-permute-done | bytes 524320 | tf_op jit(solution)/shard_map/ppermute | solution.py:131
  32.1 0.0 collective-permute-done.6.refs_6_
  32.1 0.0 collective-permute-done.4.refs_4_
  32.1 2.0 %collective-permute-start.7 = (bf16[4,256,256]{2,1,0:T(8,128)(2,1)S(1)}, bf16[4,256,256]{2,1,0:T(8,128)(2,1)S(1)}, u32[]{:S(2)}, u32[]{:S(2)}) collective-permute-start(bf16[4,256,256]{2,1,0:T(8,128)(2,1)S(1)} %collective-permute-done.6.refs_6_), channel_id=1, source_target_pairs={{0,1},{1,0},{2,3},{3,2},{4,5},{5,4},{6,7},{7,6},{8,9},{9,8},{10,11... | collective-permute-start | bytes 1572872 | tf_op jit(solution)/shard_map/ppermute | solution.py:131
  34.2 1.8 %collective-permute-done.7.refs_7_ = bf16[4,256,256]{2,1,0:T(8,128)(2,1)S(1)} collective-permute-done((bf16[4,256,256]{2,1,0:T(8,128)(2,1)S(1)}, bf16[4,256,256]{2,1,0:T(8,128)(2,1)S(1)}, u32[]{:S(2)}, u32[]{:S(2)}) %collective-permute-start.7) | collective-permute-done | bytes 524320 | tf_op jit(solution)/shard_map/ppermute | solution.py:131
  35.9 6.3 %terms.1 = bf16[4,8,64,256]{3,2,1,0:T(8,128)(2,1)S(1)} custom-call(s32[128]{0:T(128)S(1)} %select_reduce_fusion.1.list_ref, f32[128]{0:T(128)S(1)} %select_reduce_fusion.weight_ref, bf16[16,256,256]{2,1,0:T(8,128)(2,1)} %left_hbm.1, bf16[16,256,256]{2,1,0:T(8,128)(2,1)} %right_hbm.1, bf16[4,256,256]{2,1,0:T(8,128)(2,1)S(1)} %keep.1.refs_0_, ...), custom_call_target="tpu_custom_call" | custom-call | tf_op jit(solution)/shard_map/terms/pallas_call | solution.py:171
  42.3 18.4 %all_to_all.10 = bf16[4,8,64,256]{3,2,1,0:T(8,128)(2,1)S(1)} all-to-all(bf16[4,8,64,256]{3,2,1,0:T(8,128)(2,1)S(1)} %terms.1), channel_id=1, replica_groups=mesh['z'=8,'x'=4,'half'=2,'y'=4,'core'=2] {'x'}, dimensions={0} | all-to-all | bytes 2097152 | tf_op jit(solution)/shard_map/all_to_all | solution.py:187
  60.7 0.2 convert_reduce_fusion
  60.8 27.9 %all_to_all.11 = bf16[16,32,256]{2,1,0:T(8,128)(2,1)S(1)} all-to-all(bf16[16,32,256]{2,1,0:T(8,128)(2,1)S(1)} %bitcast.5), channel_id=1, replica_groups=mesh['z'=8,'x'=4,'half'=2,'y'=4,'core'=2] {'z','half'}, dimensions={0} | all-to-all | bytes 524288 | tf_op jit(solution)/shard_map/all_to_all | solution.py:191
  88.7 0.6 bitcast_add_fusion
  (5 shorter events, 0.1 us)
Async XLA Ops:
  0.0 14.6 %copy-start = (bf16[4,256,256]{2,1,0:T(8,128)(2,1)S(1)}, bf16[4,256,256]{2,1,0:T(8,128)(2,1)}, u32[]{:S(2)}) copy-start(bf16[4,256,256]{2,1,0:T(8,128)(2,1)} %param.14) | copy-start | bytes 1572868
  0.0 17.1 %copy-start.2 = (f32[16]{0:T(128)S(1)}, f32[16]{0:T(128)}, u32[]{:S(2)}) copy-start(f32[16]{0:T(128)} %param.11) | copy-start | bytes 196
  0.0 20.1 %collective-permute-start.1 = (bf16[4,256,256]{2,1,0:T(8,128)(2,1)}, bf16[4,256,256]{2,1,0:T(8,128)(2,1)S(1)}, u32[]{:S(2)}, u32[]{:S(2)}) collective-permute-start(bf16[4,256,256]{2,1,0:T(8,128)(2,1)} %block.1), channel_id=1, source_target_pairs={{2,0},{15,1},{4,2},{1,3},{6,4},{3,5},{8,6},{5,7},{10,8},{7,9},{12,... | collective-permute-start | bytes 1572872 | tf_op jit(solution)/shard_map/ppermute | solution.py:128
  7.9 12.3 %collective-permute-start = (bf16[4,256,256]{2,1,0:T(8,128)(2,1)}, bf16[4,256,256]{2,1,0:T(8,128)(2,1)S(1)}, u32[]{:S(2)}, u32[]{:S(2)}) collective-permute-start(bf16[4,256,256]{2,1,0:T(8,128)(2,1)} %block.1), channel_id=1, source_target_pairs={{14,0},{3,1},{0,2},{5,3},{2,4},{7,5},{4,6},{9,7},{6,8},{11,9},{8,1... | collective-permute-start | bytes 1572872 | tf_op jit(solution)/shard_map/ppermute | solution.py:128
  10.5 9.6 %collective-permute-start.2 = (s32[16,4]{0,1:T(4,128)S(1)}, s32[16,4]{0,1:T(4,128)S(1)}, u32[]{:S(2)}, u32[]{:S(2)}) collective-permute-start(s32[16,4]{0,1:T(4,128)S(1)} %compare_select_fusion.15), channel_id=1, source_target_pairs={{8,0},{9,1},{10,2},{11,3},{12,4},{13,5},{14,6},{15,7},{0,8},{1,9},... | collective-permute-start | bytes 776 | tf_op jit(solution)/shard_map/ppermute | solution.py:128
  13.5 1.0 %copy-start.1 = (bf16[4,256,256]{2,1,0:T(8,128)(2,1)S(1)}, bf16[4,256,256]{2,1,0:T(8,128)(2,1)}, u32[]{:S(2)}) copy-start(bf16[4,256,256]{2,1,0:T(8,128)(2,1)} %block.1) | copy-start | bytes 1572868
  20.1 12.0 %collective-permute-start.6 = (bf16[4,256,256]{2,1,0:T(8,128)(2,1)S(1)}, bf16[4,256,256]{2,1,0:T(8,128)(2,1)S(1)}, u32[]{:S(2)}, u32[]{:S(2)}) collective-permute-start(bf16[4,256,256]{2,1,0:T(8,128)(2,1)S(1)} %collective-permute-done.1.refs_2_), channel_id=1, source_target_pairs={{2,0},{15,1},{4,2},{1,3},{6,4},{3,5},{8,6},{5,7},{10,8},{7,9},{12,... | collective-permute-start | bytes 1572872 | tf_op jit(solution)/shard_map/ppermute | solution.py:128
  23.8 8.3 %collective-permute-start.4 = (bf16[4,256,256]{2,1,0:T(8,128)(2,1)S(1)}, bf16[4,256,256]{2,1,0:T(8,128)(2,1)S(1)}, u32[]{:S(2)}, u32[]{:S(2)}) collective-permute-start(bf16[4,256,256]{2,1,0:T(8,128)(2,1)S(1)} %collective-permute-done.1.refs_2_), channel_id=1, source_target_pairs={{0,1},{1,0},{2,3},{3,2},{4,5},{5,4},{6,7},{7,6},{8,9},{9,8},{10,11... | collective-permute-start | bytes 1572872 | tf_op jit(solution)/shard_map/ppermute | solution.py:131
  25.9 4.8 %collective-permute-start.3 = (bf16[4,256,256]{2,1,0:T(8,128)(2,1)S(1)}, bf16[4,256,256]{2,1,0:T(8,128)(2,1)S(1)}, u32[]{:S(2)}, u32[]{:S(2)}) collective-permute-start(bf16[4,256,256]{2,1,0:T(8,128)(2,1)S(1)} %collective-permute-done.refs_3_), channel_id=1, source_target_pairs={{0,1},{1,0},{2,3},{3,2},{4,5},{5,4},{6,7},{7,6},{8,9},{9,8},{10,11... | collective-permute-start | bytes 1572872 | tf_op jit(solution)/shard_map/ppermute | solution.py:131
  28.3 3.8 %collective-permute-start.5 = (bf16[4,256,256]{2,1,0:T(8,128)(2,1)S(1)}, bf16[4,256,256]{2,1,0:T(8,128)(2,1)S(1)}, u32[]{:S(2)}, u32[]{:S(2)}) collective-permute-start(bf16[4,256,256]{2,1,0:T(8,128)(2,1)S(1)} %keep.1.refs_0_), channel_id=1, source_target_pairs={{0,1},{1,0},{2,3},{3,2},{4,5},{5,4},{6,7},{7,6},{8,9},{9,8},{10,11... | collective-permute-start | bytes 1572872 | tf_op jit(solution)/shard_map/ppermute | solution.py:131
  32.1 3.8 %collective-permute-start.7 = (bf16[4,256,256]{2,1,0:T(8,128)(2,1)S(1)}, bf16[4,256,256]{2,1,0:T(8,128)(2,1)S(1)}, u32[]{:S(2)}, u32[]{:S(2)}) collective-permute-start(bf16[4,256,256]{2,1,0:T(8,128)(2,1)S(1)} %collective-permute-done.6.refs_6_), channel_id=1, source_target_pairs={{0,1},{1,0},{2,3},{3,2},{4,5},{5,4},{6,7},{7,6},{8,9},{9,8},{10,11... | collective-permute-start | bytes 1572872 | tf_op jit(solution)/shard_map/ppermute | solution.py:131
